TPU v7x, 32 devices: a whole 2x2x4 slice. The times are simulated.
32 devices in a mesh: lat: 4 (over x, core), lon: 8 (over z, y).
Axes of the slice: x: 2, y: 2, z: 4, core: 2. Of those that a mesh axis runs over, the one named last changes fastest.
Arguments:
- velocity: bfloat16 [2, 256, 384, 512], P(None, None, 'lon', 'lat'), may hold values from -16 to 16
- lon_metric: float32 [384, 512], P('lon', 'lat'), may hold values from 0.5 to 2
- lat_metric: float32 [384, 512], P('lon', 'lat'), may hold values from 0.5 to 2
- wet_index: int32 [196608], P(('lat', 'lon')), may hold values from 0 to 6143, as said below
- wet_count: int32 [32], P(('lat', 'lon')), may hold values from 3072 to 6144, as said below
Outputs:
- basis: bfloat16 [512, 196608], P(None, ('lat', 'lon'))
- r_factor: float32 [512, 512], replicated
Inputs may be any that keep to these rules, and one draw needn't show every extreme that they name: `wet_index`: each device's 6144 entries are a permutation of its local cells 0 to 6143. `wet_count`: some device has all 6144 cells wet.
All inputs are finite; a program needn't handle non-finite values.
Results may differ from a plain program's by a relative error of at most 0.001.
The roundings to bfloat16 on the way count: a program that leaves them out, or rounds other values in their place, can miss the bound.
Values may be sent and summed in bfloat16 or wider, within the bound.
No kernel may reach another device: no remote copies, remote signals or barrier semaphores. Data moves between devices by JAX's collectives and lax.ppermute only.
A program may use at most 128 MiB of HBM per device.

v0:
```python
import math

import jax
import jax.numpy as jnp
from jax import lax
from jax.sharding import PartitionSpec as P


def with_halo(block, sides, width, periodic):
    for axis, dim in sides:
        count = lax.axis_size(axis)
        forward = [(i, i + 1) for i in range(count - 1)]
        if periodic:
            forward.append((count - 1, 0))
        backward = [(target, source) for source, target in forward]
        low = lax.ppermute(
            lax.slice_in_dim(block, block.shape[dim] - width, None, axis=dim), axis, forward
        )
        high = lax.ppermute(lax.slice_in_dim(block, 0, width, axis=dim), axis, backward)
        block = jnp.concatenate([low, block, high], axis=dim)
    return block


def partner(block, axis, stride):
    count = lax.axis_size(axis)
    route = []
    for low in range(count):
        high = low | 1 << stride
        if high != low and high < count:
            route += [(low, high), (high, low)]
    return lax.ppermute(block, axis, route)


def upper_blocks(gram, block_size):
    block_count = gram.shape[0] // block_size
    return jnp.stack(
        [
            gram[
                row_at * block_size : (row_at + 1) * block_size,
                col_at * block_size : (col_at + 1) * block_size,
            ]
            for row_at in range(block_count)
            for col_at in range(row_at, block_count)
        ]
    )


def from_blocks(pieces, block_count):
    places = {}
    position = 0
    for row_at in range(block_count):
        for col_at in range(row_at, block_count):
            places[row_at, col_at] = pieces[position]
            position += 1
    return jnp.block(
        [
            [
                places[row_at, col_at] if col_at >= row_at else places[col_at, row_at].T
                for col_at in range(block_count)
            ]
            for row_at in range(block_count)
        ]
    )


def shards(velocity, lon_metric, lat_metric, wet_index, wet_count):
    days = velocity.shape[1]
    width_x = velocity.shape[2]
    width_y = velocity.shape[3]
    cells = width_x * width_y
    columns = 2 * days
    lon_ext = with_halo(velocity, (("lon", 2),), 1, True)
    lat_ext = with_halo(velocity, (("lat", 3),), 1, False)
    mirrored = velocity[:, :, ::-1, -1].reshape(-1)
    bit_count = lax.axis_size("lon").bit_length() - 1
    for bit_pos in range(bit_count):
        mirrored = partner(mirrored, "lon", bit_pos)
    ghost_row = -mirrored.reshape(2, days, width_x).astype(jnp.float32)
    is_top = lax.axis_index("lat") == lax.axis_size("lat") - 1
    upper_rim = jnp.where(is_top, ghost_row, lat_ext[:, :, :, -1].astype(jnp.float32))
    above = jnp.concatenate(
        [lat_ext[:, :, :, 2:-1].astype(jnp.float32), upper_rim[:, :, :, None]], axis=3
    )
    below = lat_ext[:, :, :, :-2].astype(jnp.float32)
    east_cell = lon_ext[:, :, 2:, :].astype(jnp.float32)
    west_cell = lon_ext[:, :, :-2, :].astype(jnp.float32)
    across = 0.5 * lon_metric * (east_cell - west_cell)
    along = 0.5 * lat_metric * (above - below)
    zeta = across[1] - along[0]
    divergence = across[0] + along[1]
    stacked = (
        jnp.concatenate([zeta, divergence], axis=0).astype(jnp.bfloat16).reshape(columns, cells)
    )
    picked = jnp.take(stacked, wet_index, axis=1)
    live = jnp.arange(cells, dtype=jnp.int32) < wet_count[0]
    snapshot = jnp.where(live[None, :], picked, jnp.zeros_like(picked))
    block_size = min(128, columns)
    block_count = columns // block_size
    gram_one = lax.dot_general(
        snapshot, snapshot, (((1,), (1,)), ((), ())), preferred_element_type=jnp.float32
    )
    first_total = from_blocks(
        lax.psum(upper_blocks(gram_one, block_size), ("lat", "lon")), block_count
    )
    lower_one = jnp.linalg.cholesky(first_total)
    ortho = lax.linalg.triangular_solve(
        lower_one, snapshot.astype(jnp.float32), left_side=True, lower=True
    )
    triangle = lower_one.T
    scale = math.sqrt(cells * lax.axis_size("lat") * lax.axis_size("lon"))
    return ((ortho * scale).astype(jnp.bfloat16), triangle / scale)


def solution(mesh):
    placed = (
        P(None, None, "lon", "lat"),
        P("lon", "lat"),
        P("lon", "lat"),
        P(("lat", "lon")),
        P(("lat", "lon")),
    )
    return jax.shard_map(
        shards,
        mesh=mesh,
        in_specs=placed,
        out_specs=(P(None, ("lat", "lon")), P()),
        check_vma=False,
    )
```

profile of v0, /device:TPU:0, one launch (start us, length us, event | category | flops | bytes accessed | tf_op | source)
XLA Modules:
  0.0 478.0 jit_solution(13914941225888795383)
XLA Ops:
  7.2 11.6 %fusion.60 = (bf16[2,256,48,1]{3,2,1,0:T(8,128)(2,1)}, bf16[2,256,48,1]{3,2,1,0:T(8,128)(2,1)}) fusion(bf16[2,256,48,128]{3,2,1,0:T(8,128)(2,1)} %param.5), kind=kLoop, calls=%fused_computation.134 | loop fusion | bytes 196608 | tf_op jit(solution)/shard_map/slice | solution.py:19
  18.8 7.9 %copy.85 = bf16[2,256,48,1]{1,2,3,0:T(8,128)(2,1)S(1)} copy(bf16[2,256,48,1]{3,2,1,0:T(8,128)(2,1)} %get-tuple-element.35) | data formatting | bytes 98304
  31.9 6.1 %copy.86 = bf16[2,256,48,1]{2,1,0,3:T(8,128)(2,1)S(1)} copy(bf16[2,256,48,1]{3,2,1,0:T(8,128)(2,1)} %get-tuple-element.34) | data formatting | bytes 98304
  45.0 9.0 %slice_convert_fusion = f32[2,256,48,127]{3,2,1,0:T(8,128)} fusion(bf16[2,256,48,128]{3,2,1,0:T(8,128)(2,1)} %param.5), kind=kLoop, calls=%fused_computation.29 | loop fusion | flops 3121152 | bytes 18726912 | tf_op jit(solution)/shard_map/convert_element_type | solution.py:82
  59.9 6.9 %copy.59 = bf16[2,256,48,1]{3,2,1,0:T(8,128)(2,1)} copy(bf16[2,256,48,1]{1,2,3,0:T(8,128)(2,1)S(1)} %collective-permute-done.6) | data formatting | bytes 98304 | tf_op jit(solution)/shard_map/ppermute | solution.py:16
  67.5 7.0 %copy.58 = f32[2,256,48,1]{3,2,1,0:T(8,128)} copy(f32[2,256,48,1]{2,1,0,3:T(8,128)S(1)} %convert_select_fusion) | data formatting | bytes 196608 | tf_op jit(solution)/shard_map/jit(_where)/select_n | solution.py:80
  74.5 26.6 %subtract_multiply_fusion = (f32[2,256,48,128]{3,2,1,0:T(8,128)S(1)}, f32[2,256,48,128]{3,2,1,0:T(8,128)}) fusion(bf16[2,256,48,128]{3,2,1,0:T(8,128)(2,1)} %param.5, bf16[2,256,1,128]{3,2,1,0:T(2,128)(2,1)S(1)} %copy.54, bf16[2,256,1,128]{3,2,1,0:T(2,128)(2,1)S(1)} %copy.52, f32[48,128]{1,0:T(8,128)S(1)} %get-tuple-element.65, ...), kind=kLoop, calls=%fused_computation.7 | loop fusion | flops 53477376 | bytes 44400640 | tf_op jit(solution)/shard_map/mul | solution.py:87
  101.0 7.1 %fusion.12 = (bf16[1,256,48,128]{3,2,1,0:T(8,128)(2,1)}, bf16[1,256,48,128]{3,2,1,0:T(8,128)(2,1)}) fusion(f32[2,256,48,128]{3,2,1,0:T(8,128)} %get-tuple-element.31, f32[2,256,48,128]{3,2,1,0:T(8,128)S(1)} %get-tuple-element.30), kind=kLoop, calls=%fused_computation.20 | loop fusion | flops 6291456 | bytes 31457280 | tf_op jit(solution)/shard_map/convert.3
  122.1 29.2 %gather_fusion = bf16[6144,512]{1,0:T(8,128)(2,1)} fusion(bf16[512,6144]{0,1:T(8,128)(2,1)} %pad_maximum_fusion.3, s32[6144]{0:T(1024)S(1)} %fusion.51), kind=kCustom, calls=%fused_computation | custom fusion | bytes 12607488 | tf_op jit(solution)/shard_map/jit(_take)/gather | solution.py:94
  151.3 8.6 %copy.62 = bf16[6144,512]{0,1:T(8,128)(2,1)} copy(bf16[6144,512]{1,0:T(8,128)(2,1)} %gather_fusion) | data formatting | bytes 12582912 | tf_op jit(solution)/shard_map/jit(_take)/gather | solution.py:94
  160.0 8.7 %fusion.16 = f32[512,512]{0,1:T(8,128)S(1)} fusion(bf16[6144,512]{0,1:T(8,128)(2,1)} %copy.62, pred[6144]{0:T(1024)(128)(4,1)S(1)} %get-tuple-element.66, pred[6144]{0:T(1024)(128)(4,1)S(1)} %get-tuple-element.67), kind=kOutput, calls=%fused_computation.30 | convolution fusion | flops 3227516928 | bytes 7352320 | tf_op jit(solution)/shard_map/dot_general | solution.py:99
  169.7 10.8 %fusion.56 = (f32[512,6144]{1,0:T(8,128)}, bf16[512,6144]{1,0:T(8,128)(2,1)}) fusion(bf16[6144,512]{0,1:T(8,128)(2,1)} %copy.62, pred[6144]{0:T(1024)(128)(4,1)S(1)} %get-tuple-element.67, pred[6144]{0:T(1024)(128)(4,1)S(1)} %get-tuple-element.66), kind=kLoop, calls=%fused_computation.131 | loop fusion | flops 9437184 | bytes 25178112 | tf_op jit(solution)/shard_map/convert_element_type | solution.py:107
  180.5 121.2 %all-reduce.3.cloned.1.call-done = f32[10,128,128]{1,2,0:T(8,128)} async-done(((f32[10,128,128]{1,2,0:T(8,128)}), f32[10,128,128]{1,2,0:T(8,128)}) %all-reduce.3.cloned.1.call-update) | async-done | bytes 655376 | tf_op jit(solution)/shard_map/psum | solution.py:103
  304.3 11.7 %cholesky.104 = f32[128,128]{1,0:T(8,128)S(1)} custom-call(f32[128,128]{1,0:T(8,128)S(1)} %cholesky.266), custom_call_target="Cholesky" | custom-call | tf_op jit(solution)/shard_map/jit(cholesky)/cholesky | solution.py:105
  316.2 9.8 %custom-call.30 = f32[1,128,128]{1,2,0:T(8,128)S(1)} custom-call(f32[1,128,128]{2,1,0:T(8,128)S(1)} %get-tuple-element.61), custom_call_target="InvertDiagBlocksLowerTriangular" | custom-call | tf_op jit(solution)/shard_map/jit(cholesky)/cholesky | solution.py:105
  326.7 12.2 %cholesky.217 = f32[128,128]{1,0:T(8,128)S(1)} custom-call(f32[128,128]{1,0:T(8,128)S(1)} %cholesky.270), custom_call_target="Cholesky" | custom-call | tf_op jit(solution)/shard_map/jit(cholesky)/cholesky | solution.py:105
  340.2 9.8 %custom-call.31 = f32[1,128,128]{1,2,0:T(8,128)S(1)} custom-call(f32[1,128,128]{2,1,0:T(8,128)S(1)} %get-tuple-element.58), custom_call_target="InvertDiagBlocksLowerTriangular" | custom-call | tf_op jit(solution)/shard_map/jit(cholesky)/cholesky | solution.py:105
  350.7 11.7 %cholesky.238 = f32[128,128]{1,0:T(8,128)S(1)} custom-call(f32[128,128]{1,0:T(8,128)S(1)} %cholesky.275), custom_call_target="Cholesky" | custom-call | tf_op jit(solution)/shard_map/jit(cholesky)/cholesky | solution.py:105
  363.1 9.8 %custom-call.32 = f32[1,128,128]{1,2,0:T(8,128)S(1)} custom-call(f32[1,128,128]{2,1,0:T(8,128)S(1)} %get-tuple-element.55), custom_call_target="InvertDiagBlocksLowerTriangular" | custom-call | tf_op jit(solution)/shard_map/jit(cholesky)/cholesky | solution.py:105
  373.5 11.9 %cholesky.255 = f32[128,128]{1,0:T(8,128)S(1)} custom-call(f32[128,128]{1,0:T(8,128)S(1)} %convolution_subtract_fusion.4), custom_call_target="Cholesky" | custom-call | tf_op jit(solution)/shard_map/jit(cholesky)/cholesky | solution.py:105
  388.7 8.1 %while.1 = (s32[]{:T(128)}, f32[512,512]{1,0:T(8,128)S(1)}, s32[4,2]{0,1:T(2,128)S(1)}, f32[4,128,128]{2,1,0:T(8,128)S(1)}, s32[]{:T(128)}) while((s32[]{:T(128)}, f32[512,512]{1,0:T(8,128)S(1)}, s32[4,2]{0,1:T(2,128)S(1)}, f32[4,128,128]{2,1,0:T(8,128)S(1)}, s32[]{:T(128)}) %tuple.54), condition=%wide.while_cond, body=%wide.while_body.sunk | while | flops 2 | bytes 131181 | solution.py:106
  396.8 39.3 %custom-call.33 = f32[4,128,128]{1,2,0:T(8,128)S(1)} custom-call(f32[4,128,128]{2,1,0:T(8,128)S(1)} %get-tuple-element.9), custom_call_target="InvertDiagBlocksLowerTriangular" | custom-call | tf_op jit(solution)/shard_map/triangular_solve | solution.py:106
  446.8 5.9 %convolution_subtract_fusion.1 = f32[128,6144]{1,0:T(8,128)S(1)} fusion(f32[128,6144]{1,0:T(8,128)S(1)} %fusion.35, f32[128,6144]{1,0:T(8,128)S(1)} %fusion.20, f32[512,6144]{1,0:T(8,128)} %get-tuple-element.24, f32[512,512]{1,0:T(8,128)S(1)} %get-tuple-element.113), kind=kOutput, calls=%fused_computation.15 | convolution fusion | flops 2418278400 | bytes 12713984 | tf_op jit(solution)/shard_map/triangular_solve | solution.py:106
  455.8 7.3 %fusion.8 = f32[128,6144]{1,0:T(8,128)S(1)} fusion(f32[128,6144]{1,0:T(8,128)S(1)} %fusion.33, f32[128,6144]{1,0:T(8,128)S(1)} %fusion.35, f32[128,6144]{1,0:T(8,128)S(1)} %fusion.20, f32[512,6144]{1,0:T(8,128)} %get-tuple-element.24, f32[512,512]{1,0:T(8,128)S(1)} %get-tuple-element.113), kind=kOutput, calls=%fused_computation.16 | convolution fusion | flops 3629383680 | bytes 15925248 | tf_op jit(solution)/shard_map/triangular_solve | solution.py:106
  (104 shorter events, 69.9 us)
Async XLA Ops:
  7.2 294.6 %all-reduce.3.cloned.1.call-start = ((), (), s32[]{:S(2)}) async-start(), calls=%async_computation | async-start | bytes 1310720 | tf_op jit(solution)/shard_map/psum | solution.py:103
  26.7 33.2 %collective-permute-start.6 = (bf16[2,256,48,1]{1,2,3,0:T(8,128)(2,1)S(1)}, bf16[2,256,48,1]{1,2,3,0:T(8,128)(2,1)S(1)}, u32[]{:S(2)}, u32[]{:S(2)}) collective-permute-start(bf16[2,256,48,1]{1,2,3,0:T(8,128)(2,1)S(1)} %copy.85), channel_id=1, source_target_pairs={{0,8},{8,16},{16,24},{1,9},{9,17},{17,25},{2,10},{10,18},{18,26},{... | collective-permute-start | bytes 147464 | tf_op jit(solution)/shard_map/ppermute | solution.py:16
  29.5 25.2 %collective-permute-start.2 = (bf16[24576]{0:T(1024)(128)(2,1)S(1)}, bf16[24576]{0:T(1024)(128)(2,1)S(1)}, u32[]{:S(2)}, u32[]{:S(2)}) collective-permute-start(bf16[24576]{0:T(1024)(128)(2,1)S(1)} %reshape_squeeze.3), channel_id=1, source_target_pairs={{0,1},{1,0},{2,3},{3,2},{4,5},{5,4},{6,7},{7,6},{8,9},{9,8},{10,11... | collective-permute-start | bytes 147464 | tf_op jit(solution)/shard_map/ppermute | solution.py:31
  38.0 29.4 %collective-permute-start.5 = (bf16[2,256,48,1]{2,1,0,3:T(8,128)(2,1)S(1)}, bf16[2,256,48,1]{2,1,0,3:T(8,128)(2,1)S(1)}, u32[]{:S(2)}, u32[]{:S(2)}) collective-permute-start(bf16[2,256,48,1]{2,1,0,3:T(8,128)(2,1)S(1)} %copy.86), channel_id=1, source_target_pairs={{8,0},{16,8},{24,16},{9,1},{17,9},{25,17},{10,2},{18,10},{26,18},{... | collective-permute-start | bytes 147464 | tf_op jit(solution)/shard_map/ppermute | solution.py:19
  41.3 25.5 %collective-permute-start = (bf16[2,256,1,128]{3,1,2,0:T(8,128)(2,1)S(1)}, bf16[2,256,1,128]{3,1,2,0:T(8,128)(2,1)S(1)}, u32[]{:S(2)}, u32[]{:S(2)}) collective-permute-start(bf16[2,256,1,128]{3,1,2,0:T(8,128)(2,1)S(1)} %copy.83), channel_id=1, source_target_pairs={{1,0},{2,1},{3,2},{4,3},{5,4},{6,5},{7,6},{0,7},{9,8},{10,9},{11,1... | collective-permute-start | bytes 393224 | tf_op jit(solution)/shard_map/ppermute | solution.py:19
  44.9 9.1 %copy-start.2 = (f32[48,128]{1,0:T(8,128)S(1)}, f32[48,128]{1,0:T(8,128)}, u32[]{:S(2)}) copy-start(f32[48,128]{1,0:T(8,128)} %param.7) | copy-start | bytes 73732
  44.9 9.1 %copy-start.3 = (f32[48,128]{1,0:T(8,128)S(1)}, f32[48,128]{1,0:T(8,128)}, u32[]{:S(2)}) copy-start(f32[48,128]{1,0:T(8,128)} %param.6) | copy-start | bytes 73732
  44.9 9.1 %copy-start.1 = (s32[6144]{0:T(1024)S(1)}, s32[6144]{0:T(1024)}, u32[]{:S(2)}) copy-start(s32[6144]{0:T(1024)} %param.8) | copy-start | bytes 73732
  44.9 22.1 %collective-permute-start.1 = (bf16[2,256,1,128]{3,1,2,0:T(8,128)(2,1)S(1)}, bf16[2,256,1,128]{3,1,2,0:T(8,128)(2,1)S(1)}, u32[]{:S(2)}, u32[]{:S(2)}) collective-permute-start(bf16[2,256,1,128]{3,1,2,0:T(8,128)(2,1)S(1)} %copy.84), channel_id=1, source_target_pairs={{0,1},{1,2},{2,3},{3,4},{4,5},{5,6},{6,7},{7,0},{8,9},{9,10},{10,1... | collective-permute-start | bytes 393224 | tf_op jit(solution)/shard_map/ppermute | solution.py:16
  54.7 4.2 collective-permute-start.3
  58.9 8.4 %collective-permute-start.4 = (bf16[24576]{0:T(1024)(128)(2,1)S(1)}, bf16[24576]{0:T(1024)(128)(2,1)S(1)}, u32[]{:S(2)}, u32[]{:S(2)}) collective-permute-start(bf16[24576]{0:T(1024)(128)(2,1)S(1)} %collective-permute-done.3), channel_id=1, source_target_pairs={{0,4},{4,0},{1,5},{5,1},{2,6},{6,2},{3,7},{7,3},{8,12},{12,8},{9,1... | collective-permute-start | bytes 147464 | tf_op jit(solution)/shard_map/ppermute | solution.py:31
  168.9 0.8 copy-start
Sparse Core Ops, SparseCore 0:
  169.8 131.8 all-reduce.2
where the time goes:
time: 484 us; the launch traced here: 478 us
  other arithmetic  182 us (38%)
  waiting for transfers between devices  125 us (26%)
  local copies, waits for them, and re-layouts  102 us (21%)
  matrix products  40.4 us (8%)
  between operations  17.9 us (4%)
  starting transfers between devices  10.9 us (2%)
    psum x1, waiting for transfers between devices, shards(): lax.psum(upper_blocks(gram_one, block_size), ('lat', 'lon'))  121 us
    another operation x15, other arithmetic, shards(): lower_one = jnp.linalg.cholesky(first_total)  79.6 us
    another operation x2, other arithmetic, shards(): lax.linalg.triangular_solve(lower_one, snapshot.astype(jnp.float32), left...  39.3 us
    gather x2, local copies, waits for them, and re-layouts, shards(): picked = jnp.take(stacked, wet_index, axis=1)  37.8 us
    another operation x7, matrix products, shards(): lax.linalg.triangular_solve(lower_one, snapshot.astype(jnp.float32), left...  29.8 us
    mul x1, other arithmetic, shards(): across = 0.5 * lon_metric * (east_cell - west_cell)  26.6 us
    another operation x14, local copies, waits for them, and re-layouts  16.9 us
    unnamed x25, local copies, waits for them, and re-layouts  16.6 us
  transfers between devices with their start and end apart: 8, of which 2 were waited for; matrix products, arithmetic and copies ran while one was open for 7% of the time, Pallas kernels for 0%

commit v1 on v0

v1 whole, which is shorter than its diff:
```python
import functools
import math

import jax
import jax.numpy as jnp
from jax import lax
from jax.experimental import pallas as pl
from jax.experimental.pallas import tpu as pltpu
from jax.sharding import PartitionSpec as P

F32 = jnp.float32
BF16 = jnp.bfloat16
MB = 1 << 20
NN = (((1,), (0,)), ((), ()))
NT = (((1,), (1,)), ((), ()))
TN = (((0,), (0,)), ((), ()))


def iota(shape, dim):
    return lax.broadcasted_iota(jnp.int32, shape, dim)


def relayout_kernel(half, v_ref, out_ref, south_ref, north_ref, fold_ref, wide):
    fields, days, width_x, width_y = v_ref.shape
    lane = iota((16, width_y), 1)
    for f in range(fields):
        wide[f] = v_ref[f].astype(F32).reshape(days * width_x, width_y)
    for d in range(0, days, 16):
        south = jnp.zeros((16, width_y), F32)
        north = jnp.zeros((16, width_y), F32)
        fold = jnp.zeros((16, width_y), F32)
        for f in range(fields):
            for x in range(width_x):
                piece = wide[f, pl.ds(d * width_x + x, 16, stride=width_x), :]
                out_ref[f, x, d : d + 16, :] = piece.astype(BF16)
                at = f * half + x
                turned = pltpu.roll(piece, at + 1, 1)
                north = jnp.where(lane == at, turned, north)
                south = jnp.where(lane == at + 1, turned, south)
                back = f * half + width_x - x
                fold = jnp.where(lane == back, pltpu.roll(piece, back + 1, 1), fold)
        south_ref[d : d + 16, :] = south.astype(BF16)
        north_ref[d : d + 16, :] = north.astype(BF16)
        fold_ref[d : d + 16, :] = -fold.astype(BF16)


def relayout(velocity):
    fields, days, width_x, width_y = velocity.shape
    step = 32
    edge = jax.ShapeDtypeStruct((days, width_y), BF16)
    edge_spec = pl.BlockSpec((step, width_y), lambda i: (i, 0))
    return pl.pallas_call(
        functools.partial(relayout_kernel, width_y // 2),
        grid=(days // step,),
        in_specs=[pl.BlockSpec((fields, step, width_x, width_y), lambda i: (0, i, 0, 0))],
        out_specs=[
            pl.BlockSpec((fields, width_x, step, width_y), lambda i: (0, 0, i, 0)),
            edge_spec,
            edge_spec,
            edge_spec,
        ],
        out_shape=[
            jax.ShapeDtypeStruct((fields, width_x, days, width_y), BF16),
            edge,
            edge,
            edge,
        ],
        scratch_shapes=[pltpu.VMEM((fields, step * width_x, width_y), F32)],
        compiler_params=pltpu.CompilerParams(vmem_limit_bytes=40 * MB),
        name="relayout",
    )(velocity)


def wet_metrics_kernel(index_ref, count_ref, lon_ref, lat_ref, lon_out, lat_out):
    width_x, width_y = lon_ref.shape
    cells = index_ref.shape[1]
    index = index_ref[...]
    place = iota(index.shape, 1)
    wet = place < count_ref[0]
    row = jnp.where(wet, index // width_y, -1)
    col = index % width_y
    pick_x = jnp.where(iota((width_x, cells), 0) == row, 1.0, 0.0).astype(BF16)
    pick_y = jnp.where(iota((width_y, cells), 0) == col, 1.0, 0.0).astype(BF16)
    mask = lax.dot_general(pick_x, pick_y, NT, preferred_element_type=F32)
    lon_out[...] = 0.5 * lon_ref[...] * mask
    lat_out[...] = 0.5 * lat_ref[...] * mask


def wet_metrics(wet_index, wet_count, lon_metric, lat_metric):
    vmem = pl.BlockSpec(memory_space=pltpu.VMEM)
    return pl.pallas_call(
        wet_metrics_kernel,
        in_specs=[vmem, pl.BlockSpec(memory_space=pltpu.SMEM), vmem, vmem],
        out_specs=[vmem, vmem],
        out_shape=[jax.ShapeDtypeStruct(lon_metric.shape, F32)] * 2,
        compiler_params=pltpu.CompilerParams(vmem_limit_bytes=40 * MB),
        name="wet_metrics",
    )(wet_index.reshape(1, -1), wet_count, lon_metric, lat_metric)


def stencil_kernel(
    v_ref, left_ref, right_ref, west_ref, east_ref, south_ref, north_ref, fold_ref,
    lon_ref, lat_ref, fields_ref, gram_ref, total,
):
    step, steps = pl.program_id(0), pl.num_programs(0)
    _, group, days, width_y = v_ref.shape
    half = width_y // 2
    wide = 2 * width_y

    k = iota((wide, wide), 0)
    n = iota((wide, wide), 1)
    same = k // width_y == n // width_y
    diff = jnp.where(same & (k == n + 1), 1.0, 0.0) - jnp.where(same & (k == n - 1), 1.0, 0.0)
    diff = diff.astype(BF16)
    field = n // width_y
    lane = n % width_y
    sign = jnp.where(lane == 0, -1.0, 1.0)
    aim = jnp.where(
        lane == 0, k - field * half, jnp.where(lane == width_y - 1, k - width_y - field * half - 1, -1)
    )
    rim = jnp.concatenate([south_ref[...], north_ref[...] + fold_ref[...]], axis=1)
    first = step == 0
    last = step == steps - 1

    def column(f, g):
        if g < 0:
            return jnp.where(first, west_ref[f], left_ref[f, 0])
        if g >= group:
            return jnp.where(last, east_ref[f], right_ref[f, 0])
        return v_ref[f, g]

    for g in range(group):
        x = step * group + g
        here = jnp.concatenate([v_ref[0, g], v_ref[1, g]], axis=1)
        reach = jnp.where(aim == x, sign, 0.0).astype(BF16)
        along = lax.dot_general(here, diff, NN, preferred_element_type=F32)
        along = along + lax.dot_general(rim, reach, NN, preferred_element_type=F32)
        lon = lon_ref[pl.ds(x, 1), :]
        lat = lat_ref[pl.ds(x, 1), :]
        across_u = column(0, g + 1).astype(F32) - column(0, g - 1).astype(F32)
        across_v = column(1, g + 1).astype(F32) - column(1, g - 1).astype(F32)
        zeta = lon * across_v - lat * along[:, :width_y]
        divergence = lon * across_u + lat * along[:, width_y:]
        fields_ref[:days, g * width_y : (g + 1) * width_y] = zeta.astype(BF16)
        fields_ref[days:, g * width_y : (g + 1) * width_y] = divergence.astype(BF16)

    upper = lax.dot_general(
        fields_ref[:days, :], fields_ref[...], NT, preferred_element_type=F32
    )
    lower = lax.dot_general(
        fields_ref[days:, :], fields_ref[days:, :], NT, preferred_element_type=F32
    )

    @pl.when(first)
    def _():
        total[:days, :] = upper
        total[days:, days:] = lower

    @pl.when(jnp.logical_not(first))
    def _():
        total[:days, :] += upper
        total[days:, days:] += lower

    @pl.when(last)
    def _():
        size = gram_ref.shape[1]
        at = 0
        for i in range(2 * days // size):
            for j in range(i, 2 * days // size):
                gram_ref[at] = total[i * size : (i + 1) * size, j * size : (j + 1) * size]
                at += 1


def stencil(moved, west, east, south, north, fold, lon, lat, size):
    _, width_x, days, width_y = moved.shape
    group = next(g for g in (8, 6, 4, 3, 2, 1) if width_x % g == 0)
    count = 2 * days // size
    blocks = count * (count + 1) // 2
    rim_spec = pl.BlockSpec((days, width_y), lambda i: (0, 0))
    side_spec = pl.BlockSpec((2, days, width_y), lambda i: (0, 0, 0))
    metric_spec = pl.BlockSpec((width_x, width_y), lambda i: (0, 0))
    return pl.pallas_call(
        stencil_kernel,
        grid=(width_x // group,),
        in_specs=[
            pl.BlockSpec((2, group, days, width_y), lambda i: (0, i, 0, 0)),
            pl.BlockSpec((2, 1, days, width_y), lambda i: (0, jnp.maximum(i * group - 1, 0), 0, 0)),
            pl.BlockSpec(
                (2, 1, days, width_y),
                lambda i: (0, jnp.minimum(i * group + group, width_x - 1), 0, 0),
            ),
            side_spec, side_spec, rim_spec, rim_spec, rim_spec, metric_spec, metric_spec,
        ],
        out_specs=[
            pl.BlockSpec((2 * days, group * width_y), lambda i: (0, i)),
            pl.BlockSpec((blocks, size, size), lambda i: (0, 0, 0)),
        ],
        out_shape=[
            jax.ShapeDtypeStruct((2 * days, width_x * width_y), BF16),
            jax.ShapeDtypeStruct((blocks, size, size), F32),
        ],
        scratch_shapes=[pltpu.VMEM((2 * days, 2 * days), F32)],
        compiler_params=pltpu.CompilerParams(vmem_limit_bytes=48 * MB),
        name="stencil_gram",
    )(moved, moved, moved, west, east, south, north, fold, lon, lat)


def all_sum(x):
    moves = []
    for axis in ("lat", "lon"):
        count = lax.axis_size(axis)
        assert count & (count - 1) == 0
        for bit in range(count.bit_length() - 1):
            moves.append((axis, bit))
    shape = x.shape
    x = x.reshape(-1, shape[-1])
    taken = []

    def swap(block, axis, bit):
        return lax.ppermute(
            block, axis, [(i, i ^ 1 << bit) for i in range(lax.axis_size(axis))]
        )

    for axis, bit in moves:
        halve = x.shape[0] % 16 == 0
        if halve:
            half = x.shape[0] // 2
            high = (lax.axis_index(axis) >> bit) & 1
            keep = lax.dynamic_slice_in_dim(x, high * half, half, 0)
            send = lax.dynamic_slice_in_dim(x, (1 - high) * half, half, 0)
            x = keep + swap(send, axis, bit)
        else:
            x = x + swap(x, axis, bit)
        taken.append(halve)
    for (axis, bit), halve in reversed(list(zip(moves, taken))):
        if halve:
            high = (lax.axis_index(axis) >> bit) & 1
            other = swap(x, axis, bit)
            x = jnp.where(
                high == 1, jnp.concatenate([other, x], 0), jnp.concatenate([x, other], 0)
            )
    return x.reshape(shape)


def pick_kernel(index_ref, fields_ref, out_ref, rows, picked):
    step = pl.program_id(0)
    columns, cells = fields_ref.shape
    count = out_ref.shape[0]
    parts = columns // 128

    @pl.when(step == 0)
    def _():
        unit = jnp.where(iota((128, 128), 0) == iota((128, 128), 1), 1.0, 0.0).astype(BF16)

        def turn(i, _):
            at = pl.multiple_of(i * 128, 128)
            block = fields_ref[:, pl.ds(at, 128)]
            turned = lax.dot_general(unit, block, NT, preferred_element_type=F32)
            for c in range(parts):
                rows[pl.ds(at * parts + c, 128, stride=parts), :] = turned[:, c * 128 : (c + 1) * 128]
            return 0

        lax.fori_loop(0, cells // 128, turn, 0)

    unroll = 16

    def move(i, _):
        for j in range(unroll):
            r = i * unroll + j
            source = pl.multiple_of(index_ref[step * count + r] * parts, parts)
            target = pl.multiple_of(r * parts, parts)
            picked[pl.ds(target, parts), :] = rows[pl.ds(source, parts), :]
        return 0

    lax.fori_loop(0, count // unroll, move, 0)
    for c in range(parts):
        out_ref[:, c * 128 : (c + 1) * 128] = picked[pl.ds(c, count, stride=parts), :].astype(BF16)


def pick(wet_index, fields):
    columns, cells = fields.shape
    count = next(c for c in (768, 512, 256, 128, cells) if cells % c == 0)
    parts = columns // 128
    return pl.pallas_call(
        pick_kernel,
        grid_spec=pltpu.PrefetchScalarGridSpec(
            num_scalar_prefetch=1,
            grid=(cells // count,),
            in_specs=[pl.BlockSpec((columns, cells), lambda i, _: (0, 0))],
            out_specs=pl.BlockSpec((count, columns), lambda i, _: (i, 0)),
            scratch_shapes=[
                pltpu.VMEM((cells * parts, 128), F32),
                pltpu.VMEM((count * parts, 128), F32),
            ],
        ),
        out_shape=jax.ShapeDtypeStruct((cells, columns), BF16),
        compiler_params=pltpu.CompilerParams(vmem_limit_bytes=48 * MB),
        name="pick",
    )(wet_index, fields)


def product_kernel(high_ref, low_ref, rows_ref, out_ref):
    columns = rows_ref.shape[1]
    half = columns // 2

    def dot(w, s):
        return lax.dot_general(w, s, NT, preferred_element_type=F32)

    s = rows_ref[:, :half]
    top = dot(low_ref[:half, :half], s) + dot(high_ref[:half, :half], s)
    out_ref[:half, :] = top.astype(BF16)
    s = rows_ref[...]
    bottom = dot(low_ref[half:, :], s) + dot(high_ref[half:, :], s)
    out_ref[half:, :] = bottom.astype(BF16)


def product(high, low, rows):
    cells, columns = rows.shape
    width = next(c for c in (1024, 512, 256, 128, cells) if cells % c == 0)
    factor_spec = pl.BlockSpec((columns, columns), lambda i: (0, 0))
    return pl.pallas_call(
        product_kernel,
        grid=(cells // width,),
        in_specs=[factor_spec, factor_spec, pl.BlockSpec((width, columns), lambda i: (i, 0))],
        out_specs=pl.BlockSpec((columns, width), lambda i: (0, i)),
        out_shape=jax.ShapeDtypeStruct((columns, cells), BF16),
        compiler_params=pltpu.CompilerParams(vmem_limit_bytes=48 * MB),
        name="product",
    )(high, low, rows)


def sublane(x, t):
    return jnp.broadcast_to(x[t : t + 1, :], x.shape)


def inverse_factor(block):
    size = block.shape[0]
    count = size // 8
    lane = iota((8, size), 1)
    row = iota((8, size), 0)
    tiles = [block[8 * p : 8 * p + 8, :] for p in range(count)]
    out = []
    for p in range(count):
        base = 8 * p
        cols = {
            q: [jnp.broadcast_to(tiles[q][:, base + t : base + t + 1], (8, size)) for t in range(8)]
            for q in range(p, count)
        }
        own = (lane >= base) & (lane < base + 8)
        work = jnp.where(own, jnp.where(lane == base + row, 1.0, 0.0), tiles[p])
        head = cols[p]
        done = jnp.zeros((8, size), F32)
        pivots = jnp.ones((8, size), F32)
        for t in range(8):
            at = row == t
            pivot = sublane(head[t], t)
            inverse = 1.0 / pivot
            coef = jnp.where(at, inverse, -head[t] * inverse)
            line = sublane(work, t)
            done = jnp.where(at, line, done)
            pivots = jnp.where(at, pivot, pivots)
            for u in range(t + 1, 8):
                head[u] = jnp.where(at, 0.0, head[u]) + coef * sublane(head[u], t)
            work = jnp.where(at, 0.0, work) + coef * line
        out.append(jnp.where(lane <= base + row, done * lax.rsqrt(pivots), 0.0))
        lines = [sublane(work, t) for t in range(8)]
        for q in range(p + 1, count):
            terms = [cols[q][t] * lines[t] for t in range(8)]
            while len(terms) > 1:
                terms = [terms[i] + terms[i + 1] for i in range(0, len(terms), 2)]
            tiles[q] = jnp.where(own, 0.0, tiles[q]) - terms[0]
    return jnp.concatenate(out, axis=0)


def factor_kernel(scale, pieces_ref, r_ref, high_ref, low_ref, work):
    columns = r_ref.shape[0]
    size = pieces_ref.shape[1]
    count = columns // size
    at = 0
    for i in range(count):
        for j in range(i, count):
            work[i * size : (i + 1) * size, j * size : (j + 1) * size] = pieces_ref[at]
            at += 1
        if i:
            work[i * size : (i + 1) * size, : i * size] = jnp.zeros((size, i * size), F32)

    def dot(a, b, dims):
        return lax.dot_general(
            a, b, dims, preferred_element_type=F32, precision=lax.Precision.HIGHEST
        )

    lane = iota((size, columns), 1)

    def step(k, _):
        here = pl.multiple_of(k * size, size)
        diagonal = work[pl.ds(here, size), pl.ds(here, size)]
        inverse = inverse_factor(diagonal)
        corner = dot(inverse, diagonal, NN)
        work[pl.ds(here, size), pl.ds(here, size)] = jnp.where(
            iota((size, size), 0) == iota((size, size), 1), 1.0, 0.0
        )
        fresh = dot(inverse, work[pl.ds(here, size), :], NN)
        work[pl.ds(here, size), :] = fresh
        for i in range(1, count):

            @pl.when(i > k)
            def _():
                mine = slice(i * size, (i + 1) * size)
                work[mine, pl.ds(here, size)] = jnp.zeros((size, size), F32)
                work[mine, :] -= dot(work[pl.ds(here, size), mine], work[pl.ds(here, size), :], TN)

        known = jnp.where(lane < here + size, fresh * scale, 0.0)
        high = known.astype(BF16)
        high_ref[pl.ds(here, size), :] = high
        low_ref[pl.ds(here, size), :] = (known - high.astype(F32)).astype(BF16)
        r_ref[pl.ds(here, size), :] = jnp.where(lane >= here + size, fresh * (1.0 / scale), 0.0)
        upper = iota((size, size), 0) <= iota((size, size), 1)
        r_ref[pl.ds(here, size), pl.ds(here, size)] = jnp.where(upper, corner * (1.0 / scale), 0.0)
        return 0

    lax.fori_loop(0, count, step, 0)


def factor(pieces, columns, scale):
    vmem = pl.BlockSpec(memory_space=pltpu.VMEM)
    square = (columns, columns)
    return pl.pallas_call(
        functools.partial(factor_kernel, scale),
        in_specs=[vmem],
        out_specs=[vmem, vmem, vmem],
        out_shape=[
            jax.ShapeDtypeStruct(square, F32),
            jax.ShapeDtypeStruct(square, BF16),
            jax.ShapeDtypeStruct(square, BF16),
        ],
        scratch_shapes=[pltpu.VMEM(square, F32)],
        compiler_params=pltpu.CompilerParams(vmem_limit_bytes=40 * MB),
        name="factor",
    )(pieces)


def shards(velocity, lon_metric, lat_metric, wet_index, wet_count):
    days = velocity.shape[1]
    cells = velocity.shape[2] * velocity.shape[3]
    columns = 2 * days
    lats, lons = lax.axis_size("lat"), lax.axis_size("lon")
    moved, south, north, fold = relayout(velocity)
    east_route = [(i, (i + 1) % lons) for i in range(lons)]
    west = lax.ppermute(moved[:, -1], "lon", east_route)
    east = lax.ppermute(moved[:, 0], "lon", [(t, s) for s, t in east_route])
    up = [(i, i + 1) for i in range(lats - 1)]
    below = lax.ppermute(north, "lat", up)
    above = lax.ppermute(south, "lat", [(t, s) for s, t in up])
    top = (lats - 1) * lons
    mirrored = lax.ppermute(fold, ("lat", "lon"), [(top + i, top + lons - 1 - i) for i in range(lons)])
    lon, lat = wet_metrics(wet_index, wet_count, lon_metric, lat_metric)
    size = min(128, columns)
    fields, gram = stencil(moved, west, east, below, above, mirrored, lon, lat, size)
    rows = pick(wet_index, fields)
    scale = math.sqrt(cells * lats * lons)
    triangle, high, low = factor(all_sum(gram), columns, scale)
    return product(high, low, rows), triangle


def solution(mesh):
    placed = (
        P(None, None, "lon", "lat"),
        P("lon", "lat"),
        P("lon", "lat"),
        P(("lat", "lon")),
        P(("lat", "lon")),
    )
    return jax.shard_map(
        shards,
        mesh=mesh,
        in_specs=placed,
        out_specs=(P(None, ("lat", "lon")), P()),
        check_vma=False,
    )
```

time: 484 us -> 144 us (0.30); the launches traced: 478 us -> 144 us
  other arithmetic: 182 us -> 0.18 us
  local copies, waits for them, and re-layouts: 102 us -> 5.58 us
  waiting for transfers between devices: 125 us -> 36 us
  Pallas kernels: 0 us -> 79.2 us
  matrix products: 40.4 us -> 0 us
  between operations: 17.9 us -> 1.5 us
  starting transfers between devices: 10.9 us -> 21.1 us
    another operation x18 -> x0, other arithmetic: 126 us -> none  [the longest x15 79.6 us: shards(): lower_one = jnp.linalg.cholesky(first_total)]
    psum x1 -> x0, waiting for transfers between devices: 121 us -> none  [shards(): lax.psum(upper_blocks(gram_one, block_size), ('lat', 'lon'))]
    pallas_call x0 -> x6, Pallas kernels: none -> 79.2 us  [the longest x1 25.5 us: pick(): pl.pallas_call(pick_kernel, grid_spec=pltpu.PrefetchScalarGridSpec(num_sc...]
    gather x2 -> x0, local copies, waits for them, and re-layouts: 37.8 us -> none  [shards(): picked = jnp.take(stacked, wet_index, axis=1)]
    ppermute x7 -> x15, waiting for transfers between devices: 4.04 us -> 36 us  [the longest x10 33.1 us: swap(): lax.ppermute(block, axis, [(i, i ^ 1 << bit) for i in range(lax.axis_size...]
    another operation x13 -> x0, matrix products: 31.6 us -> none  [the longest x7 29.8 us: shards(): lax.linalg.triangular_solve(lower_one, snapshot.astype(jnp.float32), left...]
    mul x2 -> x0, other arithmetic: 26.6 us -> none  [the longest x1 26.6 us: shards(): across = 0.5 * lon_metric * (east_cell - west_cell)]
    convert_element_type x3 -> x0, other arithmetic: 23.5 us -> none  [the longest x1 10.8 us: shards(): snapshot.astype(jnp.float32)]
  transfers between devices with their start and end apart: 8 -> 15, of which waited for: 2 -> 11; matrix products, arithmetic and copies ran while one was open for 7% -> 0% of each run, Pallas kernels for 0% -> 18%
where the time goes in v1:
time: 144 us
  Pallas kernels  79.2 us (55%)
  waiting for transfers between devices  36 us (25%)
  starting transfers between devices  21.1 us (15%)
  local copies, waits for them, and re-layouts  5.58 us (4%)
  between operations  1.5 us (1%)
    ppermute x10, waiting for transfers between devices, swap(): lax.ppermute(block, axis, [(i, i ^ 1 << bit) for i in range(lax.axis_size...  33.1 us
    pallas_call x1, Pallas kernels, pick(): pl.pallas_call(pick_kernel, grid_spec=pltpu.PrefetchScalarGridSpec(num_sc...  25.5 us
    pallas_call x1, Pallas kernels, factor(): pl.pallas_call(functools.partial(factor_kernel, scale), in_specs=[vmem],...  24.6 us
    pallas_call x1, Pallas kernels, stencil(): pl.pallas_call(stencil_kernel, grid=(width_x // group,), in_specs=[pl.Blo...  12.1 us
    ppermute x10, starting transfers between devices, swap(): lax.ppermute(block, axis, [(i, i ^ 1 << bit) for i in range(lax.axis_size...  11.7 us
    pallas_call x1, Pallas kernels, product(): pl.pallas_call(product_kernel, grid=(cells // width,), in_specs=[factor_s...  9.64 us
    pallas_call x1, Pallas kernels, relayout(): pl.pallas_call(functools.partial(relayout_kernel, width_y // 2), grid=(da...  6.67 us
    ppermute x1, starting transfers between devices, shards(): east = lax.ppermute(moved[:, 0], 'lon', [(t, s) for s, t in east_route])  6.06 us
  transfers between devices with their start and end apart: 15, of which 11 were waited for; matrix products, arithmetic and copies ran while one was open for 0% of the time, Pallas kernels for 18%

profile of v1, /device:TPU:0, one launch (start us, length us, event | category | flops | bytes accessed | tf_op | source)
XLA Modules:
  0.0 143.6 jit_solution(3769609809054113738)
XLA Ops:
  0.6 2.8 %copy-done.1 = bf16[2,256,48,128]{3,2,1,0:T(8,128)(2,1)S(1)} copy-done((bf16[2,256,48,128]{3,2,1,0:T(8,128)(2,1)S(1)}, bf16[2,256,48,128]{3,2,1,0:T(8,128)(2,1)}, u32[]{:S(2)}) %copy-start.1) | copy-done | bytes 6291480
  3.4 6.7 %relayout.1 = (bf16[2,48,256,128]{3,2,1,0:T(8,128)(2,1)S(1)}, bf16[256,128]{1,0:T(8,128)(2,1)S(1)}, bf16[256,128]{1,0:T(8,128)(2,1)S(1)}, bf16[256,128]{1,0:T(8,128)(2,1)S(1)}) custom-call(bf16[2,256,48,128]{3,2,1,0:T(8,128)(2,1)S(1)} %copy-done.1), custom_call_target="tpu_custom_call" | custom-call | tf_op jit(solution)/shard_map/relayout/pallas_call | solution.py:52
  10.1 2.7 %copy-done = bf16[2,48,256,128]{3,2,1,0:T(8,128)(2,1)} copy-done((bf16[2,48,256,128]{3,2,1,0:T(8,128)(2,1)}, bf16[2,48,256,128]{3,2,1,0:T(8,128)(2,1)S(1)}, u32[]{:S(2)}) %copy-start) | copy-done | bytes 6291480
  12.8 6.1 %collective-permute-start.1 = (bf16[2,256,128]{2,1,0:T(8,128)(2,1)S(1)}, bf16[2,256,128]{2,1,0:T(8,128)(2,1)S(1)}, u32[]{:S(2)}, u32[]{:S(2)}) collective-permute-start(bf16[2,256,128]{2,1,0:T(8,128)(2,1)S(1)} %get-tuple-element.24), channel_id=1, source_target_pairs={{1,0},{2,1},{3,2},{4,3},{5,4},{6,5},{7,6},{0,7},{9,8},{10,9},{11,1... | collective-permute-start | bytes 393224 | tf_op jit(solution)/shard_map/ppermute | solution.py:450
  18.9 1.5 %collective-permute-start.2 = (bf16[256,128]{1,0:T(8,128)(2,1)S(1)}, bf16[256,128]{1,0:T(8,128)(2,1)S(1)}, u32[]{:S(2)}, u32[]{:S(2)}) collective-permute-start(bf16[256,128]{1,0:T(8,128)(2,1)S(1)} %get-tuple-element.14), channel_id=1, source_target_pairs={{0,8},{8,16},{16,24},{1,9},{9,17},{17,25},{2,10},{10,18},{18,26},{... | collective-permute-start | bytes 196616 | tf_op jit(solution)/shard_map/ppermute | solution.py:452
  20.3 1.3 collective-permute-start.3
  23.7 1.3 collective-permute-done.3.north_ref
  25.1 1.5 %collective-permute-done.west_ref = bf16[2,256,128]{2,1,0:T(8,128)(2,1)S(1)} collective-permute-done((bf16[2,256,128]{2,1,0:T(8,128)(2,1)S(1)}, bf16[2,256,128]{2,1,0:T(8,128)(2,1)S(1)}, u32[]{:S(2)}, u32[]{:S(2)}) %collective-permute-start) | collective-permute-done | bytes 131104 | tf_op jit(solution)/shard_map/ppermute | solution.py:449
  26.5 12.1 %stencil_gram.1 = (bf16[512,6144]{1,0:T(8,128)(2,1)}, f32[10,128,128]{2,1,0:T(8,128)S(1)}) custom-call(bf16[2,48,256,128]{3,2,1,0:T(8,128)(2,1)} %copy-done, bf16[2,48,256,128]{3,2,1,0:T(8,128)(2,1)} %copy-done, bf16[2,48,256,128]{3,2,1,0:T(8,128)(2,1)} %copy-done, bf16[2,256,128]{2,1,0:T(8,128)(2,1)S(1)} %collective-permute-done.west_ref, ...), custom_call_target="tpu_custom_call" | custom-call | tf_op jit(solution)/shard_map/stencil_gram/pallas_call | solution.py:182
  38.6 1.6 %collective-permute-start.5 = (f32[640,128]{1,0:T(8,128)S(1)}, f32[640,128]{1,0:T(8,128)S(1)}, u32[]{:S(2)}, u32[]{:S(2)}) collective-permute-start(f32[640,128]{1,0:T(8,128)S(1)} %constant_dynamic-slice_fusion.4), channel_id=1, source_target_pairs={{0,8},{8,0},{16,24},{24,16},{1,9},{9,1},{17,25},{25,17},{2,10},{10... | collective-permute-start | bytes 983048 | tf_op jit(solution)/shard_map/ppermute | solution.py:220
  41.5 4.8 %collective-permute-start.6 = (f32[320,128]{1,0:T(8,128)S(1)}, f32[320,128]{1,0:T(8,128)S(1)}, u32[]{:S(2)}, u32[]{:S(2)}) collective-permute-start(f32[320,128]{1,0:T(8,128)S(1)} %constant_dynamic-slice_fusion.3), channel_id=1, source_target_pairs={{0,16},{8,24},{16,0},{24,8},{1,17},{9,25},{17,1},{25,9},{2,18},{10... | collective-permute-start | bytes 491528 | tf_op jit(solution)/shard_map/ppermute | solution.py:220
  46.3 4.7 %collective-permute-done.6 = f32[320,128]{1,0:T(8,128)S(1)} collective-permute-done((f32[320,128]{1,0:T(8,128)S(1)}, f32[320,128]{1,0:T(8,128)S(1)}, u32[]{:S(2)}, u32[]{:S(2)}) %collective-permute-start.6) | collective-permute-done | bytes 163872 | tf_op jit(solution)/shard_map/ppermute | solution.py:220
  51.2 4.4 %collective-permute-done.7 = f32[160,128]{1,0:T(8,128)S(1)} collective-permute-done((f32[160,128]{1,0:T(8,128)S(1)}, f32[160,128]{1,0:T(8,128)S(1)}, u32[]{:S(2)}, u32[]{:S(2)}) %collective-permute-start.7) | collective-permute-done | bytes 81952 | tf_op jit(solution)/shard_map/ppermute | solution.py:220
  55.7 4.0 %collective-permute-done.8 = f32[80,128]{1,0:T(8,128)S(1)} collective-permute-done((f32[80,128]{1,0:T(8,128)S(1)}, f32[80,128]{1,0:T(8,128)S(1)}, u32[]{:S(2)}, u32[]{:S(2)}) %collective-permute-start.8) | collective-permute-done | bytes 40992 | tf_op jit(solution)/shard_map/ppermute | solution.py:220
  59.7 1.6 %collective-permute-start.9 = (f32[40,128]{1,0:T(8,128)S(1)}, f32[40,128]{1,0:T(8,128)S(1)}, u32[]{:S(2)}, u32[]{:S(2)}) collective-permute-start(f32[40,128]{1,0:T(8,128)S(1)} %constant_dynamic-slice_fusion), channel_id=1, source_target_pairs={{0,4},{1,5},{2,6},{3,7},{4,0},{5,1},{6,2},{7,3},{8,12},{9,13},{10,... | collective-permute-start | bytes 61448 | tf_op jit(solution)/shard_map/ppermute | solution.py:220
  61.3 3.6 %collective-permute-done.9 = f32[40,128]{1,0:T(8,128)S(1)} collective-permute-done((f32[40,128]{1,0:T(8,128)S(1)}, f32[40,128]{1,0:T(8,128)S(1)}, u32[]{:S(2)}, u32[]{:S(2)}) %collective-permute-start.9) | collective-permute-done | bytes 20512 | tf_op jit(solution)/shard_map/ppermute | solution.py:220
  66.0 3.7 %collective-permute-done.10 = f32[40,128]{1,0:T(8,128)S(1)} collective-permute-done((f32[40,128]{1,0:T(8,128)S(1)}, f32[40,128]{1,0:T(8,128)S(1)}, u32[]{:S(2)}, u32[]{:S(2)}) %collective-permute-start.10) | collective-permute-done | bytes 20512 | tf_op jit(solution)/shard_map/ppermute | solution.py:220
  70.1 3.6 %collective-permute-done.11 = f32[80,128]{1,0:T(8,128)S(1)} collective-permute-done((f32[80,128]{1,0:T(8,128)S(1)}, f32[80,128]{1,0:T(8,128)S(1)}, u32[]{:S(2)}, u32[]{:S(2)}) %collective-permute-start.11) | collective-permute-done | bytes 40992 | tf_op jit(solution)/shard_map/ppermute | solution.py:220
  74.0 4.2 %collective-permute-done.12 = f32[160,128]{1,0:T(8,128)S(1)} collective-permute-done((f32[160,128]{1,0:T(8,128)S(1)}, f32[160,128]{1,0:T(8,128)S(1)}, u32[]{:S(2)}, u32[]{:S(2)}) %collective-permute-start.12) | collective-permute-done | bytes 81952 | tf_op jit(solution)/shard_map/ppermute | solution.py:220
  78.2 1.8 %collective-permute-start.13 = (f32[320,128]{1,0:T(8,128)S(1)}, f32[320,128]{1,0:T(8,128)S(1)}, u32[]{:S(2)}, u32[]{:S(2)}) collective-permute-start(f32[320,128]{1,0:T(8,128)S(1)} %maximum_select_fusion.2), channel_id=1, source_target_pairs={{0,16},{8,24},{16,0},{24,8},{1,17},{9,25},{17,1},{25,9},{2,18},{10... | collective-permute-start | bytes 491528 | tf_op jit(solution)/shard_map/ppermute | solution.py:220
  80.0 3.6 %collective-permute-done.13 = f32[320,128]{1,0:T(8,128)S(1)} collective-permute-done((f32[320,128]{1,0:T(8,128)S(1)}, f32[320,128]{1,0:T(8,128)S(1)}, u32[]{:S(2)}, u32[]{:S(2)}) %collective-permute-start.13) | collective-permute-done | bytes 163872 | tf_op jit(solution)/shard_map/ppermute | solution.py:220
  83.7 25.5 %pick.1.rows_ref = bf16[6144,512]{1,0:T(8,128)(2,1)} custom-call(s32[6144]{0:T(1024)S(1)} %copy-done.2, bf16[512,6144]{1,0:T(8,128)(2,1)} %get-tuple-element.22.fields_ref), custom_call_target="tpu_custom_call" | custom-call | tf_op jit(solution)/shard_map/pick/pallas_call | solution.py:284
  109.3 24.6 %factor.1 = (f32[512,512]{1,0:T(8,128)}, bf16[512,512]{1,0:T(8,128)(2,1)S(1)}, bf16[512,512]{1,0:T(8,128)(2,1)S(1)}) custom-call(f32[10,128,128]{2,1,0:T(8,128)S(1)} %bitcast.7), custom_call_target="tpu_custom_call" | custom-call | tf_op jit(solution)/shard_map/factor/pallas_call | solution.py:427
  134.0 9.6 %product.1 = bf16[512,6144]{1,0:T(8,128)(2,1)} custom-call(bf16[512,512]{1,0:T(8,128)(2,1)S(1)} %get-tuple-element.20.high_ref, bf16[512,512]{1,0:T(8,128)(2,1)S(1)} %get-tuple-element.21.low_ref, bf16[6144,512]{1,0:T(8,128)(2,1)} %pick.1.rows_ref), custom_call_target="tpu_custom_call" | custom-call | tf_op jit(solution)/shard_map/product/pallas_call | solution.py:321
  (38 shorter events, 4.9 us)
Async XLA Ops:
  0.6 2.8 %copy-start.1 = (bf16[2,256,48,128]{3,2,1,0:T(8,128)(2,1)S(1)}, bf16[2,256,48,128]{3,2,1,0:T(8,128)(2,1)}, u32[]{:S(2)}) copy-start(bf16[2,256,48,128]{3,2,1,0:T(8,128)(2,1)} %v_ref.1) | copy-start | bytes 18874372
  3.4 19.6 %copy-start.2 = (s32[6144]{0:T(1024)S(1)}, s32[6144]{0:T(1024)}, u32[]{:S(2)}) copy-start(s32[6144]{0:T(1024)} %index_ref.1) | copy-start | bytes 73732
  3.4 19.6 %copy-start.3 = (f32[48,128]{1,0:T(8,128)S(1)}, f32[48,128]{1,0:T(8,128)}, u32[]{:S(2)}) copy-start(f32[48,128]{1,0:T(8,128)} %lon_ref.1) | copy-start | bytes 73732
  3.4 19.6 %copy-start.4 = (f32[48,128]{1,0:T(8,128)S(1)}, f32[48,128]{1,0:T(8,128)}, u32[]{:S(2)}) copy-start(f32[48,128]{1,0:T(8,128)} %lat_ref.1) | copy-start | bytes 73732
  10.1 2.7 %copy-start = (bf16[2,48,256,128]{3,2,1,0:T(8,128)(2,1)}, bf16[2,48,256,128]{3,2,1,0:T(8,128)(2,1)S(1)}, u32[]{:S(2)}) copy-start(bf16[2,48,256,128]{3,2,1,0:T(8,128)(2,1)S(1)} %get-tuple-element.13.v_ref.left_ref.right_ref) | copy-start | bytes 18874372
  12.8 12.2 %collective-permute-start.1 = (bf16[2,256,128]{2,1,0:T(8,128)(2,1)S(1)}, bf16[2,256,128]{2,1,0:T(8,128)(2,1)S(1)}, u32[]{:S(2)}, u32[]{:S(2)}) collective-permute-start(bf16[2,256,128]{2,1,0:T(8,128)(2,1)S(1)} %get-tuple-element.24), channel_id=1, source_target_pairs={{1,0},{2,1},{3,2},{4,3},{5,4},{6,5},{7,6},{0,7},{9,8},{10,9},{11,1... | collective-permute-start | bytes 393224 | tf_op jit(solution)/shard_map/ppermute | solution.py:450
  18.9 7.7 %collective-permute-start = (bf16[2,256,128]{2,1,0:T(8,128)(2,1)S(1)}, bf16[2,256,128]{2,1,0:T(8,128)(2,1)S(1)}, u32[]{:S(2)}, u32[]{:S(2)}) collective-permute-start(bf16[2,256,128]{2,1,0:T(8,128)(2,1)S(1)} %get-tuple-element.25), channel_id=1, source_target_pairs={{0,1},{1,2},{2,3},{3,4},{4,5},{5,6},{6,7},{7,0},{8,9},{9,10},{10,1... | collective-permute-start | bytes 393224 | tf_op jit(solution)/shard_map/ppermute | solution.py:449
  18.9 4.8 %collective-permute-start.2 = (bf16[256,128]{1,0:T(8,128)(2,1)S(1)}, bf16[256,128]{1,0:T(8,128)(2,1)S(1)}, u32[]{:S(2)}, u32[]{:S(2)}) collective-permute-start(bf16[256,128]{1,0:T(8,128)(2,1)S(1)} %get-tuple-element.14), channel_id=1, source_target_pairs={{0,8},{8,16},{16,24},{1,9},{9,17},{17,25},{2,10},{10,18},{18,26},{... | collective-permute-start | bytes 196616 | tf_op jit(solution)/shard_map/ppermute | solution.py:452
  20.3 4.7 %collective-permute-start.3 = (bf16[256,128]{1,0:T(8,128)(2,1)S(1)}, bf16[256,128]{1,0:T(8,128)(2,1)S(1)}, u32[]{:S(2)}, u32[]{:S(2)}) collective-permute-start(bf16[256,128]{1,0:T(8,128)(2,1)S(1)} %get-tuple-element.15), channel_id=1, source_target_pairs={{8,0},{16,8},{24,16},{9,1},{17,9},{25,17},{10,2},{18,10},{26,18},{... | collective-permute-start | bytes 196616 | tf_op jit(solution)/shard_map/ppermute | solution.py:453
  21.6 3.4 %collective-permute-start.4 = (bf16[256,128]{1,0:T(8,128)(2,1)S(1)}, bf16[256,128]{1,0:T(8,128)(2,1)S(1)}, u32[]{:S(2)}, u32[]{:S(2)}) collective-permute-start(bf16[256,128]{1,0:T(8,128)(2,1)S(1)} %get-tuple-element.16), channel_id=1, source_target_pairs={{24,31},{25,30},{26,29},{27,28},{28,27},{29,26},{30,25},{31,24}} | collective-permute-start | bytes 196616 | tf_op jit(solution)/shard_map/ppermute | solution.py:455
  38.6 2.8 %collective-permute-start.5 = (f32[640,128]{1,0:T(8,128)S(1)}, f32[640,128]{1,0:T(8,128)S(1)}, u32[]{:S(2)}, u32[]{:S(2)}) collective-permute-start(f32[640,128]{1,0:T(8,128)S(1)} %constant_dynamic-slice_fusion.4), channel_id=1, source_target_pairs={{0,8},{8,0},{16,24},{24,16},{1,9},{9,1},{17,25},{25,17},{2,10},{10... | collective-permute-start | bytes 983048 | tf_op jit(solution)/shard_map/ppermute | solution.py:220
  41.5 9.5 %collective-permute-start.6 = (f32[320,128]{1,0:T(8,128)S(1)}, f32[320,128]{1,0:T(8,128)S(1)}, u32[]{:S(2)}, u32[]{:S(2)}) collective-permute-start(f32[320,128]{1,0:T(8,128)S(1)} %constant_dynamic-slice_fusion.3), channel_id=1, source_target_pairs={{0,16},{8,24},{16,0},{24,8},{1,17},{9,25},{17,1},{25,9},{2,18},{10... | collective-permute-start | bytes 491528 | tf_op jit(solution)/shard_map/ppermute | solution.py:220
  51.1 4.5 %collective-permute-start.7 = (f32[160,128]{1,0:T(8,128)S(1)}, f32[160,128]{1,0:T(8,128)S(1)}, u32[]{:S(2)}, u32[]{:S(2)}) collective-permute-start(f32[160,128]{1,0:T(8,128)S(1)} %constant_dynamic-slice_fusion.2), channel_id=1, source_target_pairs={{0,1},{1,0},{2,3},{3,2},{4,5},{5,4},{6,7},{7,6},{8,9},{9,8},{10,11... | collective-permute-start | bytes 245768 | tf_op jit(solution)/shard_map/ppermute | solution.py:220
  55.6 4.1 %collective-permute-start.8 = (f32[80,128]{1,0:T(8,128)S(1)}, f32[80,128]{1,0:T(8,128)S(1)}, u32[]{:S(2)}, u32[]{:S(2)}) collective-permute-start(f32[80,128]{1,0:T(8,128)S(1)} %constant_dynamic-slice_fusion.1), channel_id=1, source_target_pairs={{0,2},{1,3},{2,0},{3,1},{4,6},{5,7},{6,4},{7,5},{8,10},{9,11},{10,... | collective-permute-start | bytes 122888 | tf_op jit(solution)/shard_map/ppermute | solution.py:220
  59.7 5.1 %collective-permute-start.9 = (f32[40,128]{1,0:T(8,128)S(1)}, f32[40,128]{1,0:T(8,128)S(1)}, u32[]{:S(2)}, u32[]{:S(2)}) collective-permute-start(f32[40,128]{1,0:T(8,128)S(1)} %constant_dynamic-slice_fusion), channel_id=1, source_target_pairs={{0,4},{1,5},{2,6},{3,7},{4,0},{5,1},{6,2},{7,3},{8,12},{9,13},{10,... | collective-permute-start | bytes 61448 | tf_op jit(solution)/shard_map/ppermute | solution.py:220
  64.9 4.8 %collective-permute-start.10 = (f32[40,128]{1,0:T(8,128)S(1)}, f32[40,128]{1,0:T(8,128)S(1)}, u32[]{:S(2)}, u32[]{:S(2)}) collective-permute-start(f32[40,128]{1,0:T(8,128)S(1)} %dynamic-slice_add_fusion.4), channel_id=1, source_target_pairs={{0,4},{1,5},{2,6},{3,7},{4,0},{5,1},{6,2},{7,3},{8,12},{9,13},{10,... | collective-permute-start | bytes 61448 | tf_op jit(solution)/shard_map/ppermute | solution.py:220
  69.7 4.0 %collective-permute-start.11 = (f32[80,128]{1,0:T(8,128)S(1)}, f32[80,128]{1,0:T(8,128)S(1)}, u32[]{:S(2)}, u32[]{:S(2)}) collective-permute-start(f32[80,128]{1,0:T(8,128)S(1)} %maximum_select_fusion.4), channel_id=1, source_target_pairs={{0,2},{1,3},{2,0},{3,1},{4,6},{5,7},{6,4},{7,5},{8,10},{9,11},{10,... | collective-permute-start | bytes 122888 | tf_op jit(solution)/shard_map/ppermute | solution.py:220
  73.7 4.5 %collective-permute-start.12 = (f32[160,128]{1,0:T(8,128)S(1)}, f32[160,128]{1,0:T(8,128)S(1)}, u32[]{:S(2)}, u32[]{:S(2)}) collective-permute-start(f32[160,128]{1,0:T(8,128)S(1)} %maximum_select_fusion.3), channel_id=1, source_target_pairs={{0,1},{1,0},{2,3},{3,2},{4,5},{5,4},{6,7},{7,6},{8,9},{9,8},{10,11... | collective-permute-start | bytes 245768 | tf_op jit(solution)/shard_map/ppermute | solution.py:220
  78.2 5.4 %collective-permute-start.13 = (f32[320,128]{1,0:T(8,128)S(1)}, f32[320,128]{1,0:T(8,128)S(1)}, u32[]{:S(2)}, u32[]{:S(2)}) collective-permute-start(f32[320,128]{1,0:T(8,128)S(1)} %maximum_select_fusion.2), channel_id=1, source_target_pairs={{0,16},{8,24},{16,0},{24,8},{1,17},{9,25},{17,1},{25,9},{2,18},{10... | collective-permute-start | bytes 491528 | tf_op jit(solution)/shard_map/ppermute | solution.py:220
  83.7 25.6 %collective-permute-start.14 = (f32[640,128]{1,0:T(8,128)S(1)}, f32[640,128]{1,0:T(8,128)S(1)}, u32[]{:S(2)}, u32[]{:S(2)}) collective-permute-start(f32[640,128]{1,0:T(8,128)S(1)} %maximum_select_fusion.1), channel_id=1, source_target_pairs={{0,8},{8,0},{16,24},{24,16},{1,9},{9,1},{17,25},{25,17},{2,10},{10... | collective-permute-start | bytes 983048 | tf_op jit(solution)/shard_map/ppermute | solution.py:220

commit v2 on v1

v2 whole, which is shorter than its diff:
```python
import functools
import math

import jax
import jax.numpy as jnp
from jax import lax
from jax.experimental import pallas as pl
from jax.experimental.pallas import tpu as pltpu
from jax.sharding import PartitionSpec as P

F32 = jnp.float32
BF16 = jnp.bfloat16
MB = 1 << 20
ROOM = 24 * MB
TOKEN = jax.ShapeDtypeStruct((8, 128), F32)
NN = (((1,), (0,)), ((), ()))
NT = (((1,), (1,)), ((), ()))
TN = (((0,), (0,)), ((), ()))


def iota(shape, dim):
    return lax.broadcasted_iota(jnp.int32, shape, dim)


def lat_difference(width_y):
    wide = 2 * width_y
    k = iota((wide, wide), 0)
    n = iota((wide, wide), 1)
    same = k // width_y == n // width_y
    diff = jnp.where(same & (k == n + 1), 1.0, 0.0) - jnp.where(same & (k == n - 1), 1.0, 0.0)
    return diff.astype(BF16)


def gram_of(block, days):
    upper = lax.dot_general(block[:days, :], block, NT, preferred_element_type=F32)
    lower = lax.dot_general(block[days:, :], block[days:, :], NT, preferred_element_type=F32)
    return upper, lower


def front_kernel(
    v_hbm, index_hbm, count_ref, lon_hbm, lat_hbm,
    fields_hbm, total, lon_out, lat_out, south_ref, second_ref, north_ref, before_ref, fold_ref,
    x0_ref, x1_ref, x2_ref, x3_ref,
    index_ref, lon_ref, lat_ref, raw, moved, stage, lon_in, lat_in, sems, out_sems, small_sems,
):
    fields, days, width_x, width_y = v_hbm.shape
    step = raw.shape[2]
    half = width_y // 2

    def fetch(i):
        return pltpu.make_async_copy(
            v_hbm.at[:, pl.ds(i * step, step)], raw.at[i], sems.at[i]
        )

    small = [
        pltpu.make_async_copy(source, target, small_sems.at[i])
        for i, (source, target) in enumerate(
            ((index_hbm, index_ref), (lon_hbm, lon_ref), (lat_hbm, lat_ref))
        )
    ]
    for copy in small:
        copy.start()
    for i in range(days // step):
        fetch(i).start()
    for copy in small:
        copy.wait()

    cells = index_ref.shape[1]
    index = index_ref[...]
    wet = iota(index.shape, 1) < count_ref[0]
    row = jnp.where(wet, index // width_y, -1)
    col = index % width_y
    pick_x = jnp.where(iota((width_x, cells), 0) == row, 1.0, 0.0).astype(BF16)
    pick_y = jnp.where(iota((width_y, cells), 0) == col, 1.0, 0.0).astype(BF16)
    mask = lax.dot_general(pick_x, pick_y, NT, preferred_element_type=F32)
    x = iota((width_x, width_y), 0)
    y = iota((width_x, width_y), 1)
    inner = (x > 0) & (x < width_x - 1) & (y > 0) & (y < width_y - 1)
    lon = 0.5 * lon_ref[...] * mask
    lat = 0.5 * lat_ref[...] * mask
    lon_out[...] = lon
    lat_out[...] = lat
    lon_in[...] = jnp.where(inner, lon, 0.0)
    lat_in[...] = jnp.where(inner, lat, 0.0)

    lane = iota((16, width_y), 1)

    def turn(i, _):
        fetch(i).wait()
        for d in range(0, step, 16):
            south = second = north = before = jnp.zeros((16, width_y), BF16)
            rows = pl.ds(pl.multiple_of(i * step + d, 16), 16)
            for f in range(fields):
                columns = jnp.swapaxes(raw[i, f, d : d + 16], 0, 1)
                moved[f, :, rows, :] = columns
                for x in range(width_x):
                    at = f * half + x
                    turned = pltpu.roll(columns[x], at + 1, 1)
                    before = jnp.where(lane == (at - 1) % width_y, turned, before)
                    north = jnp.where(lane == at, turned, north)
                    south = jnp.where(lane == at + 1, turned, south)
                    second = jnp.where(lane == at + 2, turned, second)
            south_ref[rows, :] = pltpu.roll(south, width_y - 1, 1)
            second_ref[rows, :] = pltpu.roll(second, width_y - 2, 1)
            north_ref[rows, :] = north
            before_ref[rows, :] = pltpu.roll(before, 1, 1)
        return 0

    lax.fori_loop(0, days // step, turn, 0)
    k = iota((width_y, width_y), 0)
    n = iota((width_y, width_y), 1)
    mirror = (k // half == n // half) & (k + n == 2 * half * (n // half) + width_x - 1)
    mirror = jnp.where(mirror, -1.0, 0.0).astype(BF16)
    fold = lax.dot_general(north_ref[...], mirror, NN, preferred_element_type=F32)
    fold_ref[...] = fold.astype(BF16)
    x0_ref[...] = moved[:, 0]
    x1_ref[...] = moved[:, 1]
    x2_ref[...] = moved[:, width_x - 2]
    x3_ref[...] = moved[:, width_x - 1]

    wide = stage.shape[2]
    group = wide // width_y
    steps = width_x // group
    diff = lat_difference(width_y)
    total[...] = jnp.zeros_like(total)

    def send(i):
        slot = lax.rem(i, 2)
        place = pl.ds(pl.multiple_of(i * wide, wide), wide)
        return pltpu.make_async_copy(stage.at[slot], fields_hbm.at[:, place], out_sems.at[slot])

    def compute(i, _):
        slot = lax.rem(i, 2)

        @pl.when(i >= 2)
        def _():
            send(i - 2).wait()

        for g in range(group):
            x = i * group + g
            east = jnp.minimum(x + 1, width_x - 1)
            west = jnp.maximum(x - 1, 0)
            here = jnp.concatenate([moved[0, x], moved[1, x]], axis=1)
            along = lax.dot_general(here, diff, NN, preferred_element_type=F32)
            lon = lon_in[pl.ds(x, 1), :]
            lat = lat_in[pl.ds(x, 1), :]
            across_u = moved[0, east].astype(F32) - moved[0, west].astype(F32)
            across_v = moved[1, east].astype(F32) - moved[1, west].astype(F32)
            zeta = lon * across_v - lat * along[:, :width_y]
            divergence = lon * across_u + lat * along[:, width_y:]
            place = slice(g * width_y, (g + 1) * width_y)
            stage[slot, :days, place] = zeta.astype(BF16)
            stage[slot, days:, place] = divergence.astype(BF16)
        send(i).start()
        upper, lower = gram_of(stage[slot], days)
        total[:days, :] += upper
        total[days:, days:] += lower
        return 0

    lax.fori_loop(0, steps, compute, 0)
    for i in range(max(steps - 2, 0), steps):
        send(i).wait()


def front(velocity, wet_index, wet_count, lon_metric, lat_metric):
    fields, days, width_x, width_y = velocity.shape
    assert width_x <= width_y // 2 - 2
    step = next(n for n in (32, 16) if days % n == 0)
    group = next(n for n in (8, 6, 4, 3, 2, 1) if width_x % n == 0)
    vmem = pl.BlockSpec(memory_space=pltpu.VMEM)
    hbm = pl.BlockSpec(memory_space=pl.ANY)
    metric = jax.ShapeDtypeStruct((width_x, width_y), F32)
    edge = jax.ShapeDtypeStruct((days, width_y), BF16)
    column = jax.ShapeDtypeStruct((fields, days, width_y), BF16)
    return pl.pallas_call(
        front_kernel,
        in_specs=[hbm, hbm, pl.BlockSpec(memory_space=pltpu.SMEM), hbm, hbm],
        out_specs=[hbm] + [vmem] * 12,
        out_shape=[
            jax.ShapeDtypeStruct((2 * days, width_x * width_y), BF16),
            jax.ShapeDtypeStruct((2 * days, 2 * days), F32),
            metric, metric, edge, edge, edge, edge, edge, column, column, column, column,
        ],
        scratch_shapes=[
            pltpu.VMEM((1, width_x * width_y), jnp.int32),
            pltpu.VMEM((width_x, width_y), F32),
            pltpu.VMEM((width_x, width_y), F32),
            pltpu.VMEM((days // step, fields, step, width_x, width_y), BF16),
            pltpu.VMEM((fields, width_x, days, width_y), BF16),
            pltpu.VMEM((2, 2 * days, group * width_y), BF16),
            pltpu.VMEM((width_x, width_y), F32),
            pltpu.VMEM((width_x, width_y), F32),
            pltpu.SemaphoreType.DMA((days // step,)),
            pltpu.SemaphoreType.DMA((2,)),
            pltpu.SemaphoreType.DMA((3,)),
        ],
        compiler_params=pltpu.CompilerParams(vmem_limit_bytes=50 * MB),
        name="front",
    )(velocity, wet_index.reshape(1, -1), wet_count, lon_metric, lat_metric)


def rim_kernel(
    x0_ref, x1_ref, x2_ref, x3_ref, west_ref, east_ref, below_ref, above_ref, mirrored_ref,
    south_ref, second_ref, north_ref, before_ref, lon_ref, lat_ref, total_ref,
    gram_ref, rows_ref, ends_ref,
):
    _, days, width_y = x0_ref.shape
    width_x = lon_ref.shape[0]
    half = width_y // 2
    below = below_ref[...].astype(F32)
    above = above_ref[...].astype(F32) + mirrored_ref[...].astype(F32)
    lane = iota((1, width_y), 1)

    diff = lat_difference(width_y)
    column_lane = iota((days, width_y), 1)
    for end, x, own_ref, west, east in (
        (0, 0, x0_ref, west_ref, x1_ref),
        (1, width_x - 1, x3_ref, x2_ref, east_ref),
    ):
        here = jnp.concatenate([own_ref[0], own_ref[1]], axis=1)
        along = lax.dot_general(here, diff, NN, preferred_element_type=F32)
        lon = lon_ref[x : x + 1, :]
        lat = lat_ref[x : x + 1, :]
        flow = []
        for f in range(2):
            own = along[:, f * width_y : (f + 1) * width_y]
            at = f * half + x
            own = own - jnp.where(column_lane == 0, below[:, at : at + 1], 0.0)
            own = own + jnp.where(column_lane == width_y - 1, above[:, at : at + 1], 0.0)
            flow.append(own)
        across_u = east[0].astype(F32) - west[0].astype(F32)
        across_v = east[1].astype(F32) - west[1].astype(F32)
        ends_ref[end, :days, :] = (lon * across_v - lat * flow[0]).astype(BF16)
        ends_ref[end, days:, :] = (lon * across_u + lat * flow[1]).astype(BF16)

    fill = jnp.zeros((width_y - width_x, width_y), F32)
    lon_turned = jnp.concatenate([lon_ref[...], fill], axis=0).T
    lat_turned = jnp.concatenate([lat_ref[...], fill], axis=0).T
    spot = lane % half
    between = (spot > 0) & (spot < width_x - 1)
    parts = []
    for y, row, low, high in (
        (0, south_ref, below, second_ref[...].astype(F32)),
        (width_y - 1, north_ref, before_ref[...].astype(F32), above),
    ):
        lon = lon_turned[y : y + 1, :]
        lat = lat_turned[y : y + 1, :]
        lon = jnp.where(between, jnp.where(lane < half, lon, pltpu.roll(lon, half, 1)), 0.0)
        lat = jnp.where(between, jnp.where(lane < half, -lat, pltpu.roll(lat, half, 1)), 0.0)
        own = row[...].astype(F32)
        across = pltpu.roll(own, width_y - 1, 1) - pltpu.roll(own, 1, 1)
        parts.append(lon * pltpu.roll(across, half, 1) + lat * (high - low))
    low_lane = column_lane < half
    rows_ref[:days, :] = jnp.where(low_lane, parts[0], pltpu.roll(parts[1], half, 1)).astype(BF16)
    rows_ref[days:, :] = jnp.where(low_lane, pltpu.roll(parts[0], half, 1), parts[1]).astype(BF16)

    rim = jnp.concatenate([ends_ref[0], ends_ref[1], rows_ref[...]], axis=1)
    upper, lower = gram_of(rim, days)
    size = gram_ref.shape[1]
    at = 0
    for i in range(2 * days // size):
        for j in range(i, 2 * days // size):
            left = slice(i * size, (i + 1) * size)
            right = slice(j * size, (j + 1) * size)
            if i * size < days:
                extra = upper[left, right]
            else:
                extra = lower[
                    i * size - days : (i + 1) * size - days, j * size - days : (j + 1) * size - days
                ]
            gram_ref[at] = total_ref[left, right] + extra
            at += 1


def rim(ends, sides, edges, lon, lat, total, size):
    _, days, width_y = ends[0].shape
    count = 2 * days // size
    vmem = pl.BlockSpec(memory_space=pltpu.VMEM)
    operands = (*ends, *sides, *edges, lon, lat, total)
    return pl.pallas_call(
        rim_kernel,
        in_specs=[vmem] * len(operands),
        out_specs=[vmem] * 3,
        out_shape=[
            jax.ShapeDtypeStruct((count * (count + 1) // 2, size, size), F32),
            jax.ShapeDtypeStruct((2 * days, width_y), BF16),
            jax.ShapeDtypeStruct((2, 2 * days, width_y), BF16),
        ],
        compiler_params=pltpu.CompilerParams(vmem_limit_bytes=ROOM),
        name="rim",
    )(*operands)


def all_sum(x, beside):
    moves = []
    for axis in ("lat", "lon"):
        count = lax.axis_size(axis)
        assert count & (count - 1) == 0
        for bit in range(count.bit_length() - 1):
            moves.append((axis, bit))
    shape = x.shape
    x = x.reshape(-1, shape[-1])
    taken = []

    hops = 0

    def swap(block, axis, bit):
        nonlocal hops
        other = lax.ppermute(
            block, axis, [(i, i ^ 1 << bit) for i in range(lax.axis_size(axis))]
        )
        if hops in beside:
            other = other + beside[hops](block)[0, 0]
        hops += 1
        return other

    for axis, bit in moves:
        halve = x.shape[0] % 16 == 0 and x.shape[0] > shape[0] * 16
        if halve:
            half = x.shape[0] // 2
            high = (lax.axis_index(axis) >> bit) & 1
            keep = lax.dynamic_slice_in_dim(x, high * half, half, 0)
            send = lax.dynamic_slice_in_dim(x, (1 - high) * half, half, 0)
            x = keep + swap(send, axis, bit)
        else:
            x = x + swap(x, axis, bit)
        taken.append(halve)
    for (axis, bit), halve in reversed(list(zip(moves, taken))):
        if halve:
            high = (lax.axis_index(axis) >> bit) & 1
            other = swap(x, axis, bit)
            x = jnp.where(
                high == 1, jnp.concatenate([other, x], 0), jnp.concatenate([x, other], 0)
            )
    return x.reshape(shape)


def pick_kernel(
    piece, index_hbm, fields_hbm, rim_ref, ends_ref, after_ref, out_hbm, token_ref,
    index_ref, stage, rows, picked, turned_out, sems, out_sems,
):
    token_ref[...] = jnp.zeros_like(token_ref)
    columns, wide = rim_ref.shape
    count = out_hbm.shape[0]
    cells = fields_hbm.shape[1]
    width_x = cells // wide
    parts = columns // 128
    chunk = stage.shape[2]

    def fetch(i):
        return pltpu.make_async_copy(
            fields_hbm.at[:, i * chunk : (i + 1) * chunk], stage.at[i], sems.at[i]
        )

    places = pltpu.make_async_copy(index_hbm, index_ref, out_sems.at[2])
    places.start()
    for i in range(cells // chunk):
        fetch(i).start()
    unit = jnp.where(iota((wide, wide), 0) == iota((wide, wide), 1), 1.0, 0.0).astype(BF16)

    def turned(block):
        return lax.dot_general(unit, block, NT, preferred_element_type=F32)

    rim = turned(rim_ref[...])
    for i in range(cells // chunk):
        fetch(i).wait()
        for x in range(i * chunk // wide, (i + 1) * chunk // wide):
            at = x * wide * parts
            last = x == width_x - 1
            inside = x > 0 and not last
            if inside:
                start = x * wide - i * chunk
                block = turned(stage[i, :, start : start + wide])
            else:
                block = turned(ends_ref[int(last)])
            for c in range(parts):
                own = slice(c * 128, (c + 1) * 128)
                rows[pl.ds(at + c, wide, stride=parts), :] = block[:, own]
                if inside:
                    rows[at + c : at + c + 1, :] = rim[x : x + 1, own]
                    end = at + (wide - 1) * parts + c
                    rows[end : end + 1, :] = rim[wide // 2 + x : wide // 2 + x + 1, own]

    places.wait()
    share = picked.shape[1] // parts
    block = turned_out.shape[1]

    def row(at):
        return rows[pl.ds(pl.multiple_of(index_ref[at], parts), parts), :]

    def send(i):
        return pltpu.make_async_copy(
            turned_out.at[i % 2], out_hbm.at[i * block : (i + 1) * block], out_sems.at[i % 2]
        )

    for i in range(count // block):
        if i >= 2:
            send(i - 2).wait()

        def body(k, _):
            start = k * share
            slot = lax.rem(k, 2)
            source = piece * count + i * block + start
            for j in range(0, share, 2):
                pair = jnp.concatenate([row(source + j), row(source + j + 1)], axis=0)
                picked[slot, j * parts : (j + 2) * parts, :] = pair
            for c in range(parts):
                part = picked[slot, pl.ds(c, share, stride=parts), :]
                turned_out[
                    i % 2, pl.ds(pl.multiple_of(start, share), share), c * 128 : (c + 1) * 128
                ] = part.astype(BF16)
            return 0

        lax.fori_loop(0, block // share, body, 0)
        send(i).start()
    for i in range(max(count // block - 2, 0), count // block):
        send(i).wait()


def pick(piece, pieces, places, fields, rim, ends, after):
    columns, cells = fields.shape
    wide = rim.shape[1]
    parts = columns // 128
    share = 64
    block = next(n for n in (768, 512, 256, 128, 64) if cells % (pieces * n) == 0)
    chunk = next(n * wide for n in (8, 6, 4, 3, 2, 1) if cells % (n * wide) == 0)
    vmem = pl.BlockSpec(memory_space=pltpu.VMEM)
    hbm = pl.BlockSpec(memory_space=pl.ANY)
    return pl.pallas_call(
        functools.partial(pick_kernel, piece),
        in_specs=[hbm, hbm, vmem, vmem, hbm],
        out_specs=[hbm, vmem],
        out_shape=[jax.ShapeDtypeStruct((cells // pieces, columns), BF16), TOKEN],
        scratch_shapes=[
            pltpu.SMEM((cells,), jnp.int32),
            pltpu.VMEM((cells // chunk, columns, chunk), BF16),
            pltpu.VMEM((cells * parts, 128), F32),
            pltpu.VMEM((2, share * parts, 128), F32),
            pltpu.VMEM((2, block, columns), BF16),
            pltpu.SemaphoreType.DMA((cells // chunk,)),
            pltpu.SemaphoreType.DMA((3,)),
        ],
        compiler_params=pltpu.CompilerParams(vmem_limit_bytes=50 * MB),
        name="pick",
    )(places, fields, rim, ends, after)


def product_kernel(steps, high_ref, low_ref, *refs):
    out_ref = refs[-1]
    columns = high_ref.shape[0]
    half = columns // 2

    def dot(w, s):
        return lax.dot_general(w, s, NT, preferred_element_type=F32)

    for piece, rows_ref in enumerate(refs[:-1]):

        @pl.when(pl.program_id(0) // steps == piece)
        def _():
            s = rows_ref[...]
            low = s[:, :half]
            top = dot(low_ref[:half, :half], low) + dot(high_ref[:half, :half], low)
            out_ref[:half, :] = top.astype(BF16)
            bottom = dot(low_ref[half:, :], s) + dot(high_ref[half:, :], s)
            out_ref[half:, :] = bottom.astype(BF16)


def product(high, low, pieces):
    count, columns = pieces[0].shape
    width = next(c for c in (768, 512, 256, 128) if count % c == 0)
    steps = count // width
    vmem = pl.BlockSpec(memory_space=pltpu.VMEM)
    return pl.pallas_call(
        functools.partial(product_kernel, steps),
        grid=(len(pieces) * steps,),
        in_specs=[vmem, vmem]
        + [
            pl.BlockSpec((width, columns), lambda i, k=k: (jnp.clip(i - k * steps, 0, steps - 1), 0))
            for k in range(len(pieces))
        ],
        out_specs=pl.BlockSpec((columns, width), lambda i: (0, i)),
        out_shape=jax.ShapeDtypeStruct((columns, len(pieces) * count), BF16),
        compiler_params=pltpu.CompilerParams(vmem_limit_bytes=50 * MB),
        name="product",
    )(high, low, *pieces)


def sublane(x, t):
    return jnp.broadcast_to(x[t : t + 1, :], x.shape)


def inverse_factor(block):
    size = block.shape[0]
    count = size // 8
    lane = iota((8, size), 1)
    row = iota((8, size), 0)
    tiles = [block[8 * p : 8 * p + 8, :] for p in range(count)]
    out = []
    for p in range(count):
        base = 8 * p
        cols = {
            q: [jnp.broadcast_to(tiles[q][:, base + t : base + t + 1], (8, size)) for t in range(8)]
            for q in range(p, count)
        }
        own = (lane >= base) & (lane < base + 8)
        work = jnp.where(own, jnp.where(lane == base + row, 1.0, 0.0), tiles[p])
        head = cols[p]
        done = jnp.zeros((8, size), F32)
        pivots = jnp.ones((8, size), F32)
        for t in range(8):
            at = row == t
            pivot = sublane(head[t], t)
            inverse = 1.0 / pivot
            coef = jnp.where(at, inverse, -head[t] * inverse)
            line = sublane(work, t)
            done = jnp.where(at, line, done)
            pivots = jnp.where(at, pivot, pivots)
            for u in range(t + 1, 8):
                head[u] = jnp.where(at, 0.0, head[u]) + coef * sublane(head[u], t)
            work = jnp.where(at, 0.0, work) + coef * line
        out.append(jnp.where(lane <= base + row, done * lax.rsqrt(pivots), 0.0))
        lines = [sublane(work, t) for t in range(8)]
        for q in range(p + 1, count):
            terms = [cols[q][t] * lines[t] for t in range(8)]
            while len(terms) > 1:
                terms = [terms[i] + terms[i + 1] for i in range(0, len(terms), 2)]
            tiles[q] = jnp.where(own, 0.0, tiles[q]) - terms[0]
    return jnp.concatenate(out, axis=0)


def factor_kernel(scale, pieces_ref, r_ref, high_ref, low_ref, work):
    columns = r_ref.shape[0]
    size = pieces_ref.shape[1]
    count = columns // size
    at = 0
    for i in range(count):
        for j in range(i, count):
            work[i * size : (i + 1) * size, j * size : (j + 1) * size] = pieces_ref[at]
            at += 1
        if i:
            work[i * size : (i + 1) * size, : i * size] = jnp.zeros((size, i * size), F32)

    def dot(a, b, dims):
        return lax.dot_general(
            a, b, dims, preferred_element_type=F32, precision=lax.Precision.HIGHEST
        )

    lane = iota((size, columns), 1)

    def step(k, _):
        here = pl.multiple_of(k * size, size)
        diagonal = work[pl.ds(here, size), pl.ds(here, size)]
        inverse = inverse_factor(diagonal)
        corner = dot(inverse, diagonal, NN)
        work[pl.ds(here, size), pl.ds(here, size)] = jnp.where(
            iota((size, size), 0) == iota((size, size), 1), 1.0, 0.0
        )
        fresh = dot(inverse, work[pl.ds(here, size), :], NN)
        work[pl.ds(here, size), :] = fresh
        for i in range(1, count):

            @pl.when(i > k)
            def _():
                mine = slice(i * size, (i + 1) * size)
                work[mine, pl.ds(here, size)] = jnp.zeros((size, size), F32)
                work[mine, :] -= dot(work[pl.ds(here, size), mine], work[pl.ds(here, size), :], TN)

        known = jnp.where(lane < here + size, fresh * scale, 0.0)
        high = known.astype(BF16)
        high_ref[pl.ds(here, size), :] = high
        low_ref[pl.ds(here, size), :] = (known - high.astype(F32)).astype(BF16)
        r_ref[pl.ds(here, size), :] = jnp.where(lane >= here + size, fresh * (1.0 / scale), 0.0)
        upper = iota((size, size), 0) <= iota((size, size), 1)
        r_ref[pl.ds(here, size), pl.ds(here, size)] = jnp.where(upper, corner * (1.0 / scale), 0.0)
        return 0

    lax.fori_loop(0, count, step, 0)


def factor(pieces, columns, scale):
    vmem = pl.BlockSpec(memory_space=pltpu.VMEM)
    square = (columns, columns)
    return pl.pallas_call(
        functools.partial(factor_kernel, scale),
        in_specs=[vmem],
        out_specs=[vmem] * 3,
        out_shape=[
            jax.ShapeDtypeStruct(square, F32),
            jax.ShapeDtypeStruct(square, BF16),
            jax.ShapeDtypeStruct(square, BF16),
        ],
        scratch_shapes=[pltpu.VMEM(square, F32)],
        compiler_params=pltpu.CompilerParams(vmem_limit_bytes=ROOM),
        name="factor",
    )(pieces)


def shards(velocity, lon_metric, lat_metric, wet_index, wet_count):
    days = velocity.shape[1]
    cells = velocity.shape[2] * velocity.shape[3]
    columns = 2 * days
    lats, lons = lax.axis_size("lat"), lax.axis_size("lon")
    fields, total, lon, lat, south, second, north, before, fold, *outer = front(
        velocity, wet_index, wet_count, lon_metric, lat_metric
    )
    east_route = [(i, (i + 1) % lons) for i in range(lons)]
    west = lax.ppermute(outer[3], "lon", east_route)
    east = lax.ppermute(outer[0], "lon", [(t, s) for s, t in east_route])
    up = [(i, i + 1) for i in range(lats - 1)]
    below = lax.ppermute(north, "lat", up)
    above = lax.ppermute(south, "lat", [(t, s) for s, t in up])
    top = (lats - 1) * lons
    mirrored = lax.ppermute(fold, ("lat", "lon"), [(top + i, top + lons - 1 - i) for i in range(lons)])
    sides = (west, east, below, above, mirrored)
    edges = (south, second, north, before)
    gram, rows, ends = rim(outer, sides, edges, lon, lat, total, min(128, columns))

    places = wet_index * (columns // 128)
    pieces = 1
    held = {}

    def picking(piece, after):
        held[piece], token = pick(piece, pieces, places, fields, rows, ends, after)
        return token

    beside = {2 + piece: functools.partial(picking, piece) for piece in range(pieces)}
    total = all_sum(gram, beside)
    scale = math.sqrt(cells * lats * lons)
    triangle, high, low = factor(total, columns, scale)
    return product(high, low, [held[piece] for piece in range(pieces)]), triangle


def solution(mesh):
    placed = (
        P(None, None, "lon", "lat"),
        P("lon", "lat"),
        P("lon", "lat"),
        P(("lat", "lon")),
        P(("lat", "lon")),
    )
    return jax.shard_map(
        shards,
        mesh=mesh,
        in_specs=placed,
        out_specs=(P(None, ("lat", "lon")), P()),
        check_vma=False,
    )
```

time: 144 us -> 116 us (0.81)
  Pallas kernels: 79.2 us -> 61.8 us
  waiting for transfers between devices: 36 us -> 30.2 us
  local copies, waits for them, and re-layouts: 5.58 us -> 2.79 us
  starting transfers between devices: 21.1 us -> 18.6 us
    pallas_call x5 -> x4, Pallas kernels: 54.6 us -> 37.2 us  [the longest x1 14 us: front(): pl.pallas_call(front_kernel, in_specs=[hbm, hbm, pl.BlockSpec(memory_spac...]
    ppermute x10 -> x8, waiting for transfers between devices: 33.1 us -> 26.2 us  [swap(): lax.ppermute(block, axis, [(i, i ^ 1 << bit) for i in range(lax.axis_size...]
    unnamed x10 -> x8, local copies, waits for them, and re-layouts: 5.49 us -> 2.21 us
    ppermute x10 -> x8, starting transfers between devices: 11.7 us -> 8.93 us  [swap(): lax.ppermute(block, axis, [(i, i ^ 1 << bit) for i in range(lax.axis_size...]
    ppermute x1, waiting for transfers between devices: 1.35 us -> 3.19 us  [shards(): above = lax.ppermute(south, 'lat', [(t, s) for s, t in up])]
  transfers between devices with their start and end apart: 15 -> 13, of which waited for: 11 -> 9; matrix products, arithmetic and copies ran while one was open for 0% -> 0% of each run, Pallas kernels for 18% -> 10%
where the time goes in v2:
time: 116 us
  Pallas kernels  61.8 us (53%)
  waiting for transfers between devices  30.2 us (26%)
  starting transfers between devices  18.6 us (16%)
  local copies, waits for them, and re-layouts  2.79 us (2%)
  between operations  1.47 us (1%)
    ppermute x8, waiting for transfers between devices, swap(): lax.ppermute(block, axis, [(i, i ^ 1 << bit) for i in range(lax.axis_size...  26.2 us
    pallas_call x1, Pallas kernels, factor(): pl.pallas_call(functools.partial(factor_kernel, scale), in_specs=[vmem],...  24.6 us
    pallas_call x1, Pallas kernels, front(): pl.pallas_call(front_kernel, in_specs=[hbm, hbm, pl.BlockSpec(memory_spac...  14 us
    pallas_call x1, Pallas kernels, pick(): pl.pallas_call(functools.partial(pick_kernel, piece), in_specs=[hbm, hbm,...  11.6 us
    pallas_call x1, Pallas kernels, product(): pl.pallas_call(functools.partial(product_kernel, steps), grid=(len(pieces...  10.6 us
    ppermute x8, starting transfers between devices, swap(): lax.ppermute(block, axis, [(i, i ^ 1 << bit) for i in range(lax.axis_size...  8.93 us
    ppermute x1, starting transfers between devices, shards(): east = lax.ppermute(outer[0], 'lon', [(t, s) for s, t in east_route])  6.06 us
    ppermute x1, waiting for transfers between devices, shards(): above = lax.ppermute(south, 'lat', [(t, s) for s, t in up])  3.19 us
  transfers between devices with their start and end apart: 13, of which 9 were waited for; matrix products, arithmetic and copies ran while one was open for 0% of the time, Pallas kernels for 10%

profile of v2, /device:TPU:0, one launch (start us, length us, event | category | flops | bytes accessed | tf_op | source)
XLA Modules:
  0.0 115.6 jit_solution(1727190339350767356)
XLA Ops:
  1.3 0.7 copy-done
  2.0 0.7 copy-done.2
  2.8 0.7 copy-done.3
  3.5 14.0 %front.1 = (bf16[512,6144]{1,0:T(8,128)(2,1)}, f32[512,512]{1,0:T(8,128)S(1)}, f32[48,128]{1,0:T(8,128)S(1)}, f32[48,128]{1,0:T(8,128)S(1)}, bf16[256,128]{1,0:T...) custom-call(bf16[2,256,48,128]{3,2,1,0:T(8,128)(2,1)} %v_hbm.1, ...), custom_call_target="tpu_custom_call" | custom-call | tf_op jit(solution)/shard_map/front/pallas_call | solution.py:175
  17.6 6.1 %collective-permute-start.1 = (bf16[2,256,128]{2,1,0:T(8,128)(2,1)S(1)}, bf16[2,256,128]{2,1,0:T(8,128)(2,1)S(1)}, u32[]{:S(2)}, u32[]{:S(2)}) collective-permute-start(bf16[2,256,128]{2,1,0:T(8,128)(2,1)S(1)} %get-tuple-element.23.x0_ref), channel_id=1, source_target_pairs={{1,0},{2,1},{3,2},{4,3},{5,4},{6,5},{7,6},{0,7},{9,8},{10,9},{11,1... | collective-permute-start | bytes 393224 | tf_op jit(solution)/shard_map/ppermute | solution.py:608
  23.6 0.7 collective-permute-start.4
  24.3 1.5 %collective-permute-start.2 = (bf16[256,128]{1,0:T(8,128)(2,1)S(1)}, bf16[256,128]{1,0:T(8,128)(2,1)S(1)}, u32[]{:S(2)}, u32[]{:S(2)}) collective-permute-start(bf16[256,128]{1,0:T(8,128)(2,1)S(1)} %get-tuple-element.27.north_ref), channel_id=1, source_target_pairs={{0,8},{8,16},{16,24},{1,9},{9,17},{17,25},{2,10},{10,18},{18,26},{... | collective-permute-start | bytes 196616 | tf_op jit(solution)/shard_map/ppermute | solution.py:610
  25.7 1.5 %collective-permute-start.3 = (bf16[256,128]{1,0:T(8,128)(2,1)S(1)}, bf16[256,128]{1,0:T(8,128)(2,1)S(1)}, u32[]{:S(2)}, u32[]{:S(2)}) collective-permute-start(bf16[256,128]{1,0:T(8,128)(2,1)S(1)} %get-tuple-element.28.south_ref), channel_id=1, source_target_pairs={{8,0},{16,8},{24,16},{9,1},{17,9},{25,17},{10,2},{18,10},{26,18},{... | collective-permute-start | bytes 196616 | tf_op jit(solution)/shard_map/ppermute | solution.py:611
  27.3 3.2 %collective-permute-done.3.above_ref = bf16[256,128]{1,0:T(8,128)(2,1)S(1)} collective-permute-done((bf16[256,128]{1,0:T(8,128)(2,1)S(1)}, bf16[256,128]{1,0:T(8,128)(2,1)S(1)}, u32[]{:S(2)}, u32[]{:S(2)}) %collective-permute-start.3) | collective-permute-done | bytes 65568 | tf_op jit(solution)/shard_map/ppermute | solution.py:611
  30.4 0.8 collective-permute-done.west_ref
  31.3 0.9 rim.1
  32.2 5.4 %collective-permute-start.5 = (f32[640,128]{1,0:T(8,128)S(1)}, f32[640,128]{1,0:T(8,128)S(1)}, u32[]{:S(2)}, u32[]{:S(2)}) collective-permute-start(f32[640,128]{1,0:T(8,128)S(1)} %constant_dynamic-slice_fusion.2), channel_id=1, source_target_pairs={{0,8},{8,0},{16,24},{24,16},{1,9},{9,1},{17,25},{25,17},{2,10},{10... | collective-permute-start | bytes 983048 | tf_op jit(solution)/shard_map/ppermute | solution.py:309
  37.6 1.3 %collective-permute-done.5 = f32[640,128]{1,0:T(8,128)S(1)} collective-permute-done((f32[640,128]{1,0:T(8,128)S(1)}, f32[640,128]{1,0:T(8,128)S(1)}, u32[]{:S(2)}, u32[]{:S(2)}) %collective-permute-start.5) | collective-permute-done | bytes 327712 | tf_op jit(solution)/shard_map/ppermute | solution.py:309
  39.2 6.3 %collective-permute-done.6 = f32[320,128]{1,0:T(8,128)S(1)} collective-permute-done((f32[320,128]{1,0:T(8,128)S(1)}, f32[320,128]{1,0:T(8,128)S(1)}, u32[]{:S(2)}, u32[]{:S(2)}) %collective-permute-start.6) | collective-permute-done | bytes 163872 | tf_op jit(solution)/shard_map/ppermute | solution.py:309
  45.6 11.6 %pick.1 = (bf16[6144,512]{1,0:T(8,128)(2,1)}, f32[8,128]{1,0:T(8,128)S(1)}) custom-call(s32[6144]{0:T(1024)S(1)} %broadcast_multiply_fusion.index_hbm, bf16[512,6144]{1,0:T(8,128)(2,1)} %get-tuple-element.36.fields_hbm, bf16[512,128]{1,0:T(8,128)(2,1)S(1)} %get-tuple-element.37.rim_ref, bf16[2,512,128]{2,1,0:T(8,128)(2,1)S(1)} %get-tuple-element.38.ends_ref, ...), custom_call_target="tpu_custom_call" | custom-call | tf_op jit(solution)/shard_map/pick/pallas_call | solution.py:429
  57.8 0.7 add_add_fusion
  58.5 4.4 %collective-permute-done.8 = f32[160,128]{1,0:T(8,128)S(1)} collective-permute-done((f32[160,128]{1,0:T(8,128)S(1)}, f32[160,128]{1,0:T(8,128)S(1)}, u32[]{:S(2)}, u32[]{:S(2)}) %collective-permute-start.8) | collective-permute-done | bytes 81952 | tf_op jit(solution)/shard_map/ppermute | solution.py:309
  63.6 5.1 %collective-permute-done.9 = f32[160,128]{1,0:T(8,128)S(1)} collective-permute-done((f32[160,128]{1,0:T(8,128)S(1)}, f32[160,128]{1,0:T(8,128)S(1)}, u32[]{:S(2)}, u32[]{:S(2)}) %collective-permute-start.9) | collective-permute-done | bytes 81952 | tf_op jit(solution)/shard_map/ppermute | solution.py:309
  68.7 2.1 %collective-permute-start.10 = (f32[160,128]{1,0:T(8,128)S(1)}, f32[160,128]{1,0:T(8,128)S(1)}, u32[]{:S(2)}, u32[]{:S(2)}) collective-permute-start(f32[160,128]{1,0:T(8,128)S(1)} %add.51), channel_id=1, source_target_pairs={{0,1},{1,0},{2,3},{3,2},{4,5},{5,4},{6,7},{7,6},{8,9},{9,8},{10,11... | collective-permute-start | bytes 245768 | tf_op jit(solution)/shard_map/ppermute | solution.py:309
  70.8 2.5 %collective-permute-done.10 = f32[160,128]{1,0:T(8,128)S(1)} collective-permute-done((f32[160,128]{1,0:T(8,128)S(1)}, f32[160,128]{1,0:T(8,128)S(1)}, u32[]{:S(2)}, u32[]{:S(2)}) %collective-permute-start.10) | collective-permute-done | bytes 81952 | tf_op jit(solution)/shard_map/ppermute | solution.py:309
  73.6 5.0 %collective-permute-done.11 = f32[320,128]{1,0:T(8,128)S(1)} collective-permute-done((f32[320,128]{1,0:T(8,128)S(1)}, f32[320,128]{1,0:T(8,128)S(1)}, u32[]{:S(2)}, u32[]{:S(2)}) %collective-permute-start.11) | collective-permute-done | bytes 163872 | tf_op jit(solution)/shard_map/ppermute | solution.py:309
  78.7 1.6 %collective-permute-done.12 = f32[640,128]{1,0:T(8,128)S(1)} collective-permute-done((f32[640,128]{1,0:T(8,128)S(1)}, f32[640,128]{1,0:T(8,128)S(1)}, u32[]{:S(2)}, u32[]{:S(2)}) %collective-permute-start.12) | collective-permute-done | bytes 327712 | tf_op jit(solution)/shard_map/ppermute | solution.py:309
  80.4 24.6 %factor.1 = (f32[512,512]{1,0:T(8,128)}, bf16[512,512]{1,0:T(8,128)(2,1)S(1)}, bf16[512,512]{1,0:T(8,128)(2,1)S(1)}) custom-call(f32[10,128,128]{2,1,0:T(8,128)S(1)} %bitcast.4), custom_call_target="tpu_custom_call" | custom-call | tf_op jit(solution)/shard_map/factor/pallas_call | solution.py:583
  105.0 10.6 %product.1 = bf16[512,6144]{1,0:T(8,128)(2,1)} custom-call(bf16[512,512]{1,0:T(8,128)(2,1)S(1)} %get-tuple-element.40.high_ref, bf16[512,512]{1,0:T(8,128)(2,1)S(1)} %get-tuple-element.41.low_ref, bf16[6144,512]{1,0:T(8,128)(2,1)} %get-tuple-element.42.refs_0_), custom_call_target="tpu_custom_call" | custom-call | tf_op jit(solution)/shard_map/product/pallas_call | solution.py:473
  (28 shorter events, 2.2 us)
Async XLA Ops:
  1.3 0.7 copy-start
  2.0 0.7 copy-start.2
  2.8 0.7 copy-start.3
  3.5 42.1 %copy-start.1 = (s32[6144]{0:T(1024)S(1)}, s32[6144]{0:T(1024)}, u32[]{:S(2)}) copy-start(s32[6144]{0:T(1024)} %param.8) | copy-start | bytes 73732
  17.6 12.9 %collective-permute-start.1 = (bf16[2,256,128]{2,1,0:T(8,128)(2,1)S(1)}, bf16[2,256,128]{2,1,0:T(8,128)(2,1)S(1)}, u32[]{:S(2)}, u32[]{:S(2)}) collective-permute-start(bf16[2,256,128]{2,1,0:T(8,128)(2,1)S(1)} %get-tuple-element.23.x0_ref), channel_id=1, source_target_pairs={{1,0},{2,1},{3,2},{4,3},{5,4},{6,5},{7,6},{0,7},{9,8},{10,9},{11,1... | collective-permute-start | bytes 393224 | tf_op jit(solution)/shard_map/ppermute | solution.py:608
  23.6 7.7 %collective-permute-start = (bf16[2,256,128]{2,1,0:T(8,128)(2,1)S(1)}, bf16[2,256,128]{2,1,0:T(8,128)(2,1)S(1)}, u32[]{:S(2)}, u32[]{:S(2)}) collective-permute-start(bf16[2,256,128]{2,1,0:T(8,128)(2,1)S(1)} %get-tuple-element.26.x3_ref), channel_id=1, source_target_pairs={{0,1},{1,2},{2,3},{3,4},{4,5},{5,6},{6,7},{7,0},{8,9},{9,10},{10,1... | collective-permute-start | bytes 393224 | tf_op jit(solution)/shard_map/ppermute | solution.py:607
  23.6 3.6 %collective-permute-start.4 = (bf16[256,128]{1,0:T(8,128)(2,1)S(1)}, bf16[256,128]{1,0:T(8,128)(2,1)S(1)}, u32[]{:S(2)}, u32[]{:S(2)}) collective-permute-start(bf16[256,128]{1,0:T(8,128)(2,1)S(1)} %get-tuple-element.29), channel_id=1, source_target_pairs={{24,31},{25,30},{26,29},{27,28},{28,27},{29,26},{30,25},{31,24}} | collective-permute-start | bytes 196616 | tf_op jit(solution)/shard_map/ppermute | solution.py:613
  24.3 3.0 %collective-permute-start.2 = (bf16[256,128]{1,0:T(8,128)(2,1)S(1)}, bf16[256,128]{1,0:T(8,128)(2,1)S(1)}, u32[]{:S(2)}, u32[]{:S(2)}) collective-permute-start(bf16[256,128]{1,0:T(8,128)(2,1)S(1)} %get-tuple-element.27.north_ref), channel_id=1, source_target_pairs={{0,8},{8,16},{16,24},{1,9},{9,17},{17,25},{2,10},{10,18},{18,26},{... | collective-permute-start | bytes 196616 | tf_op jit(solution)/shard_map/ppermute | solution.py:610
  25.7 4.7 %collective-permute-start.3 = (bf16[256,128]{1,0:T(8,128)(2,1)S(1)}, bf16[256,128]{1,0:T(8,128)(2,1)S(1)}, u32[]{:S(2)}, u32[]{:S(2)}) collective-permute-start(bf16[256,128]{1,0:T(8,128)(2,1)S(1)} %get-tuple-element.28.south_ref), channel_id=1, source_target_pairs={{8,0},{16,8},{24,16},{9,1},{17,9},{25,17},{10,2},{18,10},{26,18},{... | collective-permute-start | bytes 196616 | tf_op jit(solution)/shard_map/ppermute | solution.py:611
  32.2 6.7 %collective-permute-start.5 = (f32[640,128]{1,0:T(8,128)S(1)}, f32[640,128]{1,0:T(8,128)S(1)}, u32[]{:S(2)}, u32[]{:S(2)}) collective-permute-start(f32[640,128]{1,0:T(8,128)S(1)} %constant_dynamic-slice_fusion.2), channel_id=1, source_target_pairs={{0,8},{8,0},{16,24},{24,16},{1,9},{9,1},{17,25},{25,17},{2,10},{10... | collective-permute-start | bytes 983048 | tf_op jit(solution)/shard_map/ppermute | solution.py:309
  38.9 6.5 %collective-permute-start.6 = (f32[320,128]{1,0:T(8,128)S(1)}, f32[320,128]{1,0:T(8,128)S(1)}, u32[]{:S(2)}, u32[]{:S(2)}) collective-permute-start(f32[320,128]{1,0:T(8,128)S(1)} %constant_dynamic-slice_fusion.1), channel_id=1, source_target_pairs={{0,16},{8,24},{16,0},{24,8},{1,17},{9,25},{17,1},{25,9},{2,18},{10... | collective-permute-start | bytes 491528 | tf_op jit(solution)/shard_map/ppermute | solution.py:309
  45.5 12.2 %collective-permute-start.7 = (f32[160,128]{1,0:T(8,128)S(1)}, f32[160,128]{1,0:T(8,128)S(1)}, u32[]{:S(2)}, u32[]{:S(2)}) collective-permute-start(f32[160,128]{1,0:T(8,128)S(1)} %constant_dynamic-slice_fusion.after_ref), channel_id=1, source_target_pairs={{0,1},{1,0},{2,3},{3,2},{4,5},{5,4},{6,7},{7,6},{8,9},{9,8},{10,11... | collective-permute-start | bytes 245768 | tf_op jit(solution)/shard_map/ppermute | solution.py:309
  58.4 4.5 %collective-permute-start.8 = (f32[160,128]{1,0:T(8,128)S(1)}, f32[160,128]{1,0:T(8,128)S(1)}, u32[]{:S(2)}, u32[]{:S(2)}) collective-permute-start(f32[160,128]{1,0:T(8,128)S(1)} %add_add_fusion), channel_id=1, source_target_pairs={{0,2},{1,3},{2,0},{3,1},{4,6},{5,7},{6,4},{7,5},{8,10},{9,11},{10,... | collective-permute-start | bytes 245768 | tf_op jit(solution)/shard_map/ppermute | solution.py:309
  63.0 5.7 %collective-permute-start.9 = (f32[160,128]{1,0:T(8,128)S(1)}, f32[160,128]{1,0:T(8,128)S(1)}, u32[]{:S(2)}, u32[]{:S(2)}) collective-permute-start(f32[160,128]{1,0:T(8,128)S(1)} %add.50), channel_id=1, source_target_pairs={{0,4},{1,5},{2,6},{3,7},{4,0},{5,1},{6,2},{7,3},{8,12},{9,13},{10,... | collective-permute-start | bytes 245768 | tf_op jit(solution)/shard_map/ppermute | solution.py:309
  68.7 4.5 %collective-permute-start.10 = (f32[160,128]{1,0:T(8,128)S(1)}, f32[160,128]{1,0:T(8,128)S(1)}, u32[]{:S(2)}, u32[]{:S(2)}) collective-permute-start(f32[160,128]{1,0:T(8,128)S(1)} %add.51), channel_id=1, source_target_pairs={{0,1},{1,0},{2,3},{3,2},{4,5},{5,4},{6,7},{7,6},{8,9},{9,8},{10,11... | collective-permute-start | bytes 245768 | tf_op jit(solution)/shard_map/ppermute | solution.py:309
  73.2 5.4 %collective-permute-start.11 = (f32[320,128]{1,0:T(8,128)S(1)}, f32[320,128]{1,0:T(8,128)S(1)}, u32[]{:S(2)}, u32[]{:S(2)}) collective-permute-start(f32[320,128]{1,0:T(8,128)S(1)} %maximum_select_fusion.2), channel_id=1, source_target_pairs={{0,16},{8,24},{16,0},{24,8},{1,17},{9,25},{17,1},{25,9},{2,18},{10... | collective-permute-start | bytes 491528 | tf_op jit(solution)/shard_map/ppermute | solution.py:309
  78.6 1.7 %collective-permute-start.12 = (f32[640,128]{1,0:T(8,128)S(1)}, f32[640,128]{1,0:T(8,128)S(1)}, u32[]{:S(2)}, u32[]{:S(2)}) collective-permute-start(f32[640,128]{1,0:T(8,128)S(1)} %maximum_select_fusion.1), channel_id=1, source_target_pairs={{0,8},{8,0},{16,24},{24,16},{1,9},{9,1},{17,25},{25,17},{2,10},{10... | collective-permute-start | bytes 983048 | tf_op jit(solution)/shard_map/ppermute | solution.py:309

commit v3 on v2

--- a/solution.py
+++ b/solution.py
@@ -38,10 +38,10 @@
 
 
 def front_kernel(
-    v_hbm, index_hbm, count_ref, lon_hbm, lat_hbm,
+    v_hbm, cells_ref, count_ref,
     fields_hbm, total, lon_out, lat_out, south_ref, second_ref, north_ref, before_ref, fold_ref,
     x0_ref, x1_ref, x2_ref, x3_ref,
-    index_ref, lon_ref, lat_ref, raw, moved, stage, lon_in, lat_in, sems, out_sems, small_sems,
+    raw, moved, stage, lon_in, lat_in, sems, out_sems,
 ):
     fields, days, width_x, width_y = v_hbm.shape
     step = raw.shape[2]
@@ -52,32 +52,23 @@
             v_hbm.at[:, pl.ds(i * step, step)], raw.at[i], sems.at[i]
         )
 
-    small = [
-        pltpu.make_async_copy(source, target, small_sems.at[i])
-        for i, (source, target) in enumerate(
-            ((index_hbm, index_ref), (lon_hbm, lon_ref), (lat_hbm, lat_ref))
-        )
-    ]
-    for copy in small:
-        copy.start()
     for i in range(days // step):
         fetch(i).start()
-    for copy in small:
-        copy.wait()
-
-    cells = index_ref.shape[1]
-    index = index_ref[...]
+
+    cells = width_x * width_y
+    index = cells_ref[2].astype(jnp.int32)
+    index = jnp.concatenate([index[x : x + 1, :] for x in range(width_x)], axis=1)
     wet = iota(index.shape, 1) < count_ref[0]
     row = jnp.where(wet, index // width_y, -1)
     col = index % width_y
     pick_x = jnp.where(iota((width_x, cells), 0) == row, 1.0, 0.0).astype(BF16)
     pick_y = jnp.where(iota((width_y, cells), 0) == col, 1.0, 0.0).astype(BF16)
     mask = lax.dot_general(pick_x, pick_y, NT, preferred_element_type=F32)
-    x = iota((width_x, width_y), 0)
-    y = iota((width_x, width_y), 1)
-    inner = (x > 0) & (x < width_x - 1) & (y > 0) & (y < width_y - 1)
-    lon = 0.5 * lon_ref[...] * mask
-    lat = 0.5 * lat_ref[...] * mask
+    at_x = iota((width_x, width_y), 0)
+    at_y = iota((width_x, width_y), 1)
+    inner = (at_x > 0) & (at_x < width_x - 1) & (at_y > 0) & (at_y < width_y - 1)
+    lon = 0.5 * cells_ref[0] * mask
+    lat = 0.5 * cells_ref[1] * mask
     lon_out[...] = lon
     lat_out[...] = lat
     lon_in[...] = jnp.where(inner, lon, 0.0)
@@ -166,6 +157,7 @@
     fields, days, width_x, width_y = velocity.shape
     assert width_x <= width_y // 2 - 2
     step = next(n for n in (32, 16) if days % n == 0)
+    places = wet_index.reshape(width_x, width_y).astype(F32)
     group = next(n for n in (8, 6, 4, 3, 2, 1) if width_x % n == 0)
     vmem = pl.BlockSpec(memory_space=pltpu.VMEM)
     hbm = pl.BlockSpec(memory_space=pl.ANY)
@@ -174,7 +166,7 @@
     column = jax.ShapeDtypeStruct((fields, days, width_y), BF16)
     return pl.pallas_call(
         front_kernel,
-        in_specs=[hbm, hbm, pl.BlockSpec(memory_space=pltpu.SMEM), hbm, hbm],
+        in_specs=[hbm, vmem, pl.BlockSpec(memory_space=pltpu.SMEM)],
         out_specs=[hbm] + [vmem] * 12,
         out_shape=[
             jax.ShapeDtypeStruct((2 * days, width_x * width_y), BF16),
@@ -182,9 +174,6 @@
             metric, metric, edge, edge, edge, edge, edge, column, column, column, column,
         ],
         scratch_shapes=[
-            pltpu.VMEM((1, width_x * width_y), jnp.int32),
-            pltpu.VMEM((width_x, width_y), F32),
-            pltpu.VMEM((width_x, width_y), F32),
             pltpu.VMEM((days // step, fields, step, width_x, width_y), BF16),
             pltpu.VMEM((fields, width_x, days, width_y), BF16),
             pltpu.VMEM((2, 2 * days, group * width_y), BF16),
@@ -192,11 +181,10 @@
             pltpu.VMEM((width_x, width_y), F32),
             pltpu.SemaphoreType.DMA((days // step,)),
             pltpu.SemaphoreType.DMA((2,)),
-            pltpu.SemaphoreType.DMA((3,)),
         ],
         compiler_params=pltpu.CompilerParams(vmem_limit_bytes=50 * MB),
         name="front",
-    )(velocity, wet_index.reshape(1, -1), wet_count, lon_metric, lat_metric)
+    )(velocity, jnp.stack([lon_metric, lat_metric, places]), wet_count)
 
 
 def rim_kernel(
@@ -445,51 +433,50 @@
     )(places, fields, rim, ends, after)
 
 
-def product_kernel(steps, high_ref, low_ref, *refs):
-    out_ref = refs[-1]
-    columns = high_ref.shape[0]
-    half = columns // 2
-
-    def dot(w, s):
-        return lax.dot_general(w, s, NT, preferred_element_type=F32)
-
-    for piece, rows_ref in enumerate(refs[:-1]):
-
-        @pl.when(pl.program_id(0) // steps == piece)
-        def _():
-            s = rows_ref[...]
-            low = s[:, :half]
-            top = dot(low_ref[:half, :half], low) + dot(high_ref[:half, :half], low)
-            out_ref[:half, :] = top.astype(BF16)
-            bottom = dot(low_ref[half:, :], s) + dot(high_ref[half:, :], s)
-            out_ref[half:, :] = bottom.astype(BF16)
-
-
-def product(high, low, pieces):
-    count, columns = pieces[0].shape
-    width = next(c for c in (768, 512, 256, 128) if count % c == 0)
-    steps = count // width
-    vmem = pl.BlockSpec(memory_space=pltpu.VMEM)
-    return pl.pallas_call(
-        functools.partial(product_kernel, steps),
-        grid=(len(pieces) * steps,),
-        in_specs=[vmem, vmem]
-        + [
-            pl.BlockSpec((width, columns), lambda i, k=k: (jnp.clip(i - k * steps, 0, steps - 1), 0))
-            for k in range(len(pieces))
-        ],
-        out_specs=pl.BlockSpec((columns, width), lambda i: (0, i)),
-        out_shape=jax.ShapeDtypeStruct((columns, len(pieces) * count), BF16),
-        compiler_params=pltpu.CompilerParams(vmem_limit_bytes=50 * MB),
-        name="product",
-    )(high, low, *pieces)
-
-
 def sublane(x, t):
     return jnp.broadcast_to(x[t : t + 1, :], x.shape)
 
 
-def inverse_factor(block):
+def lane_of(x, t):
+    at = jnp.full(x.shape, t, jnp.int32)
+    return jnp.take_along_axis(x, at, axis=1, mode="promise_in_bounds")
+
+
+def thirds(x):
+    high = x.astype(BF16).astype(F32)
+    rest = x - high
+    middle = rest.astype(BF16).astype(F32)
+    return high, middle, rest - middle
+
+
+def eliminate(work, head, row):
+    head = list(head)
+    done = jnp.zeros_like(work)
+    pivots = jnp.ones_like(work)
+    for t in range(0, 8, 2):
+        one, two = row == t, row == t + 1
+        both = one | two
+        a, b, c = sublane(head[t], t), sublane(head[t + 1], t), sublane(head[t + 1], t + 1)
+        determinant = a * c - b * b
+        inverse = 1.0 / determinant
+        first = jnp.where(one, c, jnp.where(two, -b, head[t + 1] * b - head[t] * c))
+        second = jnp.where(one, -b, jnp.where(two, a, head[t] * b - head[t + 1] * a))
+
+        def apply(x):
+            step = first * sublane(x, t) + second * sublane(x, t + 1)
+            return jnp.where(both, 0.0, x) + step * inverse
+
+        share = 1.0 / a
+        upper, lower = sublane(work, t), sublane(work, t + 1)
+        done = jnp.where(one, upper, jnp.where(two, lower - b * share * upper, done))
+        pivots = jnp.where(one, a, jnp.where(two, determinant * share, pivots))
+        for u in range(t + 2, 8):
+            head[u] = apply(head[u])
+        work = apply(work)
+    return work, done, pivots
+
+
+def inverse_factor(block, near=1):
     size = block.shape[0]
     count = size // 8
     lane = iota((8, size), 1)
@@ -498,101 +485,147 @@
     out = []
     for p in range(count):
         base = 8 * p
-        cols = {
-            q: [jnp.broadcast_to(tiles[q][:, base + t : base + t + 1], (8, size)) for t in range(8)]
-            for q in range(p, count)
-        }
+        close = range(p + 1, min(p + 1 + near, count))
+        cols = {q: [lane_of(tiles[q], base + t) for t in range(8)] for q in (p, *close)}
         own = (lane >= base) & (lane < base + 8)
-        work = jnp.where(own, jnp.where(lane == base + row, 1.0, 0.0), tiles[p])
-        head = cols[p]
-        done = jnp.zeros((8, size), F32)
-        pivots = jnp.ones((8, size), F32)
-        for t in range(8):
-            at = row == t
-            pivot = sublane(head[t], t)
-            inverse = 1.0 / pivot
-            coef = jnp.where(at, inverse, -head[t] * inverse)
-            line = sublane(work, t)
-            done = jnp.where(at, line, done)
-            pivots = jnp.where(at, pivot, pivots)
-            for u in range(t + 1, 8):
-                head[u] = jnp.where(at, 0.0, head[u]) + coef * sublane(head[u], t)
-            work = jnp.where(at, 0.0, work) + coef * line
+        unit = jnp.where(lane == base + row, 1.0, 0.0)
+        work, done, pivots = eliminate(jnp.where(own, unit, tiles[p]), cols[p], row)
         out.append(jnp.where(lane <= base + row, done * lax.rsqrt(pivots), 0.0))
         lines = [sublane(work, t) for t in range(8)]
-        for q in range(p + 1, count):
+        for q in close:
             terms = [cols[q][t] * lines[t] for t in range(8)]
             while len(terms) > 1:
                 terms = [terms[i] + terms[i + 1] for i in range(0, len(terms), 2)]
             tiles[q] = jnp.where(own, 0.0, tiles[q]) - terms[0]
+        if p + 1 + near < count:
+            ah, am, al = thirds(jnp.where(lane >= base + 8 * (1 + near), tiles[p], 0.0))
+            wh, wm, wl = thirds(work)
+            left = jnp.concatenate([ah, ah, am, ah, al, am], axis=0).astype(BF16)
+            right = jnp.concatenate([wh, wm, wh, wl, wh, wm], axis=0).astype(BF16)
+            change = lax.dot_general(left, right, TN, preferred_element_type=F32)
+            for q in range(p + 1 + near, count):
+                tiles[q] = jnp.where(own, 0.0, tiles[q]) - change[8 * q : 8 * q + 8, :]
     return jnp.concatenate(out, axis=0)
 
 
-def factor_kernel(scale, pieces_ref, r_ref, high_ref, low_ref, work):
+def factor_kernel(
+    scale, pieces_ref, rows_hbm, r_ref, basis_hbm, work, high_ref, low_ref, rows, stage, lead, sems
+):
     columns = r_ref.shape[0]
+    chunks, _, width = stage.shape[0], columns, stage.shape[2]
+    steps = rows.shape[0] // width
+    fetch = pltpu.make_async_copy(rows_hbm, rows, sems.at[chunks])
+    fetch.start()
+    opening = pltpu.make_async_copy(pieces_ref.at[0], lead, sems.at[chunks + 1])
+    opening.start()
+    opening.wait()
     size = pieces_ref.shape[1]
     count = columns // size
-    at = 0
-    for i in range(count):
-        for j in range(i, count):
-            work[i * size : (i + 1) * size, j * size : (j + 1) * size] = pieces_ref[at]
-            at += 1
-        if i:
-            work[i * size : (i + 1) * size, : i * size] = jnp.zeros((size, i * size), F32)
+    same = iota((size, size), 0) == iota((size, size), 1)
+    upper = iota((size, size), 0) <= iota((size, size), 1)
 
     def dot(a, b, dims):
         return lax.dot_general(
             a, b, dims, preferred_element_type=F32, precision=lax.Precision.HIGHEST
         )
 
-    lane = iota((size, columns), 1)
-
-    def step(k, _):
-        here = pl.multiple_of(k * size, size)
-        diagonal = work[pl.ds(here, size), pl.ds(here, size)]
+    def piece(at):
+        return pieces_ref[at] if at else lead[...]
+
+    order = [(i, j) for i in range(count) for j in range(i, count)]
+    across, along = [], []
+    for i in range(count):
+        diagonal = jnp.where(same, piece(order.index((i, i))), 0.0)
+        across.append(lax.rsqrt(jnp.sum(diagonal, axis=0, keepdims=True)))
+        along.append(lax.rsqrt(jnp.sum(diagonal, axis=1, keepdims=True)))
+    for at, (i, j) in enumerate(order):
+        work[i, j] = piece(at) * along[i] * across[j]
+
+    def place(i, j):
+        return slice(i * size, (i + 1) * size), slice(j * size, (j + 1) * size)
+
+    for k in range(count):
+        diagonal = work[k, k]
         inverse = inverse_factor(diagonal)
-        corner = dot(inverse, diagonal, NN)
-        work[pl.ds(here, size), pl.ds(here, size)] = jnp.where(
-            iota((size, size), 0) == iota((size, size), 1), 1.0, 0.0
-        )
-        fresh = dot(inverse, work[pl.ds(here, size), :], NN)
-        work[pl.ds(here, size), :] = fresh
-        for i in range(1, count):
-
-            @pl.when(i > k)
-            def _():
-                mine = slice(i * size, (i + 1) * size)
-                work[mine, pl.ds(here, size)] = jnp.zeros((size, size), F32)
-                work[mine, :] -= dot(work[pl.ds(here, size), mine], work[pl.ds(here, size), :], TN)
-
-        known = jnp.where(lane < here + size, fresh * scale, 0.0)
-        high = known.astype(BF16)
-        high_ref[pl.ds(here, size), :] = high
-        low_ref[pl.ds(here, size), :] = (known - high.astype(F32)).astype(BF16)
-        r_ref[pl.ds(here, size), :] = jnp.where(lane >= here + size, fresh * (1.0 / scale), 0.0)
-        upper = iota((size, size), 0) <= iota((size, size), 1)
-        r_ref[pl.ds(here, size), pl.ds(here, size)] = jnp.where(upper, corner * (1.0 / scale), 0.0)
+        for j in (*range(k + 1, count), *range(k)):
+            work[k, j] = dot(inverse, work[k, j], NN)
+        work[k, k] = inverse
+        for i in range(k + 1, count):
+            left = work[k, i]
+            for j in (*range(i, count), *range(k + 1)):
+                change = dot(left, work[k, j], TN)
+                work[i, j] = -change if j == k else work[i, j] - change
+        corner = jnp.where(upper, dot(inverse, diagonal, NN), 0.0)
+        for j in range(count):
+            known = work[k, j] * (across[j] * scale) if j <= k else jnp.zeros((size, size), F32)
+            high = known.astype(BF16)
+            high_ref[place(k, j)] = high
+            low_ref[place(k, j)] = (known - high.astype(F32)).astype(BF16)
+            grow = 1.0 / (across[j] * scale)
+            r_ref[place(k, j)] = (
+                corner * grow if j == k else work[k, j] * grow if j > k else jnp.zeros((size, size), F32)
+            )
+
+    fetch.wait()
+    half = columns // 2
+
+    def product(w, x):
+        return lax.dot_general(w, x, NT, preferred_element_type=F32)
+
+    def send(i):
+        slot = lax.rem(i, chunks)
+        place = pl.ds(pl.multiple_of(i * width, width), width)
+        return pltpu.make_async_copy(stage.at[slot], basis_hbm.at[:, place], sems.at[slot])
+
+    def body(i, _):
+        slot = lax.rem(i, chunks)
+
+        @pl.when(i >= chunks)
+        def _():
+            send(i - chunks).wait()
+
+        block = rows[pl.ds(pl.multiple_of(i * width, width), width), :]
+        first = block[:, :half]
+        top = product(low_ref[:half, :half], first) + product(high_ref[:half, :half], first)
+        stage[slot, :half, :] = top.astype(BF16)
+        bottom = product(low_ref[half:, :], block) + product(high_ref[half:, :], block)
+        stage[slot, half:, :] = bottom.astype(BF16)
+        send(i).start()
         return 0
 
-    lax.fori_loop(0, count, step, 0)
-
-
-def factor(pieces, columns, scale):
+    lax.fori_loop(0, steps, body, 0)
+    for i in range(max(steps - chunks, 0), steps):
+        send(i).wait()
+
+
+def factor(pieces, rows, columns, scale):
     vmem = pl.BlockSpec(memory_space=pltpu.VMEM)
+    hbm = pl.BlockSpec(memory_space=pl.ANY)
     square = (columns, columns)
+    size = pieces.shape[1]
+    cells = rows.shape[0]
+    width = next(n for n in (768, 512, 256, 128) if cells % n == 0)
+    chunks = min(3, cells // width)
     return pl.pallas_call(
         functools.partial(factor_kernel, scale),
-        in_specs=[vmem],
-        out_specs=[vmem] * 3,
+        in_specs=[vmem, hbm],
+        out_specs=[vmem, hbm],
         out_shape=[
             jax.ShapeDtypeStruct(square, F32),
-            jax.ShapeDtypeStruct(square, BF16),
-            jax.ShapeDtypeStruct(square, BF16),
+            jax.ShapeDtypeStruct((columns, cells), BF16),
         ],
-        scratch_shapes=[pltpu.VMEM(square, F32)],
-        compiler_params=pltpu.CompilerParams(vmem_limit_bytes=ROOM),
+        scratch_shapes=[
+            pltpu.VMEM((columns // size, columns // size, size, size), F32),
+            pltpu.VMEM(square, BF16),
+            pltpu.VMEM(square, BF16),
+            pltpu.VMEM((cells, columns), BF16),
+            pltpu.VMEM((chunks, columns, width), BF16),
+            pltpu.VMEM((size, size), F32),
+            pltpu.SemaphoreType.DMA((chunks + 2,)),
+        ],
+        compiler_params=pltpu.CompilerParams(vmem_limit_bytes=50 * MB),
         name="factor",
-    )(pieces)
+    )(pieces, rows)
 
 
 def shards(velocity, lon_metric, lat_metric, wet_index, wet_count):
@@ -626,8 +659,8 @@
     beside = {2 + piece: functools.partial(picking, piece) for piece in range(pieces)}
     total = all_sum(gram, beside)
     scale = math.sqrt(cells * lats * lons)
-    triangle, high, low = factor(total, columns, scale)
-    return product(high, low, [held[piece] for piece in range(pieces)]), triangle
+    triangle, basis = factor(total, held[0], columns, scale)
+    return basis, triangle
 
 
 def solution(mesh):

time: 116 us -> 102 us (0.88)
  Pallas kernels: 61.8 us -> 48.4 us
  local copies, waits for them, and re-layouts: 2.79 us -> 0.58 us
  other arithmetic: 0.82 us -> 2.4 us
    pallas_call x3 -> x2, Pallas kernels: 49.3 us -> 35.7 us  [the longest x1 21.9 us: factor(): pl.pallas_call(functools.partial(factor_kernel, scale), in_specs=[vmem, h...]
    unnamed x8 -> x0, local copies, waits for them, and re-layouts: 2.21 us -> none
  transfers between devices with their start and end apart: 13 -> 13, of which waited for: 9 -> 9; matrix products, arithmetic and copies ran while one was open for 0% -> 1% of each run, Pallas kernels for 10% -> 12%
where the time goes in v3:
time: 102 us
  Pallas kernels  48.4 us (47%)
  waiting for transfers between devices  30.3 us (30%)
  starting transfers between devices  18.5 us (18%)
  other arithmetic  2.4 us (2%)
  between operations  1.6 us (2%)
    ppermute x8, waiting for transfers between devices, swap(): lax.ppermute(block, axis, [(i, i ^ 1 << bit) for i in range(lax.axis_size...  26.1 us
    pallas_call x1, Pallas kernels, factor(): pl.pallas_call(functools.partial(factor_kernel, scale), in_specs=[vmem, h...  21.9 us
    pallas_call x1, Pallas kernels, front(): pl.pallas_call(front_kernel, in_specs=[hbm, vmem, pl.BlockSpec(memory_spa...  13.9 us
    pallas_call x1, Pallas kernels, pick(): pl.pallas_call(functools.partial(pick_kernel, piece), in_specs=[hbm, hbm,...  11.8 us
    ppermute x8, starting transfers between devices, swap(): lax.ppermute(block, axis, [(i, i ^ 1 << bit) for i in range(lax.axis_size...  9.01 us
    ppermute x1, starting transfers between devices, shards(): east = lax.ppermute(outer[0], 'lon', [(t, s) for s, t in east_route])  6.06 us
    ppermute x1, waiting for transfers between devices, shards(): above = lax.ppermute(south, 'lat', [(t, s) for s, t in up])  3.38 us
  transfers between devices with their start and end apart: 13, of which 9 were waited for; matrix products, arithmetic and copies ran while one was open for 1% of the time, Pallas kernels for 12%

profile of v3, /device:TPU:0, one launch (start us, length us, event | category | flops | bytes accessed | tf_op | source)
XLA Modules:
  0.0 101.7 jit_solution(1186737853752405912)
XLA Ops:
  1.3 0.8 broadcast_multiply_fusion
  2.1 0.8 pad_maximum_fusion.cells_ref
  2.9 13.9 %front.1 = (bf16[512,6144]{1,0:T(8,128)(2,1)}, f32[512,512]{1,0:T(8,128)S(1)}, f32[48,128]{1,0:T(8,128)S(1)}, f32[48,128]{1,0:T(8,128)S(1)}, bf16[256,128]{1,0:T...) custom-call(bf16[2,256,48,128]{3,2,1,0:T(8,128)(2,1)} %v_hbm.1, ...), custom_call_target="tpu_custom_call" | custom-call | tf_op jit(solution)/shard_map/front/pallas_call | solution.py:167
  16.8 6.1 %collective-permute-start.1 = (bf16[2,256,128]{2,1,0:T(8,128)(2,1)S(1)}, bf16[2,256,128]{2,1,0:T(8,128)(2,1)S(1)}, u32[]{:S(2)}, u32[]{:S(2)}) collective-permute-start(bf16[2,256,128]{2,1,0:T(8,128)(2,1)S(1)} %get-tuple-element.22.x0_ref), channel_id=1, source_target_pairs={{1,0},{2,1},{3,2},{4,3},{5,4},{6,5},{7,6},{0,7},{9,8},{10,9},{11,1... | collective-permute-start | bytes 393224 | tf_op jit(solution)/shard_map/ppermute | solution.py:641
  22.8 0.7 collective-permute-start.4
  23.5 1.5 %collective-permute-start.2 = (bf16[256,128]{1,0:T(8,128)(2,1)S(1)}, bf16[256,128]{1,0:T(8,128)(2,1)S(1)}, u32[]{:S(2)}, u32[]{:S(2)}) collective-permute-start(bf16[256,128]{1,0:T(8,128)(2,1)S(1)} %get-tuple-element.26.north_ref), channel_id=1, source_target_pairs={{0,8},{8,16},{16,24},{1,9},{9,17},{17,25},{2,10},{10,18},{18,26},{... | collective-permute-start | bytes 196616 | tf_op jit(solution)/shard_map/ppermute | solution.py:643
  24.9 1.3 %collective-permute-start.3 = (bf16[256,128]{1,0:T(8,128)(2,1)S(1)}, bf16[256,128]{1,0:T(8,128)(2,1)S(1)}, u32[]{:S(2)}, u32[]{:S(2)}) collective-permute-start(bf16[256,128]{1,0:T(8,128)(2,1)S(1)} %get-tuple-element.27.south_ref), channel_id=1, source_target_pairs={{8,0},{16,8},{24,16},{9,1},{17,9},{25,17},{10,2},{18,10},{26,18},{... | collective-permute-start | bytes 196616 | tf_op jit(solution)/shard_map/ppermute | solution.py:644
  26.3 3.4 %collective-permute-done.3.above_ref = bf16[256,128]{1,0:T(8,128)(2,1)S(1)} collective-permute-done((bf16[256,128]{1,0:T(8,128)(2,1)S(1)}, bf16[256,128]{1,0:T(8,128)(2,1)S(1)}, u32[]{:S(2)}, u32[]{:S(2)}) %collective-permute-start.3) | collective-permute-done | bytes 65568 | tf_op jit(solution)/shard_map/ppermute | solution.py:644
  29.7 0.8 collective-permute-done.west_ref
  30.5 0.9 rim.1
  31.4 5.4 %collective-permute-start.5 = (f32[640,128]{1,0:T(8,128)S(1)}, f32[640,128]{1,0:T(8,128)S(1)}, u32[]{:S(2)}, u32[]{:S(2)}) collective-permute-start(f32[640,128]{1,0:T(8,128)S(1)} %constant_dynamic-slice_fusion.2), channel_id=1, source_target_pairs={{0,8},{8,0},{16,24},{24,16},{1,9},{9,1},{17,25},{25,17},{2,10},{10... | collective-permute-start | bytes 983048 | tf_op jit(solution)/shard_map/ppermute | solution.py:297
  36.8 1.3 %collective-permute-done.5 = f32[640,128]{1,0:T(8,128)S(1)} collective-permute-done((f32[640,128]{1,0:T(8,128)S(1)}, f32[640,128]{1,0:T(8,128)S(1)}, u32[]{:S(2)}, u32[]{:S(2)}) %collective-permute-start.5) | collective-permute-done | bytes 327712 | tf_op jit(solution)/shard_map/ppermute | solution.py:297
  38.4 6.3 %collective-permute-done.6 = f32[320,128]{1,0:T(8,128)S(1)} collective-permute-done((f32[320,128]{1,0:T(8,128)S(1)}, f32[320,128]{1,0:T(8,128)S(1)}, u32[]{:S(2)}, u32[]{:S(2)}) %collective-permute-start.6) | collective-permute-done | bytes 163872 | tf_op jit(solution)/shard_map/ppermute | solution.py:297
  44.8 11.8 %pick.1 = (bf16[6144,512]{1,0:T(8,128)(2,1)}, f32[8,128]{1,0:T(8,128)S(1)}) custom-call(s32[6144]{0:T(1024)S(1)} %get-tuple-element.42.index_hbm, bf16[512,6144]{1,0:T(8,128)(2,1)} %get-tuple-element.35.fields_hbm, bf16[512,128]{1,0:T(8,128)(2,1)S(1)} %get-tuple-element.36.rim_ref, bf16[2,512,128]{2,1,0:T(8,128)(2,1)S(1)} %get-tuple-element.37.ends_ref, ...), custom_call_target="tpu_custom_call" | custom-call | tf_op jit(solution)/shard_map/pick/pallas_call | solution.py:417
  56.6 0.5 slice.3
  57.1 0.7 add_add_fusion
  57.9 4.4 %collective-permute-done.8 = f32[160,128]{1,0:T(8,128)S(1)} collective-permute-done((f32[160,128]{1,0:T(8,128)S(1)}, f32[160,128]{1,0:T(8,128)S(1)}, u32[]{:S(2)}, u32[]{:S(2)}) %collective-permute-start.8) | collective-permute-done | bytes 81952 | tf_op jit(solution)/shard_map/ppermute | solution.py:297
  62.3 0.7 collective-permute-start.9
  63.0 5.1 %collective-permute-done.9 = f32[160,128]{1,0:T(8,128)S(1)} collective-permute-done((f32[160,128]{1,0:T(8,128)S(1)}, f32[160,128]{1,0:T(8,128)S(1)}, u32[]{:S(2)}, u32[]{:S(2)}) %collective-permute-start.9) | collective-permute-done | bytes 81952 | tf_op jit(solution)/shard_map/ppermute | solution.py:297
  68.1 2.1 %collective-permute-start.10 = (f32[160,128]{1,0:T(8,128)S(1)}, f32[160,128]{1,0:T(8,128)S(1)}, u32[]{:S(2)}, u32[]{:S(2)}) collective-permute-start(f32[160,128]{1,0:T(8,128)S(1)} %add.51), channel_id=1, source_target_pairs={{0,1},{1,0},{2,3},{3,2},{4,5},{5,4},{6,7},{7,6},{8,9},{9,8},{10,11... | collective-permute-start | bytes 245768 | tf_op jit(solution)/shard_map/ppermute | solution.py:297
  70.1 2.4 %collective-permute-done.10 = f32[160,128]{1,0:T(8,128)S(1)} collective-permute-done((f32[160,128]{1,0:T(8,128)S(1)}, f32[160,128]{1,0:T(8,128)S(1)}, u32[]{:S(2)}, u32[]{:S(2)}) %collective-permute-start.10) | collective-permute-done | bytes 81952 | tf_op jit(solution)/shard_map/ppermute | solution.py:297
  72.9 5.0 %collective-permute-done.11 = f32[320,128]{1,0:T(8,128)S(1)} collective-permute-done((f32[320,128]{1,0:T(8,128)S(1)}, f32[320,128]{1,0:T(8,128)S(1)}, u32[]{:S(2)}, u32[]{:S(2)}) %collective-permute-start.11) | collective-permute-done | bytes 163872 | tf_op jit(solution)/shard_map/ppermute | solution.py:297
  78.1 1.6 %collective-permute-done.12 = f32[640,128]{1,0:T(8,128)S(1)} collective-permute-done((f32[640,128]{1,0:T(8,128)S(1)}, f32[640,128]{1,0:T(8,128)S(1)}, u32[]{:S(2)}, u32[]{:S(2)}) %collective-permute-start.12) | collective-permute-done | bytes 327712 | tf_op jit(solution)/shard_map/ppermute | solution.py:297
  79.7 21.9 %factor.1 = (f32[512,512]{1,0:T(8,128)}, bf16[512,6144]{1,0:T(8,128)(2,1)}) custom-call(f32[10,128,128]{2,1,0:T(8,128)S(1)} %bitcast.7, bf16[6144,512]{1,0:T(8,128)(2,1)} %get-tuple-element.39.rows_hbm), custom_call_target="tpu_custom_call" | custom-call | tf_op jit(solution)/shard_map/factor/pallas_call | solution.py:609
  (20 shorter events, 1.1 us)
Async XLA Ops:
  16.8 12.9 %collective-permute-start.1 = (bf16[2,256,128]{2,1,0:T(8,128)(2,1)S(1)}, bf16[2,256,128]{2,1,0:T(8,128)(2,1)S(1)}, u32[]{:S(2)}, u32[]{:S(2)}) collective-permute-start(bf16[2,256,128]{2,1,0:T(8,128)(2,1)S(1)} %get-tuple-element.22.x0_ref), channel_id=1, source_target_pairs={{1,0},{2,1},{3,2},{4,3},{5,4},{6,5},{7,6},{0,7},{9,8},{10,9},{11,1... | collective-permute-start | bytes 393224 | tf_op jit(solution)/shard_map/ppermute | solution.py:641
  22.8 7.7 %collective-permute-start = (bf16[2,256,128]{2,1,0:T(8,128)(2,1)S(1)}, bf16[2,256,128]{2,1,0:T(8,128)(2,1)S(1)}, u32[]{:S(2)}, u32[]{:S(2)}) collective-permute-start(bf16[2,256,128]{2,1,0:T(8,128)(2,1)S(1)} %get-tuple-element.25.x3_ref), channel_id=1, source_target_pairs={{0,1},{1,2},{2,3},{3,4},{4,5},{5,6},{6,7},{7,0},{8,9},{9,10},{10,1... | collective-permute-start | bytes 393224 | tf_op jit(solution)/shard_map/ppermute | solution.py:640
  22.8 3.4 %collective-permute-start.4 = (bf16[256,128]{1,0:T(8,128)(2,1)S(1)}, bf16[256,128]{1,0:T(8,128)(2,1)S(1)}, u32[]{:S(2)}, u32[]{:S(2)}) collective-permute-start(bf16[256,128]{1,0:T(8,128)(2,1)S(1)} %get-tuple-element.28), channel_id=1, source_target_pairs={{24,31},{25,30},{26,29},{27,28},{28,27},{29,26},{30,25},{31,24}} | collective-permute-start | bytes 196616 | tf_op jit(solution)/shard_map/ppermute | solution.py:646
  23.5 2.8 %collective-permute-start.2 = (bf16[256,128]{1,0:T(8,128)(2,1)S(1)}, bf16[256,128]{1,0:T(8,128)(2,1)S(1)}, u32[]{:S(2)}, u32[]{:S(2)}) collective-permute-start(bf16[256,128]{1,0:T(8,128)(2,1)S(1)} %get-tuple-element.26.north_ref), channel_id=1, source_target_pairs={{0,8},{8,16},{16,24},{1,9},{9,17},{17,25},{2,10},{10,18},{18,26},{... | collective-permute-start | bytes 196616 | tf_op jit(solution)/shard_map/ppermute | solution.py:643
  24.9 4.7 %collective-permute-start.3 = (bf16[256,128]{1,0:T(8,128)(2,1)S(1)}, bf16[256,128]{1,0:T(8,128)(2,1)S(1)}, u32[]{:S(2)}, u32[]{:S(2)}) collective-permute-start(bf16[256,128]{1,0:T(8,128)(2,1)S(1)} %get-tuple-element.27.south_ref), channel_id=1, source_target_pairs={{8,0},{16,8},{24,16},{9,1},{17,9},{25,17},{10,2},{18,10},{26,18},{... | collective-permute-start | bytes 196616 | tf_op jit(solution)/shard_map/ppermute | solution.py:644
  31.4 6.7 %collective-permute-start.5 = (f32[640,128]{1,0:T(8,128)S(1)}, f32[640,128]{1,0:T(8,128)S(1)}, u32[]{:S(2)}, u32[]{:S(2)}) collective-permute-start(f32[640,128]{1,0:T(8,128)S(1)} %constant_dynamic-slice_fusion.2), channel_id=1, source_target_pairs={{0,8},{8,0},{16,24},{24,16},{1,9},{9,1},{17,25},{25,17},{2,10},{10... | collective-permute-start | bytes 983048 | tf_op jit(solution)/shard_map/ppermute | solution.py:297
  38.2 6.5 %collective-permute-start.6 = (f32[320,128]{1,0:T(8,128)S(1)}, f32[320,128]{1,0:T(8,128)S(1)}, u32[]{:S(2)}, u32[]{:S(2)}) collective-permute-start(f32[320,128]{1,0:T(8,128)S(1)} %constant_dynamic-slice_fusion.1), channel_id=1, source_target_pairs={{0,16},{8,24},{16,0},{24,8},{1,17},{9,25},{17,1},{25,9},{2,18},{10... | collective-permute-start | bytes 491528 | tf_op jit(solution)/shard_map/ppermute | solution.py:297
  44.7 12.4 %collective-permute-start.7 = (f32[160,128]{1,0:T(8,128)S(1)}, f32[160,128]{1,0:T(8,128)S(1)}, u32[]{:S(2)}, u32[]{:S(2)}) collective-permute-start(f32[160,128]{1,0:T(8,128)S(1)} %constant_dynamic-slice_fusion.after_ref), channel_id=1, source_target_pairs={{0,1},{1,0},{2,3},{3,2},{4,5},{5,4},{6,7},{7,6},{8,9},{9,8},{10,11... | collective-permute-start | bytes 245768 | tf_op jit(solution)/shard_map/ppermute | solution.py:297
  57.8 4.5 %collective-permute-start.8 = (f32[160,128]{1,0:T(8,128)S(1)}, f32[160,128]{1,0:T(8,128)S(1)}, u32[]{:S(2)}, u32[]{:S(2)}) collective-permute-start(f32[160,128]{1,0:T(8,128)S(1)} %add_add_fusion), channel_id=1, source_target_pairs={{0,2},{1,3},{2,0},{3,1},{4,6},{5,7},{6,4},{7,5},{8,10},{9,11},{10,... | collective-permute-start | bytes 245768 | tf_op jit(solution)/shard_map/ppermute | solution.py:297
  62.3 5.7 %collective-permute-start.9 = (f32[160,128]{1,0:T(8,128)S(1)}, f32[160,128]{1,0:T(8,128)S(1)}, u32[]{:S(2)}, u32[]{:S(2)}) collective-permute-start(f32[160,128]{1,0:T(8,128)S(1)} %add.50), channel_id=1, source_target_pairs={{0,4},{1,5},{2,6},{3,7},{4,0},{5,1},{6,2},{7,3},{8,12},{9,13},{10,... | collective-permute-start | bytes 245768 | tf_op jit(solution)/shard_map/ppermute | solution.py:297
  68.1 4.5 %collective-permute-start.10 = (f32[160,128]{1,0:T(8,128)S(1)}, f32[160,128]{1,0:T(8,128)S(1)}, u32[]{:S(2)}, u32[]{:S(2)}) collective-permute-start(f32[160,128]{1,0:T(8,128)S(1)} %add.51), channel_id=1, source_target_pairs={{0,1},{1,0},{2,3},{3,2},{4,5},{5,4},{6,7},{7,6},{8,9},{9,8},{10,11... | collective-permute-start | bytes 245768 | tf_op jit(solution)/shard_map/ppermute | solution.py:297
  72.6 5.4 %collective-permute-start.11 = (f32[320,128]{1,0:T(8,128)S(1)}, f32[320,128]{1,0:T(8,128)S(1)}, u32[]{:S(2)}, u32[]{:S(2)}) collective-permute-start(f32[320,128]{1,0:T(8,128)S(1)} %maximum_select_fusion.2), channel_id=1, source_target_pairs={{0,16},{8,24},{16,0},{24,8},{1,17},{9,25},{17,1},{25,9},{2,18},{10... | collective-permute-start | bytes 491528 | tf_op jit(solution)/shard_map/ppermute | solution.py:297
  78.0 1.7 %collective-permute-start.12 = (f32[640,128]{1,0:T(8,128)S(1)}, f32[640,128]{1,0:T(8,128)S(1)}, u32[]{:S(2)}, u32[]{:S(2)}) collective-permute-start(f32[640,128]{1,0:T(8,128)S(1)} %maximum_select_fusion.1), channel_id=1, source_target_pairs={{0,8},{8,0},{16,24},{24,16},{1,9},{9,1},{17,25},{25,17},{2,10},{10... | collective-permute-start | bytes 983048 | tf_op jit(solution)/shard_map/ppermute | solution.py:297

commit v4 on v3

--- a/solution.py
+++ b/solution.py
@@ -39,8 +39,8 @@
 
 def front_kernel(
     v_hbm, cells_ref, count_ref,
-    fields_hbm, total, lon_out, lat_out, south_ref, second_ref, north_ref, before_ref, fold_ref,
-    x0_ref, x1_ref, x2_ref, x3_ref,
+    fields_hbm, total, lon_out, lat_out, south_ref, second_ref, north_ref, before_ref, near_ref, far_ref,
+    x0_ref, x1_ref, x2_ref, x3_ref, flag_ref,
     raw, moved, stage, lon_in, lat_in, sems, out_sems,
 ):
     fields, days, width_x, width_y = v_hbm.shape
@@ -103,7 +103,12 @@
     mirror = (k // half == n // half) & (k + n == 2 * half * (n // half) + width_x - 1)
     mirror = jnp.where(mirror, -1.0, 0.0).astype(BF16)
     fold = lax.dot_general(north_ref[...], mirror, NN, preferred_element_type=F32)
-    fold_ref[...] = fold.astype(BF16)
+    flag = cells_ref[3, :1, :]
+    flag_ref[...] = cells_ref[3, :8, :]
+    odd, top = flag % 2 == 1, flag >= 2
+    south, north = south_ref[...].astype(F32), north_ref[...].astype(F32)
+    near_ref[...] = jnp.where(odd, south, north).astype(BF16)
+    far_ref[...] = jnp.where(top, fold, jnp.where(odd, north, south)).astype(BF16)
     x0_ref[...] = moved[:, 0]
     x1_ref[...] = moved[:, 1]
     x2_ref[...] = moved[:, width_x - 2]
@@ -153,7 +158,7 @@
         send(i).wait()
 
 
-def front(velocity, wet_index, wet_count, lon_metric, lat_metric):
+def front(velocity, wet_index, wet_count, lon_metric, lat_metric, flag):
     fields, days, width_x, width_y = velocity.shape
     assert width_x <= width_y // 2 - 2
     step = next(n for n in (32, 16) if days % n == 0)
@@ -167,11 +172,11 @@
     return pl.pallas_call(
         front_kernel,
         in_specs=[hbm, vmem, pl.BlockSpec(memory_space=pltpu.SMEM)],
-        out_specs=[hbm] + [vmem] * 12,
+        out_specs=[hbm] + [vmem] * 14,
         out_shape=[
             jax.ShapeDtypeStruct((2 * days, width_x * width_y), BF16),
             jax.ShapeDtypeStruct((2 * days, 2 * days), F32),
-            metric, metric, edge, edge, edge, edge, edge, column, column, column, column,
+            metric, metric, *[edge] * 6, *[column] * 4, jax.ShapeDtypeStruct((8, width_y), F32),
         ],
         scratch_shapes=[
             pltpu.VMEM((days // step, fields, step, width_x, width_y), BF16),
@@ -184,19 +189,20 @@
         ],
         compiler_params=pltpu.CompilerParams(vmem_limit_bytes=50 * MB),
         name="front",
-    )(velocity, jnp.stack([lon_metric, lat_metric, places]), wet_count)
+    )(velocity, jnp.stack([lon_metric, lat_metric, places, jnp.full_like(places, flag)]), wet_count)
 
 
 def rim_kernel(
-    x0_ref, x1_ref, x2_ref, x3_ref, west_ref, east_ref, below_ref, above_ref, mirrored_ref,
+    x0_ref, x1_ref, x2_ref, x3_ref, west_ref, east_ref, near_ref, far_ref, flag_ref,
     south_ref, second_ref, north_ref, before_ref, lon_ref, lat_ref, total_ref,
     gram_ref, rows_ref, ends_ref,
 ):
     _, days, width_y = x0_ref.shape
     width_x = lon_ref.shape[0]
     half = width_y // 2
-    below = below_ref[...].astype(F32)
-    above = above_ref[...].astype(F32) + mirrored_ref[...].astype(F32)
+    odd = flag_ref[:1, :] % 2 == 1
+    near, far = near_ref[...].astype(F32), far_ref[...].astype(F32)
+    below, above = jnp.where(odd, near, far), jnp.where(odd, far, near)
     lane = iota((1, width_y), 1)
 
     diff = lat_difference(width_y)
@@ -324,7 +330,7 @@
 
 
 def pick_kernel(
-    piece, index_hbm, fields_hbm, rim_ref, ends_ref, after_ref, out_hbm, token_ref,
+    piece, share, index_hbm, fields_hbm, rim_ref, ends_ref, after_ref, out_hbm, token_ref,
     index_ref, stage, rows, picked, turned_out, sems, out_sems,
 ):
     token_ref[...] = jnp.zeros_like(token_ref)
@@ -370,7 +376,6 @@
                     rows[end : end + 1, :] = rim[wide // 2 + x : wide // 2 + x + 1, own]
 
     places.wait()
-    share = picked.shape[1] // parts
     block = turned_out.shape[1]
 
     def row(at):
@@ -415,15 +420,15 @@
     vmem = pl.BlockSpec(memory_space=pltpu.VMEM)
     hbm = pl.BlockSpec(memory_space=pl.ANY)
     return pl.pallas_call(
-        functools.partial(pick_kernel, piece),
+        functools.partial(pick_kernel, piece, share),
         in_specs=[hbm, hbm, vmem, vmem, hbm],
         out_specs=[hbm, vmem],
         out_shape=[jax.ShapeDtypeStruct((cells // pieces, columns), BF16), TOKEN],
         scratch_shapes=[
             pltpu.SMEM((cells,), jnp.int32),
             pltpu.VMEM((cells // chunk, columns, chunk), BF16),
-            pltpu.VMEM((cells * parts, 128), F32),
-            pltpu.VMEM((2, share * parts, 128), F32),
+            pltpu.VMEM((cells * parts + 8, 128), F32),
+            pltpu.VMEM((2, share * parts + 8, 128), F32),
             pltpu.VMEM((2, block, columns), BF16),
             pltpu.SemaphoreType.DMA((cells // chunk,)),
             pltpu.SemaphoreType.DMA((3,)),
@@ -633,22 +638,29 @@
     cells = velocity.shape[2] * velocity.shape[3]
     columns = 2 * days
     lats, lons = lax.axis_size("lat"), lax.axis_size("lon")
-    fields, total, lon, lat, south, second, north, before, fold, *outer = front(
-        velocity, wet_index, wet_count, lon_metric, lat_metric
+    row = lax.axis_index("lat")
+    flag = (row % 2 + 2 * (row == lats - 1)).astype(F32)
+    fields, total, lon, lat, south, second, north, before, near, far, *outer, flag = front(
+        velocity, wet_index, wet_count, lon_metric, lat_metric, flag
     )
     east_route = [(i, (i + 1) % lons) for i in range(lons)]
     west = lax.ppermute(outer[3], "lon", east_route)
     east = lax.ppermute(outer[0], "lon", [(t, s) for s, t in east_route])
-    up = [(i, i + 1) for i in range(lats - 1)]
-    below = lax.ppermute(north, "lat", up)
-    above = lax.ppermute(south, "lat", [(t, s) for s, t in up])
-    top = (lats - 1) * lons
-    mirrored = lax.ppermute(fold, ("lat", "lon"), [(top + i, top + lons - 1 - i) for i in range(lons)])
-    sides = (west, east, below, above, mirrored)
+    assert lats % 2 == 0
+    near = lax.ppermute(near, "lat", [(i, i ^ 1) for i in range(lats)])
+    route = []
+    for x in range(lons):
+        for y in range(1, lats - 1):
+            other = y + 1 if y % 2 else y - 1
+            route.append((y * lons + x, other * lons + x))
+        route.append(((lats - 1) * lons + x, lats * lons - 1 - x))
+    far = lax.ppermute(far, ("lat", "lon"), route)
+    sides = (west, east, near, far, flag)
+    cells_in_order, lon = lax.optimization_barrier((wet_index, lon))
+    places = cells_in_order * (columns // 128)
     edges = (south, second, north, before)
     gram, rows, ends = rim(outer, sides, edges, lon, lat, total, min(128, columns))
 
-    places = wet_index * (columns // 128)
     pieces = 1
     held = {}
 

time: 102 us -> 98 us (0.961)
  waiting for transfers between devices: 30.3 us -> 26.9 us
    ppermute x8, waiting for transfers between devices: 26.1 us -> 19.9 us  [swap(): lax.ppermute(block, axis, [(i, i ^ 1 << bit) for i in range(lax.axis_size...]
    ppermute x1, waiting for transfers between devices: 0.82 us -> 4.92 us  [shards(): west = lax.ppermute(outer[3], 'lon', east_route)]
    ppermute x3 -> x2, waiting for transfers between devices: 3.38 us -> 0.59 us  [the longest x1 0.58 us: shards(): near = lax.ppermute(near, 'lat', [(i, i ^ 1) for i in range(lats)])]
    ppermute x3 -> x2, starting transfers between devices: 3.4 us -> 0.66 us  [the longest x1 0.65 us: shards(): far = lax.ppermute(far, ('lat', 'lon'), route)]
    ppermute x8, starting transfers between devices: 9.01 us -> 11 us  [swap(): lax.ppermute(block, axis, [(i, i ^ 1 << bit) for i in range(lax.axis_size...]
    ppermute x1, waiting for transfers between devices: 0.01 us -> 1.49 us  [shards(): east = lax.ppermute(outer[0], 'lon', [(t, s) for s, t in east_route])]
  transfers between devices with their start and end apart: 13 -> 12, of which waited for: 9 -> 10; matrix products, arithmetic and copies ran while one was open for 1% -> 1% of each run, Pallas kernels for 12% -> 12%
where the time goes in v4:
time: 98 us; the launch traced here: 97.7 us
  Pallas kernels  48.5 us (49%)
  waiting for transfers between devices  26.9 us (27%)
  starting transfers between devices  17.7 us (18%)
  other arithmetic  2.39 us (2%)
  between operations  1.62 us (2%)
    pallas_call x1, Pallas kernels, factor(): pl.pallas_call(functools.partial(factor_kernel, scale), in_specs=[vmem, h...  21.9 us
    ppermute x8, waiting for transfers between devices, swap(): lax.ppermute(block, axis, [(i, i ^ 1 << bit) for i in range(lax.axis_size...  19.9 us
    pallas_call x1, Pallas kernels, front(): pl.pallas_call(front_kernel, in_specs=[hbm, vmem, pl.BlockSpec(memory_spa...  13.9 us
    pallas_call x1, Pallas kernels, pick(): pl.pallas_call(functools.partial(pick_kernel, piece, share), in_specs=[hb...  11.8 us
    ppermute x8, starting transfers between devices, swap(): lax.ppermute(block, axis, [(i, i ^ 1 << bit) for i in range(lax.axis_size...  11 us
    ppermute x1, starting transfers between devices, shards(): east = lax.ppermute(outer[0], 'lon', [(t, s) for s, t in east_route])  6.06 us
    ppermute x1, waiting for transfers between devices, shards(): west = lax.ppermute(outer[3], 'lon', east_route)  4.92 us
  transfers between devices with their start and end apart: 12, of which 10 were waited for; matrix products, arithmetic and copies ran while one was open for 1% of the time, Pallas kernels for 12%

profile of v4, /device:TPU:0, one launch (start us, length us, event | category | flops | bytes accessed | tf_op | source)
XLA Modules:
  0.0 97.7 jit_solution(13226514636831355685)
XLA Ops:
  1.3 0.7 convert_bitcast_fusion
  2.1 0.8 maximum_maximum_fusion.cells_ref
  2.9 13.9 %front.1 = (bf16[512,6144]{1,0:T(8,128)(2,1)}, f32[512,512]{1,0:T(8,128)S(1)}, f32[48,128]{1,0:T(8,128)S(1)}, f32[48,128]{1,0:T(8,128)S(1)}, bf16[256,128]{1,0:T...) custom-call(bf16[2,256,48,128]{3,2,1,0:T(8,128)(2,1)} %v_hbm.1, ...), custom_call_target="tpu_custom_call" | custom-call | tf_op jit(solution)/shard_map/front/pallas_call | solution.py:172
  16.8 6.1 %collective-permute-start.1 = (bf16[2,256,128]{2,1,0:T(8,128)(2,1)S(1)}, bf16[2,256,128]{2,1,0:T(8,128)(2,1)S(1)}, u32[]{:S(2)}, u32[]{:S(2)}) collective-permute-start(bf16[2,256,128]{2,1,0:T(8,128)(2,1)S(1)} %get-tuple-element.26.x0_ref), channel_id=1, source_target_pairs={{1,0},{2,1},{3,2},{4,3},{5,4},{6,5},{7,6},{0,7},{9,8},{10,9},{11,1... | collective-permute-start | bytes 393224 | tf_op jit(solution)/shard_map/ppermute | solution.py:648
  22.9 0.7 collective-permute-start.3
  23.6 0.6 collective-permute-done.2.near_ref
  24.2 1.5 %collective-permute-done.1.east_ref = bf16[2,256,128]{2,1,0:T(8,128)(2,1)S(1)} collective-permute-done((bf16[2,256,128]{2,1,0:T(8,128)(2,1)S(1)}, bf16[2,256,128]{2,1,0:T(8,128)(2,1)S(1)}, u32[]{:S(2)}, u32[]{:S(2)}) %collective-permute-start.1) | collective-permute-done | bytes 131104 | tf_op jit(solution)/shard_map/ppermute | solution.py:648
  25.7 4.9 %collective-permute-done.west_ref = bf16[2,256,128]{2,1,0:T(8,128)(2,1)S(1)} collective-permute-done((bf16[2,256,128]{2,1,0:T(8,128)(2,1)S(1)}, bf16[2,256,128]{2,1,0:T(8,128)(2,1)S(1)}, u32[]{:S(2)}, u32[]{:S(2)}) %collective-permute-start) | collective-permute-done | bytes 131104 | tf_op jit(solution)/shard_map/ppermute | solution.py:647
  30.6 0.9 rim.1
  31.6 1.6 %collective-permute-done.4 = f32[640,128]{1,0:T(8,128)S(1)} collective-permute-done((f32[640,128]{1,0:T(8,128)S(1)}, f32[640,128]{1,0:T(8,128)S(1)}, u32[]{:S(2)}, u32[]{:S(2)}) %collective-permute-start.4) | collective-permute-done | bytes 327712 | tf_op jit(solution)/shard_map/ppermute | solution.py:303
  33.3 2.0 %collective-permute-start.5 = (f32[320,128]{1,0:T(8,128)S(1)}, f32[320,128]{1,0:T(8,128)S(1)}, u32[]{:S(2)}, u32[]{:S(2)}) collective-permute-start(f32[320,128]{1,0:T(8,128)S(1)} %constant_dynamic-slice_fusion.1), channel_id=1, source_target_pairs={{0,16},{8,24},{16,0},{24,8},{1,17},{9,25},{17,1},{25,9},{2,18},{10... | collective-permute-start | bytes 491528 | tf_op jit(solution)/shard_map/ppermute | solution.py:303
  35.3 4.7 %collective-permute-done.5 = f32[320,128]{1,0:T(8,128)S(1)} collective-permute-done((f32[320,128]{1,0:T(8,128)S(1)}, f32[320,128]{1,0:T(8,128)S(1)}, u32[]{:S(2)}, u32[]{:S(2)}) %collective-permute-start.5) | collective-permute-done | bytes 163872 | tf_op jit(solution)/shard_map/ppermute | solution.py:303
  40.2 11.8 %pick.1 = (bf16[6144,512]{1,0:T(8,128)(2,1)}, f32[8,128]{1,0:T(8,128)S(1)}) custom-call(s32[6144]{0:T(1024)S(1)} %broadcast_multiply_fusion.index_hbm, bf16[512,6144]{1,0:T(8,128)(2,1)} %get-tuple-element.43.fields_hbm, bf16[512,128]{1,0:T(8,128)(2,1)S(1)} %get-tuple-element.44.rim_ref, bf16[2,512,128]{2,1,0:T(8,128)(2,1)S(1)} %get-tuple-element.45.ends_ref, ...), custom_call_target="tpu_custom_call" | custom-call | tf_op jit(solution)/shard_map/pick/pallas_call | solution.py:422
  52.5 0.7 add_add_fusion
  53.2 1.0 %collective-permute-start.7 = (f32[160,128]{1,0:T(8,128)S(1)}, f32[160,128]{1,0:T(8,128)S(1)}, u32[]{:S(2)}, u32[]{:S(2)}) collective-permute-start(f32[160,128]{1,0:T(8,128)S(1)} %add_add_fusion), channel_id=1, source_target_pairs={{0,2},{1,3},{2,0},{3,1},{4,6},{5,7},{6,4},{7,5},{8,10},{9,11},{10,... | collective-permute-start | bytes 245768 | tf_op jit(solution)/shard_map/ppermute | solution.py:303
  54.2 3.5 %collective-permute-done.7 = f32[160,128]{1,0:T(8,128)S(1)} collective-permute-done((f32[160,128]{1,0:T(8,128)S(1)}, f32[160,128]{1,0:T(8,128)S(1)}, u32[]{:S(2)}, u32[]{:S(2)}) %collective-permute-start.7) | collective-permute-done | bytes 81952 | tf_op jit(solution)/shard_map/ppermute | solution.py:303
  57.7 3.6 %collective-permute-start.8 = (f32[160,128]{1,0:T(8,128)S(1)}, f32[160,128]{1,0:T(8,128)S(1)}, u32[]{:S(2)}, u32[]{:S(2)}) collective-permute-start(f32[160,128]{1,0:T(8,128)S(1)} %add.59), channel_id=1, source_target_pairs={{0,4},{1,5},{2,6},{3,7},{4,0},{5,1},{6,2},{7,3},{8,12},{9,13},{10,... | collective-permute-start | bytes 245768 | tf_op jit(solution)/shard_map/ppermute | solution.py:303
  61.3 2.4 %collective-permute-done.8 = f32[160,128]{1,0:T(8,128)S(1)} collective-permute-done((f32[160,128]{1,0:T(8,128)S(1)}, f32[160,128]{1,0:T(8,128)S(1)}, u32[]{:S(2)}, u32[]{:S(2)}) %collective-permute-start.8) | collective-permute-done | bytes 81952 | tf_op jit(solution)/shard_map/ppermute | solution.py:303
  63.7 2.3 %collective-permute-start.9 = (f32[160,128]{1,0:T(8,128)S(1)}, f32[160,128]{1,0:T(8,128)S(1)}, u32[]{:S(2)}, u32[]{:S(2)}) collective-permute-start(f32[160,128]{1,0:T(8,128)S(1)} %add.60), channel_id=1, source_target_pairs={{0,1},{1,0},{2,3},{3,2},{4,5},{5,4},{6,7},{7,6},{8,9},{9,8},{10,11... | collective-permute-start | bytes 245768 | tf_op jit(solution)/shard_map/ppermute | solution.py:303
  66.1 2.4 %collective-permute-done.9 = f32[160,128]{1,0:T(8,128)S(1)} collective-permute-done((f32[160,128]{1,0:T(8,128)S(1)}, f32[160,128]{1,0:T(8,128)S(1)}, u32[]{:S(2)}, u32[]{:S(2)}) %collective-permute-start.9) | collective-permute-done | bytes 81952 | tf_op jit(solution)/shard_map/ppermute | solution.py:303
  68.5 1.8 %collective-permute-start.10 = (f32[320,128]{1,0:T(8,128)S(1)}, f32[320,128]{1,0:T(8,128)S(1)}, u32[]{:S(2)}, u32[]{:S(2)}) collective-permute-start(f32[320,128]{1,0:T(8,128)S(1)} %maximum_select_fusion.2), channel_id=1, source_target_pairs={{0,16},{8,24},{16,0},{24,8},{1,17},{9,25},{17,1},{25,9},{2,18},{10... | collective-permute-start | bytes 491528 | tf_op jit(solution)/shard_map/ppermute | solution.py:303
  70.3 3.6 %collective-permute-done.10 = f32[320,128]{1,0:T(8,128)S(1)} collective-permute-done((f32[320,128]{1,0:T(8,128)S(1)}, f32[320,128]{1,0:T(8,128)S(1)}, u32[]{:S(2)}, u32[]{:S(2)}) %collective-permute-start.10) | collective-permute-done | bytes 163872 | tf_op jit(solution)/shard_map/ppermute | solution.py:303
  74.0 1.6 %collective-permute-done.11 = f32[640,128]{1,0:T(8,128)S(1)} collective-permute-done((f32[640,128]{1,0:T(8,128)S(1)}, f32[640,128]{1,0:T(8,128)S(1)}, u32[]{:S(2)}, u32[]{:S(2)}) %collective-permute-start.11) | collective-permute-done | bytes 327712 | tf_op jit(solution)/shard_map/ppermute | solution.py:303
  75.7 21.9 %factor.1 = (f32[512,512]{1,0:T(8,128)}, bf16[512,6144]{1,0:T(8,128)(2,1)}) custom-call(f32[10,128,128]{2,1,0:T(8,128)S(1)} %bitcast.8, bf16[6144,512]{1,0:T(8,128)(2,1)} %get-tuple-element.47.rows_hbm), custom_call_target="tpu_custom_call" | custom-call | tf_op jit(solution)/shard_map/factor/pallas_call | solution.py:614
  (22 shorter events, 1.0 us)
Async XLA Ops:
  0.6 39.5 %copy-start = (s32[6144]{0:T(1024)S(1)}, s32[6144]{0:T(1024)}, u32[]{:S(2)}) copy-start(s32[6144]{0:T(1024)} %param.8) | copy-start | bytes 73732
  16.8 8.8 %collective-permute-start.1 = (bf16[2,256,128]{2,1,0:T(8,128)(2,1)S(1)}, bf16[2,256,128]{2,1,0:T(8,128)(2,1)S(1)}, u32[]{:S(2)}, u32[]{:S(2)}) collective-permute-start(bf16[2,256,128]{2,1,0:T(8,128)(2,1)S(1)} %get-tuple-element.26.x0_ref), channel_id=1, source_target_pairs={{1,0},{2,1},{3,2},{4,3},{5,4},{6,5},{7,6},{0,7},{9,8},{10,9},{11,1... | collective-permute-start | bytes 393224 | tf_op jit(solution)/shard_map/ppermute | solution.py:648
  22.9 7.7 %collective-permute-start = (bf16[2,256,128]{2,1,0:T(8,128)(2,1)S(1)}, bf16[2,256,128]{2,1,0:T(8,128)(2,1)S(1)}, u32[]{:S(2)}, u32[]{:S(2)}) collective-permute-start(bf16[2,256,128]{2,1,0:T(8,128)(2,1)S(1)} %get-tuple-element.29.x3_ref), channel_id=1, source_target_pairs={{0,1},{1,2},{2,3},{3,4},{4,5},{5,6},{6,7},{7,0},{8,9},{9,10},{10,1... | collective-permute-start | bytes 393224 | tf_op jit(solution)/shard_map/ppermute | solution.py:647
  22.9 1.3 %collective-permute-start.2 = (bf16[256,128]{1,0:T(8,128)(2,1)S(1)}, bf16[256,128]{1,0:T(8,128)(2,1)S(1)}, u32[]{:S(2)}, u32[]{:S(2)}) collective-permute-start(bf16[256,128]{1,0:T(8,128)(2,1)S(1)} %get-tuple-element.30), channel_id=1, source_target_pairs={{0,8},{8,0},{16,24},{24,16},{1,9},{9,1},{17,25},{25,17},{2,10},{10... | collective-permute-start | bytes 196616 | tf_op jit(solution)/shard_map/ppermute | solution.py:650
  22.9 1.3 %collective-permute-start.3 = (bf16[256,128]{1,0:T(8,128)(2,1)S(1)}, bf16[256,128]{1,0:T(8,128)(2,1)S(1)}, u32[]{:S(2)}, u32[]{:S(2)}) collective-permute-start(bf16[256,128]{1,0:T(8,128)(2,1)S(1)} %get-tuple-element.31), channel_id=1, source_target_pairs={{8,16},{16,8},{24,31},{9,17},{17,9},{25,30},{10,18},{18,10},{26,29... | collective-permute-start | bytes 196616 | tf_op jit(solution)/shard_map/ppermute | solution.py:657
  31.5 1.7 %collective-permute-start.4 = (f32[640,128]{1,0:T(8,128)S(1)}, f32[640,128]{1,0:T(8,128)S(1)}, u32[]{:S(2)}, u32[]{:S(2)}) collective-permute-start(f32[640,128]{1,0:T(8,128)S(1)} %constant_dynamic-slice_fusion.2), channel_id=1, source_target_pairs={{0,8},{8,0},{16,24},{24,16},{1,9},{9,1},{17,25},{25,17},{2,10},{10... | collective-permute-start | bytes 983048 | tf_op jit(solution)/shard_map/ppermute | solution.py:303
  33.3 6.8 %collective-permute-start.5 = (f32[320,128]{1,0:T(8,128)S(1)}, f32[320,128]{1,0:T(8,128)S(1)}, u32[]{:S(2)}, u32[]{:S(2)}) collective-permute-start(f32[320,128]{1,0:T(8,128)S(1)} %constant_dynamic-slice_fusion.1), channel_id=1, source_target_pairs={{0,16},{8,24},{16,0},{24,8},{1,17},{9,25},{17,1},{25,9},{2,18},{10... | collective-permute-start | bytes 491528 | tf_op jit(solution)/shard_map/ppermute | solution.py:303
  40.1 12.4 %collective-permute-start.6 = (f32[160,128]{1,0:T(8,128)S(1)}, f32[160,128]{1,0:T(8,128)S(1)}, u32[]{:S(2)}, u32[]{:S(2)}) collective-permute-start(f32[160,128]{1,0:T(8,128)S(1)} %constant_dynamic-slice_fusion.after_ref), channel_id=1, source_target_pairs={{0,1},{1,0},{2,3},{3,2},{4,5},{5,4},{6,7},{7,6},{8,9},{9,8},{10,11... | collective-permute-start | bytes 245768 | tf_op jit(solution)/shard_map/ppermute | solution.py:303
  53.2 4.5 %collective-permute-start.7 = (f32[160,128]{1,0:T(8,128)S(1)}, f32[160,128]{1,0:T(8,128)S(1)}, u32[]{:S(2)}, u32[]{:S(2)}) collective-permute-start(f32[160,128]{1,0:T(8,128)S(1)} %add_add_fusion), channel_id=1, source_target_pairs={{0,2},{1,3},{2,0},{3,1},{4,6},{5,7},{6,4},{7,5},{8,10},{9,11},{10,... | collective-permute-start | bytes 245768 | tf_op jit(solution)/shard_map/ppermute | solution.py:303
  57.7 6.0 %collective-permute-start.8 = (f32[160,128]{1,0:T(8,128)S(1)}, f32[160,128]{1,0:T(8,128)S(1)}, u32[]{:S(2)}, u32[]{:S(2)}) collective-permute-start(f32[160,128]{1,0:T(8,128)S(1)} %add.59), channel_id=1, source_target_pairs={{0,4},{1,5},{2,6},{3,7},{4,0},{5,1},{6,2},{7,3},{8,12},{9,13},{10,... | collective-permute-start | bytes 245768 | tf_op jit(solution)/shard_map/ppermute | solution.py:303
  63.7 4.8 %collective-permute-start.9 = (f32[160,128]{1,0:T(8,128)S(1)}, f32[160,128]{1,0:T(8,128)S(1)}, u32[]{:S(2)}, u32[]{:S(2)}) collective-permute-start(f32[160,128]{1,0:T(8,128)S(1)} %add.60), channel_id=1, source_target_pairs={{0,1},{1,0},{2,3},{3,2},{4,5},{5,4},{6,7},{7,6},{8,9},{9,8},{10,11... | collective-permute-start | bytes 245768 | tf_op jit(solution)/shard_map/ppermute | solution.py:303
  68.5 5.4 %collective-permute-start.10 = (f32[320,128]{1,0:T(8,128)S(1)}, f32[320,128]{1,0:T(8,128)S(1)}, u32[]{:S(2)}, u32[]{:S(2)}) collective-permute-start(f32[320,128]{1,0:T(8,128)S(1)} %maximum_select_fusion.2), channel_id=1, source_target_pairs={{0,16},{8,24},{16,0},{24,8},{1,17},{9,25},{17,1},{25,9},{2,18},{10... | collective-permute-start | bytes 491528 | tf_op jit(solution)/shard_map/ppermute | solution.py:303
  73.9 1.7 %collective-permute-start.11 = (f32[640,128]{1,0:T(8,128)S(1)}, f32[640,128]{1,0:T(8,128)S(1)}, u32[]{:S(2)}, u32[]{:S(2)}) collective-permute-start(f32[640,128]{1,0:T(8,128)S(1)} %maximum_select_fusion.1), channel_id=1, source_target_pairs={{0,8},{8,0},{16,24},{24,16},{1,9},{9,1},{17,25},{25,17},{2,10},{10... | collective-permute-start | bytes 983048 | tf_op jit(solution)/shard_map/ppermute | solution.py:303

commit v5 on v4

--- a/solution.py
+++ b/solution.py
@@ -609,7 +609,7 @@
     square = (columns, columns)
     size = pieces.shape[1]
     cells = rows.shape[0]
-    width = next(n for n in (768, 512, 256, 128) if cells % n == 0)
+    width = next(n for n in (1536, 768, 512, 256, 128) if cells % n == 0)
     chunks = min(3, cells // width)
     return pl.pallas_call(
         functools.partial(factor_kernel, scale),
@@ -668,7 +668,7 @@
         held[piece], token = pick(piece, pieces, places, fields, rows, ends, after)
         return token
 
-    beside = {2 + piece: functools.partial(picking, piece) for piece in range(pieces)}
+    beside = {1 + piece: functools.partial(picking, piece) for piece in range(pieces)}
     total = all_sum(gram, beside)
     scale = math.sqrt(cells * lats * lons)
     triangle, basis = factor(total, held[0], columns, scale)

time: 98 us -> 97.1 us (level)
  starting transfers between devices: 17.7 us -> 12.2 us
  waiting for transfers between devices: 26.9 us -> 32 us
    ppermute x8, starting transfers between devices: 11 us -> 5.52 us  [swap(): lax.ppermute(block, axis, [(i, i ^ 1 << bit) for i in range(lax.axis_size...]
    ppermute x8, waiting for transfers between devices: 19.9 us -> 25 us  [swap(): lax.ppermute(block, axis, [(i, i ^ 1 << bit) for i in range(lax.axis_size...]
where the time goes in v5:
time: 97.1 us; the launch traced here: 96.8 us
  Pallas kernels  47.9 us (49%)
  waiting for transfers between devices  32 us (33%)
  starting transfers between devices  12.2 us (13%)
  other arithmetic  2.39 us (2%)
  between operations  1.62 us (2%)
    ppermute x8, waiting for transfers between devices, swap(): lax.ppermute(block, axis, [(i, i ^ 1 << bit) for i in range(lax.axis_size...  25 us
    pallas_call x1, Pallas kernels, factor(): pl.pallas_call(functools.partial(factor_kernel, scale), in_specs=[vmem, h...  21.3 us
    pallas_call x1, Pallas kernels, front(): pl.pallas_call(front_kernel, in_specs=[hbm, vmem, pl.BlockSpec(memory_spa...  13.9 us
    pallas_call x1, Pallas kernels, pick(): pl.pallas_call(functools.partial(pick_kernel, piece, share), in_specs=[hb...  11.8 us
    ppermute x1, starting transfers between devices, shards(): east = lax.ppermute(outer[0], 'lon', [(t, s) for s, t in east_route])  6.06 us
    ppermute x8, starting transfers between devices, swap(): lax.ppermute(block, axis, [(i, i ^ 1 << bit) for i in range(lax.axis_size...  5.52 us
    ppermute x1, waiting for transfers between devices, shards(): west = lax.ppermute(outer[3], 'lon', east_route)  4.92 us
  transfers between devices with their start and end apart: 12, of which 10 were waited for; matrix products, arithmetic and copies ran while one was open for 1% of the time, Pallas kernels for 12%

profile of v5, /device:TPU:0, one launch (start us, length us, event | category | flops | bytes accessed | tf_op | source)
XLA Modules:
  0.0 96.8 jit_solution(11291013374519430344)
XLA Ops:
  1.3 0.7 convert_bitcast_fusion
  2.1 0.8 maximum_maximum_fusion.cells_ref
  2.9 13.9 %front.1 = (bf16[512,6144]{1,0:T(8,128)(2,1)}, f32[512,512]{1,0:T(8,128)S(1)}, f32[48,128]{1,0:T(8,128)S(1)}, f32[48,128]{1,0:T(8,128)S(1)}, bf16[256,128]{1,0:T...) custom-call(bf16[2,256,48,128]{3,2,1,0:T(8,128)(2,1)} %v_hbm.1, ...), custom_call_target="tpu_custom_call" | custom-call | tf_op jit(solution)/shard_map/front/pallas_call | solution.py:172
  16.8 6.1 %collective-permute-start.1 = (bf16[2,256,128]{2,1,0:T(8,128)(2,1)S(1)}, bf16[2,256,128]{2,1,0:T(8,128)(2,1)S(1)}, u32[]{:S(2)}, u32[]{:S(2)}) collective-permute-start(bf16[2,256,128]{2,1,0:T(8,128)(2,1)S(1)} %get-tuple-element.26.x0_ref), channel_id=1, source_target_pairs={{1,0},{2,1},{3,2},{4,3},{5,4},{6,5},{7,6},{0,7},{9,8},{10,9},{11,1... | collective-permute-start | bytes 393224 | tf_op jit(solution)/shard_map/ppermute | solution.py:648
  22.9 0.7 collective-permute-start.3
  23.6 0.6 collective-permute-done.2.near_ref
  24.2 1.5 %collective-permute-done.1.east_ref = bf16[2,256,128]{2,1,0:T(8,128)(2,1)S(1)} collective-permute-done((bf16[2,256,128]{2,1,0:T(8,128)(2,1)S(1)}, bf16[2,256,128]{2,1,0:T(8,128)(2,1)S(1)}, u32[]{:S(2)}, u32[]{:S(2)}) %collective-permute-start.1) | collective-permute-done | bytes 131104 | tf_op jit(solution)/shard_map/ppermute | solution.py:648
  25.7 4.9 %collective-permute-done.west_ref = bf16[2,256,128]{2,1,0:T(8,128)(2,1)S(1)} collective-permute-done((bf16[2,256,128]{2,1,0:T(8,128)(2,1)S(1)}, bf16[2,256,128]{2,1,0:T(8,128)(2,1)S(1)}, u32[]{:S(2)}, u32[]{:S(2)}) %collective-permute-start) | collective-permute-done | bytes 131104 | tf_op jit(solution)/shard_map/ppermute | solution.py:647
  30.6 0.9 rim.1
  31.6 1.6 %collective-permute-done.4 = f32[640,128]{1,0:T(8,128)S(1)} collective-permute-done((f32[640,128]{1,0:T(8,128)S(1)}, f32[640,128]{1,0:T(8,128)S(1)}, u32[]{:S(2)}, u32[]{:S(2)}) %collective-permute-start.4) | collective-permute-done | bytes 327712 | tf_op jit(solution)/shard_map/ppermute | solution.py:303
  33.3 2.0 %collective-permute-start.5 = (f32[320,128]{1,0:T(8,128)S(1)}, f32[320,128]{1,0:T(8,128)S(1)}, u32[]{:S(2)}, u32[]{:S(2)}) collective-permute-start(f32[320,128]{1,0:T(8,128)S(1)} %constant_dynamic-slice_fusion.1.after_ref), channel_id=1, source_target_pairs={{0,16},{8,24},{16,0},{24,8},{1,17},{9,25},{17,1},{25,9},{2,18},{10... | collective-permute-start | bytes 491528 | tf_op jit(solution)/shard_map/ppermute | solution.py:303
  35.3 11.8 %pick.1 = (bf16[6144,512]{1,0:T(8,128)(2,1)}, f32[8,128]{1,0:T(8,128)S(1)}) custom-call(s32[6144]{0:T(1024)S(1)} %broadcast_multiply_fusion.index_hbm, bf16[512,6144]{1,0:T(8,128)(2,1)} %get-tuple-element.43.fields_hbm, bf16[512,128]{1,0:T(8,128)(2,1)S(1)} %get-tuple-element.44.rim_ref, bf16[2,512,128]{2,1,0:T(8,128)(2,1)S(1)} %get-tuple-element.45.ends_ref, ...), custom_call_target="tpu_custom_call" | custom-call | tf_op jit(solution)/shard_map/pick/pallas_call | solution.py:422
  47.2 0.5 slice.3
  47.7 0.7 add_add_fusion
  48.4 4.4 %collective-permute-done.6 = f32[160,128]{1,0:T(8,128)S(1)} collective-permute-done((f32[160,128]{1,0:T(8,128)S(1)}, f32[160,128]{1,0:T(8,128)S(1)}, u32[]{:S(2)}, u32[]{:S(2)}) %collective-permute-start.6) | collective-permute-done | bytes 81952 | tf_op jit(solution)/shard_map/ppermute | solution.py:303
  52.9 1.0 %collective-permute-start.7 = (f32[160,128]{1,0:T(8,128)S(1)}, f32[160,128]{1,0:T(8,128)S(1)}, u32[]{:S(2)}, u32[]{:S(2)}) collective-permute-start(f32[160,128]{1,0:T(8,128)S(1)} %dynamic-slice_add_fusion.1), channel_id=1, source_target_pairs={{0,2},{1,3},{2,0},{3,1},{4,6},{5,7},{6,4},{7,5},{8,10},{9,11},{10,... | collective-permute-start | bytes 245768 | tf_op jit(solution)/shard_map/ppermute | solution.py:303
  53.9 3.5 %collective-permute-done.7 = f32[160,128]{1,0:T(8,128)S(1)} collective-permute-done((f32[160,128]{1,0:T(8,128)S(1)}, f32[160,128]{1,0:T(8,128)S(1)}, u32[]{:S(2)}, u32[]{:S(2)}) %collective-permute-start.7) | collective-permute-done | bytes 81952 | tf_op jit(solution)/shard_map/ppermute | solution.py:303
  57.4 1.8 %collective-permute-start.8 = (f32[160,128]{1,0:T(8,128)S(1)}, f32[160,128]{1,0:T(8,128)S(1)}, u32[]{:S(2)}, u32[]{:S(2)}) collective-permute-start(f32[160,128]{1,0:T(8,128)S(1)} %add.59), channel_id=1, source_target_pairs={{0,4},{1,5},{2,6},{3,7},{4,0},{5,1},{6,2},{7,3},{8,12},{9,13},{10,... | collective-permute-start | bytes 245768 | tf_op jit(solution)/shard_map/ppermute | solution.py:303
  59.2 4.4 %collective-permute-done.8 = f32[160,128]{1,0:T(8,128)S(1)} collective-permute-done((f32[160,128]{1,0:T(8,128)S(1)}, f32[160,128]{1,0:T(8,128)S(1)}, u32[]{:S(2)}, u32[]{:S(2)}) %collective-permute-start.8) | collective-permute-done | bytes 81952 | tf_op jit(solution)/shard_map/ppermute | solution.py:303
  63.8 4.4 %collective-permute-done.9 = f32[160,128]{1,0:T(8,128)S(1)} collective-permute-done((f32[160,128]{1,0:T(8,128)S(1)}, f32[160,128]{1,0:T(8,128)S(1)}, u32[]{:S(2)}, u32[]{:S(2)}) %collective-permute-start.9) | collective-permute-done | bytes 81952 | tf_op jit(solution)/shard_map/ppermute | solution.py:303
  68.2 0.4 collective-permute-start.10
  68.6 5.0 %collective-permute-done.10 = f32[320,128]{1,0:T(8,128)S(1)} collective-permute-done((f32[320,128]{1,0:T(8,128)S(1)}, f32[320,128]{1,0:T(8,128)S(1)}, u32[]{:S(2)}, u32[]{:S(2)}) %collective-permute-start.10) | collective-permute-done | bytes 163872 | tf_op jit(solution)/shard_map/ppermute | solution.py:303
  73.7 1.6 %collective-permute-done.11 = f32[640,128]{1,0:T(8,128)S(1)} collective-permute-done((f32[640,128]{1,0:T(8,128)S(1)}, f32[640,128]{1,0:T(8,128)S(1)}, u32[]{:S(2)}, u32[]{:S(2)}) %collective-permute-start.11) | collective-permute-done | bytes 327712 | tf_op jit(solution)/shard_map/ppermute | solution.py:303
  75.4 21.3 %factor.1 = (f32[512,512]{1,0:T(8,128)}, bf16[512,6144]{1,0:T(8,128)(2,1)}) custom-call(f32[10,128,128]{2,1,0:T(8,128)S(1)} %bitcast.8, bf16[6144,512]{1,0:T(8,128)(2,1)} %get-tuple-element.47.rows_hbm), custom_call_target="tpu_custom_call" | custom-call | tf_op jit(solution)/shard_map/factor/pallas_call | solution.py:614
  (22 shorter events, 0.6 us)
Async XLA Ops:
  0.6 34.7 %copy-start = (s32[6144]{0:T(1024)S(1)}, s32[6144]{0:T(1024)}, u32[]{:S(2)}) copy-start(s32[6144]{0:T(1024)} %param.8) | copy-start | bytes 73732
  16.8 8.8 %collective-permute-start.1 = (bf16[2,256,128]{2,1,0:T(8,128)(2,1)S(1)}, bf16[2,256,128]{2,1,0:T(8,128)(2,1)S(1)}, u32[]{:S(2)}, u32[]{:S(2)}) collective-permute-start(bf16[2,256,128]{2,1,0:T(8,128)(2,1)S(1)} %get-tuple-element.26.x0_ref), channel_id=1, source_target_pairs={{1,0},{2,1},{3,2},{4,3},{5,4},{6,5},{7,6},{0,7},{9,8},{10,9},{11,1... | collective-permute-start | bytes 393224 | tf_op jit(solution)/shard_map/ppermute | solution.py:648
  22.9 7.7 %collective-permute-start = (bf16[2,256,128]{2,1,0:T(8,128)(2,1)S(1)}, bf16[2,256,128]{2,1,0:T(8,128)(2,1)S(1)}, u32[]{:S(2)}, u32[]{:S(2)}) collective-permute-start(bf16[2,256,128]{2,1,0:T(8,128)(2,1)S(1)} %get-tuple-element.29.x3_ref), channel_id=1, source_target_pairs={{0,1},{1,2},{2,3},{3,4},{4,5},{5,6},{6,7},{7,0},{8,9},{9,10},{10,1... | collective-permute-start | bytes 393224 | tf_op jit(solution)/shard_map/ppermute | solution.py:647
  22.9 1.3 %collective-permute-start.2 = (bf16[256,128]{1,0:T(8,128)(2,1)S(1)}, bf16[256,128]{1,0:T(8,128)(2,1)S(1)}, u32[]{:S(2)}, u32[]{:S(2)}) collective-permute-start(bf16[256,128]{1,0:T(8,128)(2,1)S(1)} %get-tuple-element.30), channel_id=1, source_target_pairs={{0,8},{8,0},{16,24},{24,16},{1,9},{9,1},{17,25},{25,17},{2,10},{10... | collective-permute-start | bytes 196616 | tf_op jit(solution)/shard_map/ppermute | solution.py:650
  22.9 1.3 %collective-permute-start.3 = (bf16[256,128]{1,0:T(8,128)(2,1)S(1)}, bf16[256,128]{1,0:T(8,128)(2,1)S(1)}, u32[]{:S(2)}, u32[]{:S(2)}) collective-permute-start(bf16[256,128]{1,0:T(8,128)(2,1)S(1)} %get-tuple-element.31), channel_id=1, source_target_pairs={{8,16},{16,8},{24,31},{9,17},{17,9},{25,30},{10,18},{18,10},{26,29... | collective-permute-start | bytes 196616 | tf_op jit(solution)/shard_map/ppermute | solution.py:657
  31.5 1.7 %collective-permute-start.4 = (f32[640,128]{1,0:T(8,128)S(1)}, f32[640,128]{1,0:T(8,128)S(1)}, u32[]{:S(2)}, u32[]{:S(2)}) collective-permute-start(f32[640,128]{1,0:T(8,128)S(1)} %constant_dynamic-slice_fusion.2), channel_id=1, source_target_pairs={{0,8},{8,0},{16,24},{24,16},{1,9},{9,1},{17,25},{25,17},{2,10},{10... | collective-permute-start | bytes 983048 | tf_op jit(solution)/shard_map/ppermute | solution.py:303
  33.3 14.4 %collective-permute-start.5 = (f32[320,128]{1,0:T(8,128)S(1)}, f32[320,128]{1,0:T(8,128)S(1)}, u32[]{:S(2)}, u32[]{:S(2)}) collective-permute-start(f32[320,128]{1,0:T(8,128)S(1)} %constant_dynamic-slice_fusion.1.after_ref), channel_id=1, source_target_pairs={{0,16},{8,24},{16,0},{24,8},{1,17},{9,25},{17,1},{25,9},{2,18},{10... | collective-permute-start | bytes 491528 | tf_op jit(solution)/shard_map/ppermute | solution.py:303
  48.4 4.5 %collective-permute-start.6 = (f32[160,128]{1,0:T(8,128)S(1)}, f32[160,128]{1,0:T(8,128)S(1)}, u32[]{:S(2)}, u32[]{:S(2)}) collective-permute-start(f32[160,128]{1,0:T(8,128)S(1)} %constant_dynamic-slice_fusion), channel_id=1, source_target_pairs={{0,1},{1,0},{2,3},{3,2},{4,5},{5,4},{6,7},{7,6},{8,9},{9,8},{10,11... | collective-permute-start | bytes 245768 | tf_op jit(solution)/shard_map/ppermute | solution.py:303
  52.9 4.5 %collective-permute-start.7 = (f32[160,128]{1,0:T(8,128)S(1)}, f32[160,128]{1,0:T(8,128)S(1)}, u32[]{:S(2)}, u32[]{:S(2)}) collective-permute-start(f32[160,128]{1,0:T(8,128)S(1)} %dynamic-slice_add_fusion.1), channel_id=1, source_target_pairs={{0,2},{1,3},{2,0},{3,1},{4,6},{5,7},{6,4},{7,5},{8,10},{9,11},{10,... | collective-permute-start | bytes 245768 | tf_op jit(solution)/shard_map/ppermute | solution.py:303
  57.4 6.3 %collective-permute-start.8 = (f32[160,128]{1,0:T(8,128)S(1)}, f32[160,128]{1,0:T(8,128)S(1)}, u32[]{:S(2)}, u32[]{:S(2)}) collective-permute-start(f32[160,128]{1,0:T(8,128)S(1)} %add.59), channel_id=1, source_target_pairs={{0,4},{1,5},{2,6},{3,7},{4,0},{5,1},{6,2},{7,3},{8,12},{9,13},{10,... | collective-permute-start | bytes 245768 | tf_op jit(solution)/shard_map/ppermute | solution.py:303
  63.7 4.5 %collective-permute-start.9 = (f32[160,128]{1,0:T(8,128)S(1)}, f32[160,128]{1,0:T(8,128)S(1)}, u32[]{:S(2)}, u32[]{:S(2)}) collective-permute-start(f32[160,128]{1,0:T(8,128)S(1)} %add.60), channel_id=1, source_target_pairs={{0,1},{1,0},{2,3},{3,2},{4,5},{5,4},{6,7},{7,6},{8,9},{9,8},{10,11... | collective-permute-start | bytes 245768 | tf_op jit(solution)/shard_map/ppermute | solution.py:303
  68.2 5.4 %collective-permute-start.10 = (f32[320,128]{1,0:T(8,128)S(1)}, f32[320,128]{1,0:T(8,128)S(1)}, u32[]{:S(2)}, u32[]{:S(2)}) collective-permute-start(f32[320,128]{1,0:T(8,128)S(1)} %maximum_select_fusion.2), channel_id=1, source_target_pairs={{0,16},{8,24},{16,0},{24,8},{1,17},{9,25},{17,1},{25,9},{2,18},{10... | collective-permute-start | bytes 491528 | tf_op jit(solution)/shard_map/ppermute | solution.py:303
  73.6 1.7 %collective-permute-start.11 = (f32[640,128]{1,0:T(8,128)S(1)}, f32[640,128]{1,0:T(8,128)S(1)}, u32[]{:S(2)}, u32[]{:S(2)}) collective-permute-start(f32[640,128]{1,0:T(8,128)S(1)} %maximum_select_fusion.1), channel_id=1, source_target_pairs={{0,8},{8,0},{16,24},{24,16},{1,9},{9,1},{17,25},{25,17},{2,10},{10... | collective-permute-start | bytes 983048 | tf_op jit(solution)/shard_map/ppermute | solution.py:303

commit v6 on v5

--- a/solution.py
+++ b/solution.py
@@ -163,7 +163,7 @@
     assert width_x <= width_y // 2 - 2
     step = next(n for n in (32, 16) if days % n == 0)
     places = wet_index.reshape(width_x, width_y).astype(F32)
-    group = next(n for n in (8, 6, 4, 3, 2, 1) if width_x % n == 0)
+    group = next(n for n in (16, 8, 6, 4, 3, 2, 1) if width_x % n == 0)
     vmem = pl.BlockSpec(memory_space=pltpu.VMEM)
     hbm = pl.BlockSpec(memory_space=pl.ANY)
     metric = jax.ShapeDtypeStruct((width_x, width_y), F32)

time: 97.1 us -> 96.2 us (level)
  no operation moved by 1% of the time
where the time goes in v6:
time: 96.2 us; the launch traced here: 95.9 us
  Pallas kernels  47 us (49%)
  waiting for transfers between devices  32 us (33%)
  starting transfers between devices  12.3 us (13%)
  other arithmetic  2.39 us (2%)
  between operations  1.62 us (2%)
    ppermute x8, waiting for transfers between devices, swap(): lax.ppermute(block, axis, [(i, i ^ 1 << bit) for i in range(lax.axis_size...  25 us
    pallas_call x1, Pallas kernels, factor(): pl.pallas_call(functools.partial(factor_kernel, scale), in_specs=[vmem, h...  21.3 us
    pallas_call x1, Pallas kernels, front(): pl.pallas_call(front_kernel, in_specs=[hbm, vmem, pl.BlockSpec(memory_spa...  13 us
    pallas_call x1, Pallas kernels, pick(): pl.pallas_call(functools.partial(pick_kernel, piece, share), in_specs=[hb...  11.8 us
    ppermute x1, starting transfers between devices, shards(): east = lax.ppermute(outer[0], 'lon', [(t, s) for s, t in east_route])  6.06 us
    ppermute x8, starting transfers between devices, swap(): lax.ppermute(block, axis, [(i, i ^ 1 << bit) for i in range(lax.axis_size...  5.54 us
    ppermute x1, waiting for transfers between devices, shards(): west = lax.ppermute(outer[3], 'lon', east_route)  4.91 us
  transfers between devices with their start and end apart: 12, of which 10 were waited for; matrix products, arithmetic and copies ran while one was open for 1% of the time, Pallas kernels for 12%

profile of v6, /device:TPU:0, one launch (start us, length us, event | category | flops | bytes accessed | tf_op | source)
XLA Modules:
  0.0 95.9 jit_solution(11647750408625446639)
XLA Ops:
  1.3 0.7 convert_bitcast_fusion
  2.1 0.8 maximum_maximum_fusion.cells_ref
  2.9 13.0 %front.1 = (bf16[512,6144]{1,0:T(8,128)(2,1)}, f32[512,512]{1,0:T(8,128)S(1)}, f32[48,128]{1,0:T(8,128)S(1)}, f32[48,128]{1,0:T(8,128)S(1)}, bf16[256,128]{1,0:T...) custom-call(bf16[2,256,48,128]{3,2,1,0:T(8,128)(2,1)} %v_hbm.1, ...), custom_call_target="tpu_custom_call" | custom-call | tf_op jit(solution)/shard_map/front/pallas_call | solution.py:172
  16.0 6.1 %collective-permute-start.1 = (bf16[2,256,128]{2,1,0:T(8,128)(2,1)S(1)}, bf16[2,256,128]{2,1,0:T(8,128)(2,1)S(1)}, u32[]{:S(2)}, u32[]{:S(2)}) collective-permute-start(bf16[2,256,128]{2,1,0:T(8,128)(2,1)S(1)} %get-tuple-element.26.x0_ref), channel_id=1, source_target_pairs={{1,0},{2,1},{3,2},{4,3},{5,4},{6,5},{7,6},{0,7},{9,8},{10,9},{11,1... | collective-permute-start | bytes 393224 | tf_op jit(solution)/shard_map/ppermute | solution.py:648
  22.0 0.7 collective-permute-start.3
  22.7 0.6 collective-permute-done.2.near_ref
  23.3 1.5 %collective-permute-done.1.east_ref = bf16[2,256,128]{2,1,0:T(8,128)(2,1)S(1)} collective-permute-done((bf16[2,256,128]{2,1,0:T(8,128)(2,1)S(1)}, bf16[2,256,128]{2,1,0:T(8,128)(2,1)S(1)}, u32[]{:S(2)}, u32[]{:S(2)}) %collective-permute-start.1) | collective-permute-done | bytes 131104 | tf_op jit(solution)/shard_map/ppermute | solution.py:648
  24.8 4.9 %collective-permute-done.west_ref = bf16[2,256,128]{2,1,0:T(8,128)(2,1)S(1)} collective-permute-done((bf16[2,256,128]{2,1,0:T(8,128)(2,1)S(1)}, bf16[2,256,128]{2,1,0:T(8,128)(2,1)S(1)}, u32[]{:S(2)}, u32[]{:S(2)}) %collective-permute-start) | collective-permute-done | bytes 131104 | tf_op jit(solution)/shard_map/ppermute | solution.py:647
  29.7 0.9 rim.1
  30.7 1.6 %collective-permute-done.4 = f32[640,128]{1,0:T(8,128)S(1)} collective-permute-done((f32[640,128]{1,0:T(8,128)S(1)}, f32[640,128]{1,0:T(8,128)S(1)}, u32[]{:S(2)}, u32[]{:S(2)}) %collective-permute-start.4) | collective-permute-done | bytes 327712 | tf_op jit(solution)/shard_map/ppermute | solution.py:303
  32.4 2.0 %collective-permute-start.5 = (f32[320,128]{1,0:T(8,128)S(1)}, f32[320,128]{1,0:T(8,128)S(1)}, u32[]{:S(2)}, u32[]{:S(2)}) collective-permute-start(f32[320,128]{1,0:T(8,128)S(1)} %constant_dynamic-slice_fusion.1.after_ref), channel_id=1, source_target_pairs={{0,16},{8,24},{16,0},{24,8},{1,17},{9,25},{17,1},{25,9},{2,18},{10... | collective-permute-start | bytes 491528 | tf_op jit(solution)/shard_map/ppermute | solution.py:303
  34.4 11.8 %pick.1 = (bf16[6144,512]{1,0:T(8,128)(2,1)}, f32[8,128]{1,0:T(8,128)S(1)}) custom-call(s32[6144]{0:T(1024)S(1)} %broadcast_multiply_fusion.index_hbm, bf16[512,6144]{1,0:T(8,128)(2,1)} %get-tuple-element.43.fields_hbm, bf16[512,128]{1,0:T(8,128)(2,1)S(1)} %get-tuple-element.44.rim_ref, bf16[2,512,128]{2,1,0:T(8,128)(2,1)S(1)} %get-tuple-element.45.ends_ref, ...), custom_call_target="tpu_custom_call" | custom-call | tf_op jit(solution)/shard_map/pick/pallas_call | solution.py:422
  46.3 0.5 slice.3
  46.8 0.7 add_add_fusion
  47.6 4.4 %collective-permute-done.6 = f32[160,128]{1,0:T(8,128)S(1)} collective-permute-done((f32[160,128]{1,0:T(8,128)S(1)}, f32[160,128]{1,0:T(8,128)S(1)}, u32[]{:S(2)}, u32[]{:S(2)}) %collective-permute-start.6) | collective-permute-done | bytes 81952 | tf_op jit(solution)/shard_map/ppermute | solution.py:303
  52.0 1.0 %collective-permute-start.7 = (f32[160,128]{1,0:T(8,128)S(1)}, f32[160,128]{1,0:T(8,128)S(1)}, u32[]{:S(2)}, u32[]{:S(2)}) collective-permute-start(f32[160,128]{1,0:T(8,128)S(1)} %dynamic-slice_add_fusion.1), channel_id=1, source_target_pairs={{0,2},{1,3},{2,0},{3,1},{4,6},{5,7},{6,4},{7,5},{8,10},{9,11},{10,... | collective-permute-start | bytes 245768 | tf_op jit(solution)/shard_map/ppermute | solution.py:303
  53.0 3.5 %collective-permute-done.7 = f32[160,128]{1,0:T(8,128)S(1)} collective-permute-done((f32[160,128]{1,0:T(8,128)S(1)}, f32[160,128]{1,0:T(8,128)S(1)}, u32[]{:S(2)}, u32[]{:S(2)}) %collective-permute-start.7) | collective-permute-done | bytes 81952 | tf_op jit(solution)/shard_map/ppermute | solution.py:303
  56.5 1.8 %collective-permute-start.8 = (f32[160,128]{1,0:T(8,128)S(1)}, f32[160,128]{1,0:T(8,128)S(1)}, u32[]{:S(2)}, u32[]{:S(2)}) collective-permute-start(f32[160,128]{1,0:T(8,128)S(1)} %add.59), channel_id=1, source_target_pairs={{0,4},{1,5},{2,6},{3,7},{4,0},{5,1},{6,2},{7,3},{8,12},{9,13},{10,... | collective-permute-start | bytes 245768 | tf_op jit(solution)/shard_map/ppermute | solution.py:303
  58.4 4.4 %collective-permute-done.8 = f32[160,128]{1,0:T(8,128)S(1)} collective-permute-done((f32[160,128]{1,0:T(8,128)S(1)}, f32[160,128]{1,0:T(8,128)S(1)}, u32[]{:S(2)}, u32[]{:S(2)}) %collective-permute-start.8) | collective-permute-done | bytes 81952 | tf_op jit(solution)/shard_map/ppermute | solution.py:303
  62.9 4.4 %collective-permute-done.9 = f32[160,128]{1,0:T(8,128)S(1)} collective-permute-done((f32[160,128]{1,0:T(8,128)S(1)}, f32[160,128]{1,0:T(8,128)S(1)}, u32[]{:S(2)}, u32[]{:S(2)}) %collective-permute-start.9) | collective-permute-done | bytes 81952 | tf_op jit(solution)/shard_map/ppermute | solution.py:303
  67.3 0.4 collective-permute-start.10
  67.7 5.0 %collective-permute-done.10 = f32[320,128]{1,0:T(8,128)S(1)} collective-permute-done((f32[320,128]{1,0:T(8,128)S(1)}, f32[320,128]{1,0:T(8,128)S(1)}, u32[]{:S(2)}, u32[]{:S(2)}) %collective-permute-start.10) | collective-permute-done | bytes 163872 | tf_op jit(solution)/shard_map/ppermute | solution.py:303
  72.8 1.6 %collective-permute-done.11 = f32[640,128]{1,0:T(8,128)S(1)} collective-permute-done((f32[640,128]{1,0:T(8,128)S(1)}, f32[640,128]{1,0:T(8,128)S(1)}, u32[]{:S(2)}, u32[]{:S(2)}) %collective-permute-start.11) | collective-permute-done | bytes 327712 | tf_op jit(solution)/shard_map/ppermute | solution.py:303
  74.5 21.3 %factor.1 = (f32[512,512]{1,0:T(8,128)}, bf16[512,6144]{1,0:T(8,128)(2,1)}) custom-call(f32[10,128,128]{2,1,0:T(8,128)S(1)} %bitcast.8, bf16[6144,512]{1,0:T(8,128)(2,1)} %get-tuple-element.47.rows_hbm), custom_call_target="tpu_custom_call" | custom-call | tf_op jit(solution)/shard_map/factor/pallas_call | solution.py:614
  (22 shorter events, 0.6 us)
Async XLA Ops:
  0.6 33.8 %copy-start = (s32[6144]{0:T(1024)S(1)}, s32[6144]{0:T(1024)}, u32[]{:S(2)}) copy-start(s32[6144]{0:T(1024)} %param.8) | copy-start | bytes 73732
  16.0 8.8 %collective-permute-start.1 = (bf16[2,256,128]{2,1,0:T(8,128)(2,1)S(1)}, bf16[2,256,128]{2,1,0:T(8,128)(2,1)S(1)}, u32[]{:S(2)}, u32[]{:S(2)}) collective-permute-start(bf16[2,256,128]{2,1,0:T(8,128)(2,1)S(1)} %get-tuple-element.26.x0_ref), channel_id=1, source_target_pairs={{1,0},{2,1},{3,2},{4,3},{5,4},{6,5},{7,6},{0,7},{9,8},{10,9},{11,1... | collective-permute-start | bytes 393224 | tf_op jit(solution)/shard_map/ppermute | solution.py:648
  22.0 7.7 %collective-permute-start = (bf16[2,256,128]{2,1,0:T(8,128)(2,1)S(1)}, bf16[2,256,128]{2,1,0:T(8,128)(2,1)S(1)}, u32[]{:S(2)}, u32[]{:S(2)}) collective-permute-start(bf16[2,256,128]{2,1,0:T(8,128)(2,1)S(1)} %get-tuple-element.29.x3_ref), channel_id=1, source_target_pairs={{0,1},{1,2},{2,3},{3,4},{4,5},{5,6},{6,7},{7,0},{8,9},{9,10},{10,1... | collective-permute-start | bytes 393224 | tf_op jit(solution)/shard_map/ppermute | solution.py:647
  22.0 1.3 %collective-permute-start.2 = (bf16[256,128]{1,0:T(8,128)(2,1)S(1)}, bf16[256,128]{1,0:T(8,128)(2,1)S(1)}, u32[]{:S(2)}, u32[]{:S(2)}) collective-permute-start(bf16[256,128]{1,0:T(8,128)(2,1)S(1)} %get-tuple-element.30), channel_id=1, source_target_pairs={{0,8},{8,0},{16,24},{24,16},{1,9},{9,1},{17,25},{25,17},{2,10},{10... | collective-permute-start | bytes 196616 | tf_op jit(solution)/shard_map/ppermute | solution.py:650
  22.0 1.3 %collective-permute-start.3 = (bf16[256,128]{1,0:T(8,128)(2,1)S(1)}, bf16[256,128]{1,0:T(8,128)(2,1)S(1)}, u32[]{:S(2)}, u32[]{:S(2)}) collective-permute-start(bf16[256,128]{1,0:T(8,128)(2,1)S(1)} %get-tuple-element.31), channel_id=1, source_target_pairs={{8,16},{16,8},{24,31},{9,17},{17,9},{25,30},{10,18},{18,10},{26,29... | collective-permute-start | bytes 196616 | tf_op jit(solution)/shard_map/ppermute | solution.py:657
  30.6 1.7 %collective-permute-start.4 = (f32[640,128]{1,0:T(8,128)S(1)}, f32[640,128]{1,0:T(8,128)S(1)}, u32[]{:S(2)}, u32[]{:S(2)}) collective-permute-start(f32[640,128]{1,0:T(8,128)S(1)} %constant_dynamic-slice_fusion.2), channel_id=1, source_target_pairs={{0,8},{8,0},{16,24},{24,16},{1,9},{9,1},{17,25},{25,17},{2,10},{10... | collective-permute-start | bytes 983048 | tf_op jit(solution)/shard_map/ppermute | solution.py:303
  32.4 14.4 %collective-permute-start.5 = (f32[320,128]{1,0:T(8,128)S(1)}, f32[320,128]{1,0:T(8,128)S(1)}, u32[]{:S(2)}, u32[]{:S(2)}) collective-permute-start(f32[320,128]{1,0:T(8,128)S(1)} %constant_dynamic-slice_fusion.1.after_ref), channel_id=1, source_target_pairs={{0,16},{8,24},{16,0},{24,8},{1,17},{9,25},{17,1},{25,9},{2,18},{10... | collective-permute-start | bytes 491528 | tf_op jit(solution)/shard_map/ppermute | solution.py:303
  47.5 4.5 %collective-permute-start.6 = (f32[160,128]{1,0:T(8,128)S(1)}, f32[160,128]{1,0:T(8,128)S(1)}, u32[]{:S(2)}, u32[]{:S(2)}) collective-permute-start(f32[160,128]{1,0:T(8,128)S(1)} %constant_dynamic-slice_fusion), channel_id=1, source_target_pairs={{0,1},{1,0},{2,3},{3,2},{4,5},{5,4},{6,7},{7,6},{8,9},{9,8},{10,11... | collective-permute-start | bytes 245768 | tf_op jit(solution)/shard_map/ppermute | solution.py:303
  52.0 4.5 %collective-permute-start.7 = (f32[160,128]{1,0:T(8,128)S(1)}, f32[160,128]{1,0:T(8,128)S(1)}, u32[]{:S(2)}, u32[]{:S(2)}) collective-permute-start(f32[160,128]{1,0:T(8,128)S(1)} %dynamic-slice_add_fusion.1), channel_id=1, source_target_pairs={{0,2},{1,3},{2,0},{3,1},{4,6},{5,7},{6,4},{7,5},{8,10},{9,11},{10,... | collective-permute-start | bytes 245768 | tf_op jit(solution)/shard_map/ppermute | solution.py:303
  56.5 6.3 %collective-permute-start.8 = (f32[160,128]{1,0:T(8,128)S(1)}, f32[160,128]{1,0:T(8,128)S(1)}, u32[]{:S(2)}, u32[]{:S(2)}) collective-permute-start(f32[160,128]{1,0:T(8,128)S(1)} %add.59), channel_id=1, source_target_pairs={{0,4},{1,5},{2,6},{3,7},{4,0},{5,1},{6,2},{7,3},{8,12},{9,13},{10,... | collective-permute-start | bytes 245768 | tf_op jit(solution)/shard_map/ppermute | solution.py:303
  62.8 4.5 %collective-permute-start.9 = (f32[160,128]{1,0:T(8,128)S(1)}, f32[160,128]{1,0:T(8,128)S(1)}, u32[]{:S(2)}, u32[]{:S(2)}) collective-permute-start(f32[160,128]{1,0:T(8,128)S(1)} %add.60), channel_id=1, source_target_pairs={{0,1},{1,0},{2,3},{3,2},{4,5},{5,4},{6,7},{7,6},{8,9},{9,8},{10,11... | collective-permute-start | bytes 245768 | tf_op jit(solution)/shard_map/ppermute | solution.py:303
  67.3 5.4 %collective-permute-start.10 = (f32[320,128]{1,0:T(8,128)S(1)}, f32[320,128]{1,0:T(8,128)S(1)}, u32[]{:S(2)}, u32[]{:S(2)}) collective-permute-start(f32[320,128]{1,0:T(8,128)S(1)} %maximum_select_fusion.2), channel_id=1, source_target_pairs={{0,16},{8,24},{16,0},{24,8},{1,17},{9,25},{17,1},{25,9},{2,18},{10... | collective-permute-start | bytes 491528 | tf_op jit(solution)/shard_map/ppermute | solution.py:303
  72.8 1.7 %collective-permute-start.11 = (f32[640,128]{1,0:T(8,128)S(1)}, f32[640,128]{1,0:T(8,128)S(1)}, u32[]{:S(2)}, u32[]{:S(2)}) collective-permute-start(f32[640,128]{1,0:T(8,128)S(1)} %maximum_select_fusion.1), channel_id=1, source_target_pairs={{0,8},{8,0},{16,24},{24,16},{1,9},{9,1},{17,25},{25,17},{2,10},{10... | collective-permute-start | bytes 983048 | tf_op jit(solution)/shard_map/ppermute | solution.py:303
